TPU v7x, 32 devices: a whole 2x2x4 slice. The times are simulated.
32 devices in a mesh: clip: 8 (over z, y), win: 4 (over x, core).
Axes of the slice: x: 2, y: 2, z: 4, core: 2. Of those that a mesh axis runs over, the one named last changes fastest.
Arguments:
- tokens: bfloat16 [16, 8, 392, 512], P('clip', 'win'), may hold values from -6 to 6
- cotangent: bfloat16 [16, 8, 392, 512], P('clip', 'win'), may hold values from -6 to 6
- adapter_ids: int32 [16], P('clip'), may hold values from 0 to 7, as said below
- ln1_gain: bfloat16 [512], P('clip'), may hold values from 0.5 to 1.5
- qkv_weight: bfloat16 [512, 1536], P('clip', 'win'), may hold values from -0.25 to 0.25
- qkv_bias: bfloat16 [1536], P('clip'), may hold values from -1.5 to 1.5
- proj_weight: bfloat16 [512, 512], P('clip', 'win'), may hold values from -2 to 2
- proj_bias: bfloat16 [512], P('clip'), may hold values from -1.5 to 1.5
- ln2_gain: bfloat16 [512], P('clip'), may hold values from 0.5 to 1.5
- fc1_weight: bfloat16 [512, 2048], P('clip', 'win'), may hold values from -0.25 to 0.25
- fc1_bias: bfloat16 [2048], P('clip'), may hold values from -1.5 to 1.5
- fc2_weight: bfloat16 [2048, 512], P('clip', 'win'), may hold values from -0.125 to 0.125
- fc2_bias: bfloat16 [512], P('clip'), may hold values from -1.5 to 1.5
- bias_table: bfloat16 [16, 2535], replicated, may hold values from -4 to 4
- qkv_down: bfloat16 [8, 512, 16], P('win', 'clip'), may hold values from -0.25 to 0.25
- qkv_up: bfloat16 [8, 16, 1536], P('win', None, 'clip'), may hold values from -0.75 to 0.75
- proj_down: bfloat16 [8, 512, 16], P('win', 'clip'), may hold values from -2 to 2
- proj_up: bfloat16 [8, 16, 512], P('win', None, 'clip'), may hold values from -0.75 to 0.75
- fc1_down: bfloat16 [8, 512, 16], P('win', 'clip'), may hold values from -0.25 to 0.25
- fc1_up: bfloat16 [8, 16, 2048], P('win', None, 'clip'), may hold values from -0.75 to 0.75
- fc2_down: bfloat16 [8, 2048, 16], P('win', 'clip'), may hold values from -0.125 to 0.125
- fc2_up: bfloat16 [8, 16, 512], P('win', None, 'clip'), may hold values from -0.75 to 0.75
Outputs:
- activations: bfloat16 [16, 8, 392, 512], P('clip', 'win')
- input_grad: bfloat16 [16, 8, 392, 512], P('clip', 'win')
- grad_qkv_down: float32 [8, 512, 16], P('win', 'clip')
- grad_qkv_up: float32 [8, 16, 1536], P('win', None, 'clip')
- grad_proj_down: float32 [8, 512, 16], P('win', 'clip')
- grad_proj_up: float32 [8, 16, 512], P('win', None, 'clip')
- grad_fc1_down: float32 [8, 512, 16], P('win', 'clip')
- grad_fc1_up: float32 [8, 16, 2048], P('win', None, 'clip')
- grad_fc2_down: float32 [8, 2048, 16], P('win', 'clip')
- grad_fc2_up: float32 [8, 16, 512], P('win', None, 'clip')
Inputs may be any that keep to these rules, and one draw needn't show every extreme that they name: `adapter_ids`: ids never fall from one clip to the next (clips are grouped by adapter); adapters 0 and 7 appear in every draw.
All inputs are finite; a program needn't handle non-finite values.
Results may differ from a plain program's by a relative error of at most 0.017.
Values may be sent and summed in bfloat16 or wider, within the bound.
A program may use at most 256 MiB of HBM per device.

v0:
```python
import jax
import jax.numpy as jnp
from jax import lax
from jax.sharding import PartitionSpec as P

masked_score = -1000000000.0
inverse_root_two = 0.7071067811865476
inverse_root_tau = 0.3989422804014327
shift_plan = ((1, 4, 4), (2, 5, 3), (3, 6, 3))


def swapped(shard, axis, distance):
    return lax.ppermute(shard, axis, [(i, i ^ 1 << distance) for i in range(lax.axis_size(axis))])


def norm_rows(values, gain):
    average = jnp.mean(values, axis=-1, keepdims=True)
    centred = values - average
    variance = jnp.mean(centred * centred, axis=-1, keepdims=True)
    inverse_dev = lax.rsqrt(variance + 1e-05)
    normed = centred * inverse_dev
    return (normed * gain, normed, inverse_dev)


def norm_back(gradient_output, gain, normed, inverse_dev):
    grad_norm = gradient_output * gain
    centre_term = jnp.mean(grad_norm, axis=-1, keepdims=True)
    slope_term = jnp.mean(grad_norm * normed, axis=-1, keepdims=True)
    return inverse_dev * (grad_norm - centre_term - normed * slope_term)


def cyclic_move(field, local_bits, sender, forward):
    for bit_number, (group_axis, row_axis, amount) in zip((2, 1, 0), shift_plan):
        length = field.shape[row_axis]
        cut_at = amount if forward else length - amount
        front = lax.slice_in_dim(field, 0, cut_at, axis=row_axis)
        behind = lax.slice_in_dim(field, cut_at, length, axis=row_axis)
        moving = front if forward else behind
        staying = behind if forward else front
        if bit_number < local_bits:
            arrived = jnp.flip(moving, axis=group_axis)
        else:
            arrived = sender(moving, bit_number - local_bits)
        field = jnp.concatenate(
            (staying, arrived) if forward else (arrived, staying), axis=row_axis
        )
    return field


def linear_project(input_tokens, weight):
    return jnp.einsum("ctd,de->cte", input_tokens, weight, preferred_element_type=jnp.float32)


def linear_project_backward(gradient_bundle, weight):
    return jnp.einsum("cte,de->ctd", gradient_bundle, weight, preferred_element_type=jnp.float32)


def apply_low_rank(input_tokens, down_matrix, up_matrix):
    rank_reduced = jnp.einsum(
        "ctd,cdr->ctr", input_tokens, down_matrix, preferred_element_type=jnp.float32
    ).astype(jnp.bfloat16)
    return (
        rank_reduced,
        jnp.einsum("ctr,cre->cte", rank_reduced, up_matrix, preferred_element_type=jnp.float32),
    )


def adapter_backward(input_tokens, rank_reduced, gradient_bundle, down_matrix, up_matrix):
    grad_up = jnp.einsum(
        "ctr,cte->cre", rank_reduced, gradient_bundle, preferred_element_type=jnp.float32
    )
    grad_reduced = jnp.einsum(
        "cte,cre->ctr", gradient_bundle, up_matrix, preferred_element_type=jnp.float32
    ).astype(jnp.bfloat16)
    grad_down = jnp.einsum(
        "ctd,ctr->cdr", input_tokens, grad_reduced, preferred_element_type=jnp.float32
    )
    grad_input = jnp.einsum(
        "ctr,cdr->ctd", grad_reduced, down_matrix, preferred_element_type=jnp.float32
    )
    return (grad_down, grad_up, grad_input)


def attend_forward(operands, pos_bias, scale):
    query_rows, key_rows, value_rows, allowed_pairs = operands
    raw_scores = jnp.einsum(
        "qhd,khd->hqk", query_rows, key_rows, preferred_element_type=jnp.float32
    )
    scores = jnp.where(allowed_pairs[None], raw_scores * scale + pos_bias, masked_score)
    largest = jnp.max(scores, axis=-1, keepdims=True)
    log_total = largest + jnp.log(jnp.sum(jnp.exp(scores - largest), axis=-1, keepdims=True))
    probs = jnp.exp(scores - log_total).astype(jnp.bfloat16)
    attended = jnp.einsum("hqk,khd->qhd", probs, value_rows, preferred_element_type=jnp.float32)
    return (attended.astype(jnp.bfloat16), log_total[..., 0])


def attend_backward(operands, pos_bias, scale):
    query_rows, key_rows, value_rows, allowed_pairs, log_total, gradient_output = operands
    raw_scores = jnp.einsum(
        "qhd,khd->hqk", query_rows, key_rows, preferred_element_type=jnp.float32
    )
    scores = jnp.where(allowed_pairs[None], raw_scores * scale + pos_bias, masked_score)
    probs = jnp.exp(scores - log_total[..., None])
    grad_values = jnp.einsum(
        "hqk,qhd->khd",
        probs.astype(jnp.bfloat16),
        gradient_output,
        preferred_element_type=jnp.float32,
    )
    grad_probs = jnp.einsum(
        "qhd,khd->hqk", gradient_output, value_rows, preferred_element_type=jnp.float32
    )
    grad_scores = probs * (grad_probs - jnp.sum(probs * grad_probs, axis=-1, keepdims=True))
    grad_raw = (grad_scores * scale).astype(jnp.bfloat16)
    grad_query = jnp.einsum("hqk,khd->qhd", grad_raw, key_rows, preferred_element_type=jnp.float32)
    grad_keys = jnp.einsum("hqk,qhd->khd", grad_raw, query_rows, preferred_element_type=jnp.float32)
    return (
        grad_query.astype(jnp.bfloat16),
        grad_keys.astype(jnp.bfloat16),
        grad_values.astype(jnp.bfloat16),
    )


def gather_forward(matrices, vectors):
    (
        qkv_mat,
        proj_mat,
        fc1_mat,
        fc2_mat,
        qkv_down,
        qkv_up,
        proj_down,
        proj_up,
        fc1_down,
        fc1_up,
        fc2_down,
        fc2_up,
    ) = matrices
    gain_first, qkv_bias, proj_bias, gain_second, fc1_bias, fc2_bias = vectors
    (
        qkv_mat,
        proj_mat,
        fc1_mat,
        fc2_mat,
        qkv_down,
        qkv_up,
        proj_down,
        proj_up,
        fc1_down,
        fc1_up,
        fc2_down,
        fc2_up,
    ) = (
        lax.all_gather(qkv_mat, "win", axis=1, tiled=True),
        lax.all_gather(proj_mat, "win", axis=1, tiled=True),
        lax.all_gather(fc1_mat, "win", axis=1, tiled=True),
        lax.all_gather(fc2_mat, "win", axis=1, tiled=True),
        lax.all_gather(qkv_down, "win", axis=0, tiled=True),
        lax.all_gather(qkv_up, "win", axis=0, tiled=True),
        lax.all_gather(proj_down, "win", axis=0, tiled=True),
        lax.all_gather(proj_up, "win", axis=0, tiled=True),
        lax.all_gather(fc1_down, "win", axis=0, tiled=True),
        lax.all_gather(fc1_up, "win", axis=0, tiled=True),
        lax.all_gather(fc2_down, "win", axis=0, tiled=True),
        lax.all_gather(fc2_up, "win", axis=0, tiled=True),
    )
    return (
        lax.all_gather(qkv_mat, "clip", axis=0, tiled=True),
        lax.all_gather(proj_mat, "clip", axis=0, tiled=True),
        lax.all_gather(fc1_mat, "clip", axis=0, tiled=True),
        lax.all_gather(fc2_mat, "clip", axis=0, tiled=True),
        lax.all_gather(qkv_down, "clip", axis=1, tiled=True),
        lax.all_gather(qkv_up, "clip", axis=2, tiled=True),
        lax.all_gather(proj_down, "clip", axis=1, tiled=True),
        lax.all_gather(proj_up, "clip", axis=2, tiled=True),
        lax.all_gather(fc1_down, "clip", axis=1, tiled=True),
        lax.all_gather(fc1_up, "clip", axis=2, tiled=True),
        lax.all_gather(fc2_down, "clip", axis=1, tiled=True),
        lax.all_gather(fc2_up, "clip", axis=2, tiled=True),
        lax.all_gather(gain_first, "clip", axis=0, tiled=True),
        lax.all_gather(qkv_bias, "clip", axis=0, tiled=True),
        lax.all_gather(proj_bias, "clip", axis=0, tiled=True),
        lax.all_gather(gain_second, "clip", axis=0, tiled=True),
        lax.all_gather(fc1_bias, "clip", axis=0, tiled=True),
        lax.all_gather(fc2_bias, "clip", axis=0, tiled=True),
    )


def gather_backward(matrices, vectors):
    (
        qkv_mat,
        proj_mat,
        fc1_mat,
        fc2_mat,
        qkv_down,
        qkv_up,
        proj_down,
        proj_up,
        fc1_down,
        fc1_up,
        fc2_down,
        fc2_up,
    ) = matrices
    gain_first, qkv_bias, proj_bias, gain_second, fc1_bias, fc2_bias = vectors
    (
        qkv_mat,
        proj_mat,
        fc1_mat,
        fc2_mat,
        qkv_down,
        qkv_up,
        proj_down,
        proj_up,
        fc1_down,
        fc1_up,
        fc2_down,
        fc2_up,
    ) = (
        lax.all_gather(qkv_mat, "win", axis=1, tiled=True),
        lax.all_gather(proj_mat, "win", axis=1, tiled=True),
        lax.all_gather(fc1_mat, "win", axis=1, tiled=True),
        lax.all_gather(fc2_mat, "win", axis=1, tiled=True),
        lax.all_gather(qkv_down, "win", axis=0, tiled=True),
        lax.all_gather(qkv_up, "win", axis=0, tiled=True),
        lax.all_gather(proj_down, "win", axis=0, tiled=True),
        lax.all_gather(proj_up, "win", axis=0, tiled=True),
        lax.all_gather(fc1_down, "win", axis=0, tiled=True),
        lax.all_gather(fc1_up, "win", axis=0, tiled=True),
        lax.all_gather(fc2_down, "win", axis=0, tiled=True),
        lax.all_gather(fc2_up, "win", axis=0, tiled=True),
    )
    return (
        lax.all_gather(qkv_mat, "clip", axis=0, tiled=True),
        lax.all_gather(proj_mat, "clip", axis=0, tiled=True),
        lax.all_gather(fc1_mat, "clip", axis=0, tiled=True),
        lax.all_gather(fc2_mat, "clip", axis=0, tiled=True),
        lax.all_gather(qkv_down, "clip", axis=1, tiled=True),
        lax.all_gather(qkv_up, "clip", axis=2, tiled=True),
        lax.all_gather(proj_down, "clip", axis=1, tiled=True),
        lax.all_gather(proj_up, "clip", axis=2, tiled=True),
        lax.all_gather(fc1_down, "clip", axis=1, tiled=True),
        lax.all_gather(fc1_up, "clip", axis=2, tiled=True),
        lax.all_gather(fc2_down, "clip", axis=1, tiled=True),
        lax.all_gather(fc2_up, "clip", axis=2, tiled=True),
        lax.all_gather(gain_first, "clip", axis=0, tiled=True),
        lax.all_gather(qkv_bias, "clip", axis=0, tiled=True),
        lax.all_gather(proj_bias, "clip", axis=0, tiled=True),
        lax.all_gather(gain_second, "clip", axis=0, tiled=True),
        lax.all_gather(fc1_bias, "clip", axis=0, tiled=True),
        lax.all_gather(fc2_bias, "clip", axis=0, tiled=True),
    )


def window_tables(win_index, local_count, table):
    token_ids = jnp.arange(392)
    depth_pos = token_ids // 49
    height_pos = token_ids // 7 % 7
    width_pos = token_ids % 7
    relative = (
        (depth_pos[:, None] - depth_pos[None, :] + 7) * 169
        + (height_pos[:, None] - height_pos[None, :] + 6) * 13
        + (width_pos[:, None] - width_pos[None, :] + 6)
    )
    pos_bias = jnp.take(table.astype(jnp.float32), relative, axis=1)
    window_ids = win_index * local_count + jnp.arange(local_count)
    labels = window_ids[:, None] // 4 % 2 * (depth_pos[None, :] >= 4).astype(jnp.int32) * 4
    labels = (
        labels + window_ids[:, None] // 2 % 2 * (height_pos[None, :] >= 4).astype(jnp.int32) * 2
    )
    labels = labels + window_ids[:, None] % 2 * (width_pos[None, :] >= 4).astype(jnp.int32)
    return (pos_bias, labels[:, :, None] == labels[:, None, :])


def select_adapters(hot_low, tables):
    return tuple(
        (
            jnp.einsum("ca,a...->c...", hot_low, table, preferred_element_type=jnp.float32).astype(
                jnp.bfloat16
            )
            for table in tables
        )
    )


def spread_rows(hot_float, per_clip):
    return jnp.sum(hot_float[:, :, None, None] * per_clip[:, None], axis=0)


def per_device(
    tokens,
    cotangent,
    adapter_ids,
    ln1_gain,
    qkv_weight,
    qkv_bias,
    proj_weight,
    proj_bias,
    ln2_gain,
    fc1_weight,
    fc1_bias,
    fc2_weight,
    fc2_bias,
    bias_table,
    qkv_down,
    qkv_up,
    proj_down,
    proj_up,
    fc1_down,
    fc1_up,
    fc2_down,
    fc2_up,
):
    clip_count, local_count, window_tokens, features = tokens.shape
    local_bits = local_count.bit_length() - 1
    head_count = bias_table.shape[0]
    head_size = features // head_count
    scale = head_size ** (-0.5)
    row_count = local_count * window_tokens
    item_count = clip_count * local_count
    grid_shape = (
        clip_count,
        max(local_count // 4, 1),
        min(max(local_count // 2, 1), 2),
        min(local_count, 2),
        8,
        7,
        7,
        features,
    )
    flat_shape = (clip_count, row_count, features)
    matrices = (
        qkv_weight,
        proj_weight,
        fc1_weight,
        fc2_weight,
        qkv_down,
        qkv_up,
        proj_down,
        proj_up,
        fc1_down,
        fc1_up,
        fc2_down,
        fc2_up,
    )
    vectors = (ln1_gain, qkv_bias, proj_bias, ln2_gain, fc1_bias, fc2_bias)
    gathered = gather_forward(matrices, vectors)
    adapter_count = gathered[4].shape[0]
    hot = adapter_ids[:, None] == jnp.arange(adapter_count, dtype=jnp.int32)[None, :]
    hot_low = hot.astype(jnp.bfloat16)
    hot_float = hot.astype(jnp.float32)
    triple_input_weight, projection_weight_matrix, hidden_dense_weight, outer_dense_weight = (
        gathered[0],
        gathered[1],
        gathered[2],
        gathered[3],
    )
    (
        triple_down_matrix,
        triple_up_matrix,
        projection_down_matrix,
        projection_up_matrix,
        hidden_down_matrix,
        hidden_up_matrix,
        outer_down_matrix,
        outer_up_matrix,
    ) = select_adapters(hot_low, gathered[4:12])
    gain_first = gathered[12].astype(jnp.float32)
    triple_input_bias = gathered[13].astype(jnp.float32)
    projection_bias_vector = gathered[14].astype(jnp.float32)
    gain_second = gathered[15].astype(jnp.float32)
    hidden_dense_bias = gathered[16].astype(jnp.float32)
    outer_dense_bias = gathered[17].astype(jnp.float32)
    pos_bias, allowed = window_tables(lax.axis_index("win"), local_count, bias_table)
    allowed_items = jnp.broadcast_to(
        allowed[None], (clip_count, local_count, window_tokens, window_tokens)
    ).reshape(item_count, window_tokens, window_tokens)
    tokens_in = tokens.reshape(flat_shape)
    gradient_output = cotangent.reshape(flat_shape)
    input_tokens = tokens_in.astype(jnp.float32)
    first_norm, normed_first, inverse_first = norm_rows(input_tokens, gain_first)
    first_low = first_norm.astype(jnp.bfloat16)
    rolled_tokens = cyclic_move(
        first_low.reshape(grid_shape),
        local_bits,
        lambda piece, bit_number: swapped(piece, "win", bit_number),
        True,
    ).reshape(flat_shape)
    triple_reduced, triple_adapter = apply_low_rank(
        rolled_tokens, triple_down_matrix, triple_up_matrix
    )
    triple_rows = (
        linear_project(rolled_tokens, triple_input_weight) + triple_input_bias + triple_adapter
    )
    head_shape = (item_count, window_tokens, head_count, head_size)
    query = triple_rows[..., :features].astype(jnp.bfloat16).reshape(head_shape)
    keys_all = triple_rows[..., features : 2 * features].astype(jnp.bfloat16).reshape(head_shape)
    values_all = triple_rows[..., 2 * features :].astype(jnp.bfloat16).reshape(head_shape)
    attended, log_totals = lax.map(
        lambda operands: attend_forward(operands, pos_bias, scale),
        (query, keys_all, values_all, allowed_items),
    )
    unshifted_tokens = cyclic_move(
        attended.reshape(grid_shape),
        local_bits,
        lambda piece, bit_number: swapped(piece, "win", bit_number),
        False,
    ).reshape(flat_shape)
    projection_reduced, projection_adapter = apply_low_rank(
        unshifted_tokens, projection_down_matrix, projection_up_matrix
    )
    middle_state = (
        input_tokens
        + linear_project(unshifted_tokens, projection_weight_matrix)
        + projection_bias_vector
        + projection_adapter
    )
    second_norm, normed_second, inverse_second = norm_rows(middle_state, gain_second)
    second_low_rank = second_norm.astype(jnp.bfloat16)
    hidden_rank_reduced, hidden_adapter = apply_low_rank(
        second_low_rank, hidden_down_matrix, hidden_up_matrix
    )
    preactivation = (
        linear_project(second_low_rank, hidden_dense_weight) + hidden_dense_bias + hidden_adapter
    )
    erf_part = lax.erf(preactivation * inverse_root_two)
    gelu_activated = (0.5 * preactivation * (1.0 + erf_part)).astype(jnp.bfloat16)
    outer_rank_reduced, outer_adapter = apply_low_rank(
        gelu_activated, outer_down_matrix, outer_up_matrix
    )
    output_tokens = (
        middle_state
        + linear_project(gelu_activated, outer_dense_weight)
        + outer_dense_bias
        + outer_adapter
    )
    out_low = output_tokens.astype(jnp.bfloat16)
    again = gather_backward(matrices, vectors)
    triple_input_weight, projection_weight_matrix, hidden_dense_weight, outer_dense_weight = (
        again[0],
        again[1],
        again[2],
        again[3],
    )
    (
        triple_down_matrix,
        triple_up_matrix,
        projection_down_matrix,
        projection_up_matrix,
        hidden_down_matrix,
        hidden_up_matrix,
        outer_down_matrix,
        outer_up_matrix,
    ) = select_adapters(hot_low, again[4:12])
    gain_first = again[12].astype(jnp.float32)
    gain_second = again[15].astype(jnp.float32)
    gradient_outer_down, gradient_outer_up, gradient_outer_adapter = adapter_backward(
        gelu_activated, outer_rank_reduced, gradient_output, outer_down_matrix, outer_up_matrix
    )
    gradient_activation = (
        linear_project_backward(gradient_output, outer_dense_weight) + gradient_outer_adapter
    )
    slope = (
        0.5 * (1.0 + erf_part)
        + preactivation * jnp.exp(-0.5 * preactivation * preactivation) * inverse_root_tau
    )
    gradient_preactivation = (gradient_activation * slope).astype(jnp.bfloat16)
    gradient_hidden_down, gradient_hidden_up, gradient_hidden_adapter = adapter_backward(
        second_low_rank,
        hidden_rank_reduced,
        gradient_preactivation,
        hidden_down_matrix,
        hidden_up_matrix,
    )
    gradient_second_half = (
        linear_project_backward(gradient_preactivation, hidden_dense_weight)
        + gradient_hidden_adapter
    )
    grad_middle = gradient_output.astype(jnp.float32) + norm_back(
        gradient_second_half, gain_second, normed_second, inverse_second
    )
    gradient_branch_path = grad_middle.astype(jnp.bfloat16)
    gradient_projection_down, gradient_projection_up, gradient_projection_adapter = (
        adapter_backward(
            unshifted_tokens,
            projection_reduced,
            gradient_branch_path,
            projection_down_matrix,
            projection_up_matrix,
        )
    )
    gradient_unshifted = (
        linear_project_backward(gradient_branch_path, projection_weight_matrix)
        + gradient_projection_adapter
    ).astype(jnp.bfloat16)
    grad_attended = cyclic_move(
        gradient_unshifted.reshape(grid_shape),
        local_bits,
        lambda piece, bit_number: swapped(piece, "win", bit_number),
        True,
    ).reshape(head_shape)
    grad_query, grad_keys, grad_values = lax.map(
        lambda operands: attend_backward(operands, pos_bias, scale),
        (query, keys_all, values_all, allowed_items, log_totals, grad_attended),
    )
    gradient_triple_rows = jnp.concatenate(
        (
            grad_query.reshape(flat_shape),
            grad_keys.reshape(flat_shape),
            grad_values.reshape(flat_shape),
        ),
        axis=-1,
    )
    gradient_triple_down, gradient_triple_up, gradient_triple_adapter = adapter_backward(
        rolled_tokens, triple_reduced, gradient_triple_rows, triple_down_matrix, triple_up_matrix
    )
    gradient_rolled = (
        linear_project_backward(gradient_triple_rows, triple_input_weight) + gradient_triple_adapter
    ).astype(jnp.bfloat16)
    grad_first = cyclic_move(
        gradient_rolled.reshape(grid_shape),
        local_bits,
        lambda piece, bit_number: swapped(piece, "win", bit_number),
        False,
    ).reshape(flat_shape)
    grad_inputs = grad_middle + norm_back(
        grad_first.astype(jnp.float32), gain_first, normed_first, inverse_first
    )
    grad_low = grad_inputs.astype(jnp.bfloat16)
    activations = out_low.reshape(clip_count, local_count, window_tokens, features)
    input_grad = grad_low.reshape(clip_count, local_count, window_tokens, features)
    sum_qkv_down = spread_rows(hot_float, gradient_triple_down)
    sum_qkv_up = spread_rows(hot_float, gradient_triple_up)
    sum_proj_down = spread_rows(hot_float, gradient_projection_down)
    sum_proj_up = spread_rows(hot_float, gradient_projection_up)
    sum_fc1_down = spread_rows(hot_float, gradient_hidden_down)
    sum_fc1_up = spread_rows(hot_float, gradient_hidden_up)
    sum_fc2_down = spread_rows(hot_float, gradient_outer_down)
    sum_fc2_up = spread_rows(hot_float, gradient_outer_up)
    (
        sum_qkv_down,
        sum_qkv_up,
        sum_proj_down,
        sum_proj_up,
        sum_fc1_down,
        sum_fc1_up,
        sum_fc2_down,
        sum_fc2_up,
    ) = (
        lax.psum_scatter(
            sum_qkv_down.astype(jnp.bfloat16), "clip", scatter_dimension=1, tiled=True
        ).astype(jnp.float32),
        lax.psum_scatter(
            sum_qkv_up.astype(jnp.bfloat16), "clip", scatter_dimension=2, tiled=True
        ).astype(jnp.float32),
        lax.psum_scatter(
            sum_proj_down.astype(jnp.bfloat16), "clip", scatter_dimension=1, tiled=True
        ).astype(jnp.float32),
        lax.psum_scatter(
            sum_proj_up.astype(jnp.bfloat16), "clip", scatter_dimension=2, tiled=True
        ).astype(jnp.float32),
        lax.psum_scatter(
            sum_fc1_down.astype(jnp.bfloat16), "clip", scatter_dimension=1, tiled=True
        ).astype(jnp.float32),
        lax.psum_scatter(
            sum_fc1_up.astype(jnp.bfloat16), "clip", scatter_dimension=2, tiled=True
        ).astype(jnp.float32),
        lax.psum_scatter(
            sum_fc2_down.astype(jnp.bfloat16), "clip", scatter_dimension=1, tiled=True
        ).astype(jnp.float32),
        lax.psum_scatter(
            sum_fc2_up.astype(jnp.bfloat16), "clip", scatter_dimension=2, tiled=True
        ).astype(jnp.float32),
    )
    (
        sum_qkv_down,
        sum_qkv_up,
        sum_proj_down,
        sum_proj_up,
        sum_fc1_down,
        sum_fc1_up,
        sum_fc2_down,
        sum_fc2_up,
    ) = (
        lax.psum_scatter(
            sum_qkv_down.astype(jnp.bfloat16), "win", scatter_dimension=0, tiled=True
        ).astype(jnp.float32),
        lax.psum_scatter(
            sum_qkv_up.astype(jnp.bfloat16), "win", scatter_dimension=0, tiled=True
        ).astype(jnp.float32),
        lax.psum_scatter(
            sum_proj_down.astype(jnp.bfloat16), "win", scatter_dimension=0, tiled=True
        ).astype(jnp.float32),
        lax.psum_scatter(
            sum_proj_up.astype(jnp.bfloat16), "win", scatter_dimension=0, tiled=True
        ).astype(jnp.float32),
        lax.psum_scatter(
            sum_fc1_down.astype(jnp.bfloat16), "win", scatter_dimension=0, tiled=True
        ).astype(jnp.float32),
        lax.psum_scatter(
            sum_fc1_up.astype(jnp.bfloat16), "win", scatter_dimension=0, tiled=True
        ).astype(jnp.float32),
        lax.psum_scatter(
            sum_fc2_down.astype(jnp.bfloat16), "win", scatter_dimension=0, tiled=True
        ).astype(jnp.float32),
        lax.psum_scatter(
            sum_fc2_up.astype(jnp.bfloat16), "win", scatter_dimension=0, tiled=True
        ).astype(jnp.float32),
    )
    return (
        activations,
        input_grad,
        sum_qkv_down,
        sum_qkv_up,
        sum_proj_down,
        sum_proj_up,
        sum_fc1_down,
        sum_fc1_up,
        sum_fc2_down,
        sum_fc2_up,
    )


def solution(mesh):
    return jax.shard_map(
        per_device,
        mesh=mesh,
        in_specs=(
            P("clip", "win", None, None),
            P("clip", "win", None, None),
            P("clip"),
            P("clip"),
            P("clip", "win"),
            P("clip"),
            P("clip", "win"),
            P("clip"),
            P("clip"),
            P("clip", "win"),
            P("clip"),
            P("clip", "win"),
            P("clip"),
            P(),
            P("win", "clip", None),
            P("win", None, "clip"),
            P("win", "clip", None),
            P("win", None, "clip"),
            P("win", "clip", None),
            P("win", None, "clip"),
            P("win", "clip", None),
            P("win", None, "clip"),
        ),
        out_specs=(
            P("clip", "win", None, None),
            P("clip", "win", None, None),
            P("win", "clip", None),
            P("win", None, "clip"),
            P("win", "clip", None),
            P("win", None, "clip"),
            P("win", "clip", None),
            P("win", None, "clip"),
            P("win", "clip", None),
            P("win", None, "clip"),
        ),
        check_vma=False,
    )
```

profile of v0, /device:TPU:0, one launch (start us, length us, event | category | flops | bytes accessed | tf_op | source)
XLA Modules:
  0.0 1969.4 jit_solution(8495276521311042542)
XLA Ops:
  29.8 22.9 %all-reduce.5 = (bf16[512]{0:T(512)(128)(2,1)}, bf16[512]{0:T(512)(128)(2,1)S(1)}, bf16[1536]{0:T(1024)(128)(2,1)S(1)}, bf16[512]{0:T(512)(128)(2,1)}, bf16[512]{0:T(512)(128)(2,1)}) all-reduce(bf16[512]{0:T(512)(128)(2,1)S(1)} %dynamic-update-slice.2, ...), channel_id=1, replica_groups=mesh['clip'=8,'win'=4] {'clip'}, use_global_device_ids=true, to_apply=%add.2 | all-reduce | flops 3584 | bytes 14336
  105.3 34.5 %all_gather.121 = bf16[8,512,16]{2,0,1:T(8,128)(2,1)S(1)} all-gather(bf16[8,64,16]{2,0,1:T(8,128)(2,1)S(1)} %copy.402), channel_id=1, replica_groups=mesh['clip'=8,'win'=4] {'clip'}, dimensions={1}, use_global_device_ids=true | all-gather | bytes 147456 | tf_op jit(solution)/shard_map/all_gather | solution.py:172
  146.7 72.6 %all_gather.123 = bf16[8,16,1536]{1,0,2:T(8,128)(2,1)S(1)} all-gather(bf16[8,16,192]{1,0,2:T(8,128)(2,1)S(1)} %copy.406), channel_id=1, replica_groups=mesh['clip'=8,'win'=4] {'clip'}, dimensions={2}, use_global_device_ids=true | all-gather | bytes 442368 | tf_op jit(solution)/shard_map/all_gather | solution.py:173
  225.0 281.5 %gather_fusion = f32[153664,16]{1,0:T(8,128)} fusion(f32[16,2535]{0,1:T(8,128)S(1)} %copy.412, s32[154624]{0:T(1024)S(1)} %pad_clamp_fusion), kind=kCustom, calls=%fused_computation | custom fusion | bytes 20283648 | tf_op jit(solution)/shard_map/jit(_take)/gather | solution.py:264
  506.4 54.5 %copy.413 = f32[392,392,16]{0,1,2:T(8,128)} copy(f32[392,392,16]{2,1,0:T(8,128)} %bitcast.27) | data formatting | bytes 19668992 | tf_op jit(solution)/shard_map/jit(_take)/gather | solution.py:264
  566.3 33.2 %all_gather.125 = bf16[512,512]{1,0:T(8,128)(2,1)} all-gather(bf16[64,512]{1,0:T(8,128)(2,1)S(1)} %all_gather.124), channel_id=1, replica_groups=mesh['clip'=8,'win'=4] {'clip'}, dimensions={0}, use_global_device_ids=true | all-gather | bytes 589824 | tf_op jit(solution)/shard_map/all_gather | solution.py:169
  604.9 33.0 %all_gather.128 = bf16[8,512,16]{2,0,1:T(8,128)(2,1)S(1)} all-gather(bf16[8,64,16]{2,0,1:T(8,128)(2,1)S(1)} %copy.420), channel_id=1, replica_groups=mesh['clip'=8,'win'=4] {'clip'}, dimensions={1}, use_global_device_ids=true | all-gather | bytes 147456 | tf_op jit(solution)/shard_map/all_gather | solution.py:174
  645.2 32.9 %all_gather.130 = bf16[8,16,512]{1,0,2:T(8,128)(2,1)S(1)} all-gather(bf16[8,16,64]{1,0,2:T(8,128)(2,1)S(1)} %copy.424), channel_id=1, replica_groups=mesh['clip'=8,'win'=4] {'clip'}, dimensions={2}, use_global_device_ids=true | all-gather | bytes 147456 | tf_op jit(solution)/shard_map/all_gather | solution.py:175
  685.1 32.9 %all_gather.136 = bf16[8,512,16]{2,0,1:T(8,128)(2,1)S(1)} all-gather(bf16[8,64,16]{2,0,1:T(8,128)(2,1)S(1)} %copy.427), channel_id=1, replica_groups=mesh['clip'=8,'win'=4] {'clip'}, dimensions={1}, use_global_device_ids=true | all-gather | bytes 147456 | tf_op jit(solution)/shard_map/all_gather | solution.py:176
  741.7 33.0 %all_gather.145 = bf16[8,16,512]{1,0,2:T(8,128)(2,1)S(1)} all-gather(bf16[8,16,64]{1,0,2:T(8,128)(2,1)S(1)} %copy.434), channel_id=1, replica_groups=mesh['clip'=8,'win'=4] {'clip'}, dimensions={2}, use_global_device_ids=true | all-gather | bytes 147456 | tf_op jit(solution)/shard_map/all_gather | solution.py:179
  781.4 33.3 %all_gather.138 = bf16[8,16,2048]{2,0,1:T(8,128)(2,1)} all-gather(bf16[8,16,256]{2,0,1:T(8,128)(2,1)S(1)} %copy.430), channel_id=1, replica_groups=mesh['clip'=8,'win'=4] {'clip'}, dimensions={2}, use_global_device_ids=true | all-gather | bytes 589824 | tf_op jit(solution)/shard_map/all_gather | solution.py:177
  814.7 33.2 %all_gather.143 = bf16[8,2048,16]{1,0,2:T(8,128)(2,1)} all-gather(bf16[8,256,16]{1,0,2:T(8,128)(2,1)S(1)} %copy.432), channel_id=1, replica_groups=mesh['clip'=8,'win'=4] {'clip'}, dimensions={1}, use_global_device_ids=true | all-gather | bytes 589824 | tf_op jit(solution)/shard_map/all_gather | solution.py:178
  921.4 55.2 %while.26 = (s32[]{:T(128)}, bf16[4,392,16,32]{1,3,2,0:T(8,128)(2,1)}, f32[4,16,392]{2,1,0:T(8,128)}, bf16[4,392,16,32]{1,3,2,0:T(8,128)(2,1)S(1)}, pred[4,392,3...) while((s32[]{:T(128)}, ...), condition=%wide.region_5.6_spmd, body=%wide.region_2.5_spmd.sunk | while | flops 334567296 | bytes 48135968 | solution.py:398
  1021.9 18.5 all-gather
  1196.2 253.5 %while.27 = (s32[]{:T(128)}, bf16[4,392,16,32]{1,3,2,0:T(8,128)(2,1)}, bf16[4,392,16,32]{1,3,2,0:T(8,128)(2,1)}, bf16[4,392,16,32]{1,3,2,0:T(8,128)(2,1)}, bf16[...) while((s32[]{:T(128)}, ...), condition=%wide.region_12.13_spmd, body=%wide.region_10.12_spmd.sunk | while | flops 824254464 | bytes 153958656 | solution.py:501
  1233.7 18.5 fusion.257
  1278.8 18.3 fusion.258
  1297.1 18.4 fusion.257
  1342.0 18.3 fusion.258
  1360.3 18.5 fusion.257
  1423.6 18.5 fusion.257
  1526.9 30.9 %reduce-scatter.49.cloned.1.call-done = bf16[64,128]{1,0:T(8,128)(2,1)} async-done(((bf16[512,128]{1,0:T(8,128)(2,1)}), bf16[64,128]{1,0:T(8,128)(2,1)}) %reduce-scatter.49.cloned.1.call-update) | async-done | bytes 16400
  1559.5 61.6 %reduce-scatter.53.cloned.1.call-done = bf16[64,128]{1,0:T(8,128)(2,1)} async-done(((bf16[512,128]{1,0:T(8,128)(2,1)}), bf16[64,128]{1,0:T(8,128)(2,1)}) %reduce-scatter.53.cloned.1.call-update) | async-done | bytes 16400
  1622.9 61.3 %reduce-scatter.57.cloned.1.call-done = bf16[64,128]{1,0:T(8,128)(2,1)} async-done(((bf16[512,128]{1,0:T(8,128)(2,1)}), bf16[64,128]{1,0:T(8,128)(2,1)}) %reduce-scatter.57.cloned.1.call-update) | async-done | bytes 16400
  1698.0 49.9 %reduce-scatter.51.cloned.1.call-done = bf16[192,128]{1,0:T(8,128)(2,1)} async-done(((bf16[1536,128]{1,0:T(8,128)(2,1)}), bf16[192,128]{1,0:T(8,128)(2,1)}) %reduce-scatter.51.cloned.1.call-update) | async-done | bytes 49168
  1770.5 21.2 %reduce-scatter.47.cloned.1.call-done = bf16[2,16,64]{2,1,0:T(8,128)(2,1)} async-done(((bf16[8,16,64]{2,1,0:T(8,128)(2,1)}), bf16[2,16,64]{2,1,0:T(8,128)(2,1)}) %reduce-scatter.47.cloned.1.call-update) | async-done | bytes 4112 | tf_op jit(solution)/shard_map/reduce_scatter | solution.py:605
  1793.0 20.4 %reduce-scatter.41.cloned.1.call-done = bf16[2,16,256]{2,1,0:T(8,128)(2,1)} async-done(((bf16[8,16,256]{2,1,0:T(8,128)(2,1)}), bf16[2,16,256]{2,1,0:T(8,128)(2,1)}) %reduce-scatter.41.cloned.1.call-update) | async-done | bytes 16400 | tf_op jit(solution)/shard_map/reduce_scatter | solution.py:599
  1814.7 20.5 %reduce-scatter.45.cloned.1.call-done = bf16[2,256,16]{1,2,0:T(8,128)(2,1)} async-done(((bf16[8,256,16]{1,2,0:T(8,128)(2,1)}), bf16[2,256,16]{1,2,0:T(8,128)(2,1)}) %reduce-scatter.45.cloned.1.call-update) | async-done | bytes 16400 | tf_op jit(solution)/shard_map/reduce_scatter | solution.py:602
  1836.5 20.9 %reduce-scatter.29.cloned.1.call-done = bf16[2,64,16]{1,2,0:T(8,128)(2,1)} async-done(((bf16[8,64,16]{1,2,0:T(8,128)(2,1)}), bf16[2,64,16]{1,2,0:T(8,128)(2,1)}) %reduce-scatter.29.cloned.1.call-update) | async-done | bytes 4112 | tf_op jit(solution)/shard_map/reduce_scatter | solution.py:584
  1858.7 20.5 %reduce-scatter.33.cloned.1.call-done = bf16[2,64,16]{1,2,0:T(8,128)(2,1)} async-done(((bf16[8,64,16]{1,2,0:T(8,128)(2,1)}), bf16[2,64,16]{1,2,0:T(8,128)(2,1)}) %reduce-scatter.33.cloned.1.call-update) | async-done | bytes 4112 | tf_op jit(solution)/shard_map/reduce_scatter | solution.py:590
  1880.5 20.3 %reduce-scatter.37.cloned.1.call-done = bf16[2,64,16]{1,2,0:T(8,128)(2,1)} async-done(((bf16[8,64,16]{1,2,0:T(8,128)(2,1)}), bf16[2,64,16]{1,2,0:T(8,128)(2,1)}) %reduce-scatter.37.cloned.1.call-update) | async-done | bytes 4112 | tf_op jit(solution)/shard_map/reduce_scatter | solution.py:596
  1904.0 18.9 reduce-scatter.31.cloned.1.call-done
  (541 shorter events, 778.6 us)
Async XLA Ops:
  7.2 866.3 %all-gather.5.cloned.1.call-start = ((), (), s32[]{:S(2)}) async-start(), calls=%async_computation.16 | async-start | bytes 1769472 | tf_op jit(solution)/shard_map/all_gather | solution.py:168
  16.0 1024.4 %all-gather.9.cloned.1.call-start = ((), (), s32[]{:S(2)}) async-start(), calls=%async_computation.18 | async-start | bytes 2359296 | tf_op jit(solution)/shard_map/all_gather | solution.py:171
  23.0 1051.1 %all-gather.7.cloned.1.call-start = ((), (), s32[]{:S(2)}) async-start(), calls=%async_computation.17 | async-start | bytes 2359296 | tf_op jit(solution)/shard_map/all_gather | solution.py:170
  75.5 773.5 %collective-permute-start = (bf16[2,1,1,2,4,7,7,512]{7,3,6,5,4,0,2,1:T(2,128)(2,1)}, bf16[2,1,1,2,4,7,7,512]{7,3,6,5,4,0,2,1:T(2,128)(2,1)}, u32[]{:S(2)}, u32[]{:S(2)}) collective-permute-start(bf16[2,1,1,2,4,7,7,512]{7,3,6,5,4,0,2,1:T(2,128)(2,1)} %get-tuple-element.297), channel_id=1, source_target_pairs={{0,2},{1,3},{2,0},{3,1},{4,6},{5,7},{6,4},{7,5},{8,10},{9,11},{10,... | collective-permute-start | bytes 2408456 | tf_op jit(solution)/shard_map/ppermute | solution.py:13
  94.7 1427.8 %reduce-scatter.55.cloned.1.call-start = ((), (), s32[]{:S(2)}) async-start(), calls=%async_computation.32 | async-start | bytes 147456
  560.9 118.9 %copy-start.91 = (bf16[2,64,16]{1,2,0:T(8,128)(2,1)S(1)}, bf16[2,64,16]{1,2,0:T(8,128)(2,1)}, u32[]{:S(2)}) copy-start(bf16[2,64,16]{1,2,0:T(8,128)(2,1)} %param.44) | copy-start | bytes 12292
  639.0 233.9 %copy-start.65 = (bf16[2,512,16]{1,0,2:T(2,128)(2,1)}, bf16[2,512,16]{1,0,2:T(2,128)(2,1)S(1)}, u32[]{:S(2)}) copy-start(bf16[2,512,16]{1,0,2:T(2,128)(2,1)S(1)} %convolution_convert_fusion.13) | copy-start | bytes 98308
  730.8 118.2 %copy-start.25 = (bf16[2,1,1,2,4,7,7,512]{7,3,6,5,4,0,2,1:T(2,128)(2,1)S(1)}, bf16[2,1,1,2,4,7,7,512]{7,3,6,5,4,0,2,1:T(2,128)(2,1)}, u32[]{:S(2)}) copy-start(bf16[2,1,1,2,4,7,7,512]{7,3,6,5,4,0,2,1:T(2,128)(2,1)} %get-tuple-element.296) | copy-start | bytes 2408452
  741.7 109.3 %copy-start.46 = (bf16[8,512,16]{1,0,2:T(8,128)(2,1)S(1)}, bf16[8,512,16]{1,0,2:T(8,128)(2,1)}, u32[]{:S(2)}) copy-start(bf16[8,512,16]{1,0,2:T(8,128)(2,1)} %copy.428) | copy-start | bytes 393220
  850.9 12.5 collective-permute-start.1
  997.8 20.3 %collective-permute-start.2 = (bf16[2,1,1,2,4,7,7,512]{7,3,0,6,5,4,2,1:T(2,128)(2,1)S(1)}, bf16[2,1,1,2,4,7,7,512]{7,3,0,6,5,4,2,1:T(2,128)(2,1)S(1)}, u32[]{:S(2)}, u32[]{:S(2)}) collective-permute-start(bf16[2,1,1,2,4,7,7,512]{7,3,0,6,5,4,2,1:T(2,128)(2,1)S(1)} %get-tuple-element.294), channel_id=1, source_target_pairs={{0,2},{1,3},{2,0},{3,1},{4,6},{5,7},{6,4},{7,5},{8,10},{9,11},{10,... | collective-permute-start | bytes 2408456 | tf_op jit(solution)/shard_map/ppermute | solution.py:13
  1019.9 30.9 %collective-permute-start.3 = (bf16[2,1,1,2,8,3,7,512]{7,3,0,6,5,4,2,1:T(2,128)(2,1)}, bf16[2,1,1,2,8,3,7,512]{7,3,0,6,5,4,2,1:T(2,128)(2,1)}, u32[]{:S(2)}, u32[]{:S(2)}) collective-permute-start(bf16[2,1,1,2,8,3,7,512]{7,3,0,6,5,4,2,1:T(2,128)(2,1)} %pad_maximum_fusion.10), channel_id=1, source_target_pairs={{0,1},{1,0},{2,3},{3,2},{4,5},{5,4},{6,7},{7,6},{8,9},{9,8},{10,11... | collective-permute-start | bytes 2064392 | tf_op jit(solution)/shard_map/ppermute | solution.py:13
  1127.7 396.4 %reduce-scatter.59.cloned.1.call-start = ((), (), s32[]{:S(2)}) async-start(), calls=%async_computation.34 | async-start | bytes 147456
  1136.3 389.5 %reduce-scatter.39.cloned.1.call-start = ((), (), s32[]{:S(2)}) async-start(), calls=%async_computation.24 | async-start | bytes 589824 | tf_op jit(solution)/shard_map/reduce_scatter | solution.py:564
  1143.1 383.2 %reduce-scatter.43.cloned.1.call-start = ((), (), s32[]{:S(2)}) async-start(), calls=%async_computation.26 | async-start | bytes 589824 | tf_op jit(solution)/shard_map/reduce_scatter | solution.py:567
  1145.4 16.8 collective-permute-start.4
  1151.3 406.5 %reduce-scatter.49.cloned.1.call-start = ((), (), s32[]{:S(2)}) async-start(), calls=%async_computation.29 | async-start | bytes 147456
  1164.2 4.3 collective-permute-start.5
  1500.0 121.1 %reduce-scatter.53.cloned.1.call-start = ((), (), s32[]{:S(2)}) async-start(), calls=%async_computation.31 | async-start | bytes 147456
  1502.3 181.9 %reduce-scatter.57.cloned.1.call-start = ((), (), s32[]{:S(2)}) async-start(), calls=%async_computation.33 | async-start | bytes 147456
  1504.5 243.4 %reduce-scatter.51.cloned.1.call-start = ((), (), s32[]{:S(2)}) async-start(), calls=%async_computation.30 | async-start | bytes 442368
  1512.3 256.9 %reduce-scatter.35.cloned.1.call-start = ((), (), s32[]{:S(2)}) async-start(), calls=%async_computation.22 | async-start | bytes 40960 | tf_op jit(solution)/shard_map/reduce_scatter | solution.py:593
  1521.5 164.5 %collective-permute-start.6 = (bf16[2,1,1,2,4,7,7,512]{7,3,6,5,4,0,2,1:T(2,128)(2,1)S(1)}, bf16[2,1,1,2,4,7,7,512]{7,3,6,5,4,0,2,1:T(2,128)(2,1)S(1)}, u32[]{:S(2)}, u32[]{:S(2)}) collective-permute-start(bf16[2,1,1,2,4,7,7,512]{7,3,6,5,4,0,2,1:T(2,128)(2,1)S(1)} %copy.484), channel_id=1, source_target_pairs={{0,2},{1,3},{2,0},{3,1},{4,6},{5,7},{6,4},{7,5},{8,10},{9,11},{10,... | collective-permute-start | bytes 2408456 | tf_op jit(solution)/shard_map/ppermute | solution.py:13
  1524.0 267.6 %reduce-scatter.47.cloned.1.call-start = ((), (), s32[]{:S(2)}) async-start(), calls=%async_computation.28 | async-start | bytes 40960 | tf_op jit(solution)/shard_map/reduce_scatter | solution.py:605
  1525.7 287.6 %reduce-scatter.41.cloned.1.call-start = ((), (), s32[]{:S(2)}) async-start(), calls=%async_computation.25 | async-start | bytes 81920 | tf_op jit(solution)/shard_map/reduce_scatter | solution.py:599
  1526.3 308.9 %reduce-scatter.45.cloned.1.call-start = ((), (), s32[]{:S(2)}) async-start(), calls=%async_computation.27 | async-start | bytes 81920 | tf_op jit(solution)/shard_map/reduce_scatter | solution.py:602
  1526.9 330.6 %reduce-scatter.29.cloned.1.call-start = ((), (), s32[]{:S(2)}) async-start(), calls=%async_computation.19 | async-start | bytes 40960 | tf_op jit(solution)/shard_map/reduce_scatter | solution.py:584
  1559.4 319.8 %reduce-scatter.33.cloned.1.call-start = ((), (), s32[]{:S(2)}) async-start(), calls=%async_computation.21 | async-start | bytes 40960 | tf_op jit(solution)/shard_map/reduce_scatter | solution.py:590
  1622.7 278.2 %reduce-scatter.37.cloned.1.call-start = ((), (), s32[]{:S(2)}) async-start(), calls=%async_computation.23 | async-start | bytes 40960 | tf_op jit(solution)/shard_map/reduce_scatter | solution.py:596
  1685.8 237.0 %reduce-scatter.31.cloned.1.call-start = ((), (), s32[]{:S(2)}) async-start(), calls=%async_computation.20 | async-start | bytes 81920 | tf_op jit(solution)/shard_map/reduce_scatter | solution.py:587
  1689.8 234.4 %collective-permute-start.7 = (bf16[2,1,1,2,8,3,7,512]{7,3,6,5,4,0,2,1:T(2,128)(2,1)}, bf16[2,1,1,2,8,3,7,512]{7,3,6,5,4,0,2,1:T(2,128)(2,1)}, u32[]{:S(2)}, u32[]{:S(2)}) collective-permute-start(bf16[2,1,1,2,8,3,7,512]{7,3,6,5,4,0,2,1:T(2,128)(2,1)} %slice.132), channel_id=1, source_target_pairs={{0,1},{1,0},{2,3},{3,2},{4,5},{5,4},{6,7},{7,6},{8,9},{9,8},{10,11... | collective-permute-start | bytes 2064392 | tf_op jit(solution)/shard_map/ppermute | solution.py:13
  1755.3 174.5 %copy-start.79 = (f32[512]{0:T(512)S(1)}, f32[512]{0:T(512)}, u32[]{:S(2)}) copy-start(f32[512]{0:T(512)} %copy-done.78) | copy-start | bytes 6148
  (99 other events, 1823.8 us)
Sparse Core Ops, SparseCore 0:
  16.1 44.4 all-gather.4
  62.8 48.9 all-gather.8
  113.9 78.7 all-gather.6
  1127.8 57.4 reduce-scatter.54
  1188.5 59.9 reduce-scatter.58
  1251.6 61.5 reduce-scatter.38
  1316.9 61.4 reduce-scatter.42
  1500.1 57.6 reduce-scatter.48
  1561.1 59.9 reduce-scatter.52
  1624.3 59.8 reduce-scatter.56
  1687.5 60.4 reduce-scatter.50
  1750.8 18.3 reduce-scatter.34
  1772.3 19.3 reduce-scatter.46
  1793.9 19.3 reduce-scatter.40
  1815.8 19.3 reduce-scatter.44
  1838.0 19.3 reduce-scatter.28
  1859.8 19.3 reduce-scatter.32
  1881.5 19.3 reduce-scatter.36
  1903.4 19.3 reduce-scatter.30
where the time goes:
time: 1980 us; the launch traced here: 1970 us
  local copies, waits for them, and re-layouts  573 us (29%)
  blocking collectives  461 us (23%)
  matrix products  400 us (20%)
  waiting for transfers between devices  390 us (20%)
  other arithmetic  123 us (6%)
    gather x2, local copies, waits for them, and re-layouts, window_tables(): pos_bias = jnp.take(table.astype(jnp.float32), relative, axis=1)  336 us
    unnamed x25, waiting for transfers between devices  205 us
    dot_general x4, matrix products, attend_backward(): jnp.einsum('hqk,khd->qhd', grad_raw, key_rows, preferred_element_type=jnp...  73.9 us
    dot_general x4, matrix products, attend_backward(): jnp.einsum('hqk,qhd->khd', grad_raw, query_rows, preferred_element_type=j...  73.2 us
    all_gather x1, blocking collectives, gather_forward(): lax.all_gather(qkv_up, 'clip', axis=2, tiled=True)  72.6 us
    unnamed x249, local copies, waits for them, and re-layouts  46.5 us
  transfers between devices with their start and end apart: 27, of which 14 were waited for; matrix products, arithmetic and copies ran while one was open for 51% of the time, Pallas kernels for 0%

commit v1 on v0

v1 whole, which is shorter than its diff:
```python
import functools
import jax
import jax.numpy as jnp
from jax import lax
from jax.experimental import pallas as pl
from jax.experimental.pallas import tpu as pltpu
from jax.sharding import PartitionSpec as P

BF = jnp.bfloat16
F32 = jnp.float32
NN = (((1,), (0,)), ((), ()))
NT = (((1,), (1,)), ((), ()))
TN = (((0,), (0,)), ((), ()))
LOG2E = 1.4426950408889634
LN2 = 0.6931471805599453
FAR = 1e9
VMEM_LIMIT = 60 * 2**20
TOK = 392


def dot(left, right, dims):
    return lax.dot_general(left, right, dims, preferred_element_type=F32)


def lane_ids(shape):
    return lax.broadcasted_iota(jnp.int32, shape, len(shape) - 1)


def norm_stats(values):
    average = jnp.mean(values, axis=-1, keepdims=True)
    centred = values - average
    variance = jnp.mean(centred * centred, axis=-1, keepdims=True)
    inverse = lax.rsqrt(variance + 1e-05)
    return centred * inverse, inverse


def norm_back(gradient, gain, normed, inverse):
    scaled = gradient * gain
    centre = jnp.mean(scaled, axis=-1, keepdims=True)
    slope = jnp.mean(scaled * normed, axis=-1, keepdims=True)
    return inverse * (scaled - centre - normed * slope)


def add_rows(ref, at, value, first):
    @pl.when(first)
    def _():
        ref[0, :, at] = value

    @pl.when(jnp.logical_not(first))
    def _():
        ref[0, :, at] += value


def attend_kernel(
    ids_ref,
    x_ref,
    gain_ref,
    weight_ref,
    bias_ref,
    down_ref,
    up_ref,
    key_mask_ref,
    query_mask_ref,
    table_ref,
    probs_ref,
    out_ref,
    qkv_ref,
    reduced_ref,
    keys,
    queries,
    values_t,
    out_t,
    scores,
    *,
    scale,
    per_group,
    width,
):
    group = pl.program_id(1)
    groups = pl.num_programs(1)
    feats = x_ref.shape[-1]

    @pl.when(group == 0)
    def _():
        normed, _ = norm_stats(x_ref[0].astype(F32))
        low = (normed * gain_ref[...]).astype(BF)
        reduced = dot(low, down_ref[0], NT).astype(BF)
        reduced_ref[0] = reduced

        def columns(part):
            at = pl.ds(part * feats, feats)
            return (
                dot(low, weight_ref[:, at], NN)
                + bias_ref[:, at]
                + dot(reduced, up_ref[0, :, at], NN)
            )

        query = (columns(0) * (scale * LOG2E)).astype(BF)
        queries[...] = query
        qkv_ref[0, :, :feats] = query
        key = columns(1).astype(BF)
        qkv_ref[0, :, feats : 2 * feats] = key
        for g in range(feats // 128):
            keys[:, 256 * g : 256 * g + 128] = key[:, 128 * g : 128 * g + 128]
            keys[:, 256 * g + 128 : 256 * g + 256] = key_mask_ref[0]
        value = columns(2)
        qkv_ref[0, :, 2 * feats :] = value.astype(BF)
        values_t[...] = value.T.astype(BF)

    keys_now = keys[:, pl.ds(pl.multiple_of(group * 256, 256), 256)]
    query_now = queries[:, pl.ds(pl.multiple_of(group * 128, 128), 128)]
    head_of_lane = lane_ids(query_now.shape) // width

    def raw(h):
        own = jnp.where(head_of_lane == h, query_now, jnp.zeros_like(query_now))
        own = jnp.concatenate([own, query_mask_ref[0]], axis=1)
        return dot(keys_now, own, NT) + table_ref[group * per_group + h]

    def finish(h):
        score = scores[h % 2]
        largest = jnp.max(score, axis=0, keepdims=True)
        probs = jnp.exp2(score - largest)
        total = jnp.sum(probs, axis=0, keepdims=True)
        probs = (probs * (1.0 / total)).astype(BF)
        probs_ref[0, h] = probs
        at = pl.ds(pl.multiple_of((group * per_group + h) * width, width), width)
        out_t[at, :] = dot(values_t[at, :], probs, NN)

    scores[0] = raw(0)
    for h in range(per_group):
        if h + 1 < per_group:
            scores[(h + 1) % 2] = raw(h + 1)
        finish(h)

    @pl.when(group == groups - 1)
    def _():
        out_ref[0] = out_t[...].T.astype(BF)


def dense_kernel(
    ids_ref,
    x_ref,
    attn_ref,
    dy_ref,
    gain_ref,
    proj_ref,
    proj_bias_ref,
    fc1_ref,
    fc1_bias_ref,
    fc2_ref,
    fc2_bias_ref,
    proj_down_ref,
    proj_up_ref,
    fc1_down_ref,
    fc1_up_ref,
    fc2_down_ref,
    fc2_up_ref,
    act_ref,
    dx1_ref,
    dattn_ref,
    grad_ref,
    *,
    per_clip,
    chunk,
):
    first = pl.program_id(0) % per_clip == 0
    feats = x_ref.shape[-1]
    hidden = fc1_ref.shape[-1]
    attn = attn_ref[0]
    reduced_proj = dot(attn, proj_down_ref[0], NT).astype(BF)
    middle = (
        x_ref[0].astype(F32)
        + dot(attn, proj_ref[...], NN)
        + proj_bias_ref[...]
        + dot(reduced_proj, proj_up_ref[0], NN)
    )
    normed, inverse = norm_stats(middle)
    low = (normed * gain_ref[...]).astype(BF)
    reduced_fc1 = dot(low, fc1_down_ref[0], NT).astype(BF)
    dy = dy_ref[0]
    grad_reduced_fc2 = dot(dy, fc2_up_ref[0], NT).astype(BF)
    fc1_up_at = 3 * feats
    fc2_down_at = fc1_up_at + hidden
    fc2_up_at = fc2_down_at + hidden
    total = middle + fc2_bias_ref[...]
    reduced_fc2 = None
    grad_low = None
    grad_reduced_fc1 = None
    for j in range(hidden // chunk):
        at = slice(j * chunk, (j + 1) * chunk)
        pre = (
            dot(low, fc1_ref[:, at], NN)
            + fc1_bias_ref[:, at]
            + dot(reduced_fc1, fc1_up_ref[0, :, at], NN)
        )
        size = jnp.abs(pre)
        bell = jnp.exp2((pre * pre) * (-0.5 * LOG2E))
        t = 1.0 / (1.0 + size * (0.3275911 * 0.7071067811865476))
        poly = ((((0.5 * 1.061405429) * t - 0.5 * 1.453152027) * t + 0.5 * 1.421413741) * t - 0.5 * 0.284496736) * t + 0.5 * 0.254829592
        tail = poly * t * bell
        below = jnp.where(pre >= 0.0, 1.0 - tail, tail)
        act = (pre * below).astype(BF)
        slope = below + pre * bell * 0.3989422804014327
        partial = dot(act, fc2_ref[at, :], NN)
        total = total + partial
        partial = dot(act, fc2_down_ref[0, :, at], NT)
        reduced_fc2 = partial if reduced_fc2 is None else reduced_fc2 + partial
        dact = dot(dy, fc2_ref[at, :], NT) + dot(grad_reduced_fc2, fc2_down_ref[0, :, at], NN)
        dpre = (dact * slope).astype(BF)
        partial = dot(dpre, fc1_ref[:, at], NT)
        grad_low = partial if grad_low is None else grad_low + partial
        partial = dot(dpre, fc1_up_ref[0, :, at], NT)
        grad_reduced_fc1 = partial if grad_reduced_fc1 is None else grad_reduced_fc1 + partial
        add_rows(grad_ref, slice(fc1_up_at + j * chunk, fc1_up_at + (j + 1) * chunk), dot(reduced_fc1, dpre, TN), first)
        add_rows(grad_ref, slice(fc2_down_at + j * chunk, fc2_down_at + (j + 1) * chunk), dot(grad_reduced_fc2, act, TN), first)
    reduced_fc2 = reduced_fc2.astype(BF)
    act_ref[0] = (total + dot(reduced_fc2, fc2_up_ref[0], NN)).astype(BF)
    add_rows(grad_ref, slice(fc2_up_at, fc2_up_at + feats), dot(reduced_fc2, dy, TN), first)
    grad_reduced_fc1 = grad_reduced_fc1.astype(BF)
    grad_low = grad_low + dot(grad_reduced_fc1, fc1_down_ref[0], NN)
    add_rows(grad_ref, slice(2 * feats, 3 * feats), dot(grad_reduced_fc1, low, TN), first)
    dx1 = dy.astype(F32) + norm_back(grad_low, gain_ref[...], normed, inverse)
    dx1_ref[0] = dx1
    branch = dx1.astype(BF)
    grad_reduced_proj = dot(branch, proj_up_ref[0], NT).astype(BF)
    add_rows(grad_ref, slice(feats, 2 * feats), dot(reduced_proj, branch, TN), first)
    add_rows(grad_ref, slice(0, feats), dot(grad_reduced_proj, attn, TN), first)
    dattn_ref[0] = (
        dot(branch, proj_ref[...], NT) + dot(grad_reduced_proj, proj_down_ref[0], NN)
    ).astype(BF)


def attend_back_kernel(
    ids_ref,
    x_ref,
    gain_ref,
    weight_ref,
    down_ref,
    up_ref,
    probs_ref,
    attn_ref,
    qkv_ref,
    reduced_ref,
    dattn_ref,
    dx1_ref,
    dx_ref,
    grad_ref,
    values,
    keys_t,
    inner,
    dqkv,
    dquery_t,
    *,
    scale,
    per_group,
    width,
    per_clip,
):
    group = pl.program_id(1)
    groups = pl.num_programs(1)
    feats = x_ref.shape[-1]
    rows = x_ref.shape[1]

    @pl.when(group == 0)
    def _():
        keys_t[...] = qkv_ref[0, :, feats : 2 * feats].astype(F32).T.astype(BF)
        lane = lane_ids((rows, 128))
        ones = jnp.where(lane % width < 2, 1.0, 0.0).astype(BF)
        source = lax.broadcasted_iota(jnp.int32, (128, 128), 0)
        target = lane_ids((128, 128))
        pick = jnp.where(
            (source // width == target // width) & (target % width < 2), 1.0, 0.0
        ).astype(BF)
        pick = jnp.concatenate([pick, pick], axis=0)
        for g in range(feats // 128):
            at = slice(128 * g, 128 * g + 128)
            values[:, 256 * g : 256 * g + 128] = qkv_ref[0, :, 2 * feats + 128 * g : 2 * feats + 128 * g + 128]
            values[:, 256 * g + 128 : 256 * g + 256] = ones
            product = dattn_ref[0, :, at].astype(F32) * attn_ref[0, :, at].astype(F32)
            high = product.astype(BF)
            rest = (product - high.astype(F32)).astype(BF)
            sums = dot(jnp.concatenate([high, rest], axis=1), pick, NN)
            coarse = sums.astype(BF)
            fine = (sums - coarse.astype(F32)).astype(BF)
            inner[:, at] = -jnp.where(lane % width == 0, coarse, fine)

    blocks = pl.ds(pl.multiple_of(group * 128, 128), 128)
    values_now = values[:, pl.ds(pl.multiple_of(group * 256, 256), 256)]
    dattn_now = dattn_ref[0, :, blocks]
    inner_now = inner[:, blocks]
    query_now = qkv_ref[0, :, blocks]
    head_of_lane = lane_ids((rows, 128)) // width
    zero = jnp.zeros((rows, 128), BF)
    dvalue = None
    dkey = None
    for h in range(per_group):
        mine = head_of_lane == h
        dattn_own = jnp.where(mine, dattn_now, zero)
        query_own = jnp.where(mine, query_now, zero)
        right = jnp.concatenate([dattn_own, jnp.where(mine, inner_now, zero)], axis=1)
        probs = probs_ref[0, h]
        dscore = probs * dot(values_now, right, NT).astype(BF)
        partial = dot(probs, dattn_own, NN)
        dvalue = partial if dvalue is None else dvalue + partial
        partial = dot(dscore, query_own, NN)
        dkey = partial if dkey is None else dkey + partial
        at = pl.ds(pl.multiple_of((group * per_group + h) * width, width), width)
        dquery_t[at, :] = dot(keys_t[at, :], dscore, NN)
    dqkv[:, pl.ds(pl.multiple_of(2 * feats + group * 128, 128), 128)] = dvalue.astype(BF)
    dqkv[:, pl.ds(pl.multiple_of(feats + group * 128, 128), 128)] = (dkey * LN2).astype(BF)

    @pl.when(group == groups - 1)
    def _():
        first = pl.program_id(0) % per_clip == 0
        dqkv[:, :feats] = (dquery_t[...].T * scale).astype(BF)
        dall = dqkv[...]
        normed, inverse = norm_stats(x_ref[0].astype(F32))
        low = (normed * gain_ref[...]).astype(BF)
        grad_reduced = dot(dall, up_ref[0], NT).astype(BF)
        add_rows(grad_ref, slice(feats, 4 * feats), dot(reduced_ref[0], dall, TN), first)
        add_rows(grad_ref, slice(0, feats), dot(grad_reduced, low, TN), first)
        dlow = (dot(dall, weight_ref[...], NT) + dot(grad_reduced, down_ref[0], NN)).astype(BF)
        dx_ref[0] = (
            dx1_ref[0] + norm_back(dlow.astype(F32), gain_ref[...], normed, inverse)
        ).astype(BF)


def whole(shape):
    return pl.BlockSpec(shape, lambda *at: (0,) * len(shape), pipeline_mode=pl.Buffered(1))


def compute(
    x,
    dy,
    item_ids,
    vectors,
    weights,
    adapters,
    masks,
    table,
    per_clip,
):
    items, rows, feats = x.shape
    heads = table.shape[0]
    width = feats // heads
    per_group = 128 // width
    groups = heads // per_group
    scale = width**-0.5
    gain1, qkv_bias, proj_bias, gain2, fc1_bias, fc2_bias = vectors
    qkv_w, proj_w, fc1_w, fc2_w = weights
    qkv_down, qkv_up, proj_down, proj_up, fc1_down, fc1_up, fc2_down, fc2_up = adapters
    key_mask, query_mask = masks
    rank = qkv_down.shape[1]
    hidden = fc1_w.shape[1]
    clips = items // per_clip

    def item(shape):
        return pl.BlockSpec((1, *shape), lambda i, *rest: (i,) + (0,) * len(shape))

    def adapter(array):
        return pl.BlockSpec((1, *array.shape[1:]), lambda i, *rest: (rest[-1][i], 0, 0))

    probs, attn, qkv, reduced = pl.pallas_call(
        functools.partial(attend_kernel, scale=scale, per_group=per_group, width=width),
        grid_spec=pltpu.PrefetchScalarGridSpec(
            num_scalar_prefetch=1,
            grid=(items, groups),
            in_specs=[
                item((rows, feats)),
                whole(gain1.shape),
                whole(qkv_w.shape),
                whole(qkv_bias.shape),
                adapter(qkv_down),
                adapter(qkv_up),
                pl.BlockSpec((1, rows, 128), lambda i, g, ids: (i % per_clip, 0, 0)),
                pl.BlockSpec((1, rows, 128), lambda i, g, ids: (i % per_clip, 0, 0)),
                whole(table.shape),
            ],
            out_specs=[
                pl.BlockSpec((1, per_group, rows, rows), lambda i, g, ids: (i, g, 0, 0)),
                item((rows, feats)),
                item((rows, 3 * feats)),
                item((rows, rank)),
            ],
            scratch_shapes=[
                pltpu.VMEM((rows, 2 * feats), BF),
                pltpu.VMEM((rows, feats), BF),
                pltpu.VMEM((feats, rows), BF),
                pltpu.VMEM((feats, rows), F32),
                pltpu.VMEM((2, rows, rows), F32),
            ],
        ),
        out_shape=[
            jax.ShapeDtypeStruct((items, heads, rows, rows), BF),
            jax.ShapeDtypeStruct((items, rows, feats), BF),
            jax.ShapeDtypeStruct((items, rows, 3 * feats), BF),
            jax.ShapeDtypeStruct((items, rows, rank), BF),
        ],
        compiler_params=pltpu.CompilerParams(
            vmem_limit_bytes=VMEM_LIMIT, dimension_semantics=("arbitrary", "arbitrary")
        ),
        name="attend",
    )(item_ids, x, gain1, qkv_w, qkv_bias, qkv_down, qkv_up, key_mask, query_mask, table)

    span = 4 * feats + 2 * hidden
    act, dx1, dattn, grad_dense = pl.pallas_call(
        functools.partial(dense_kernel, per_clip=per_clip, chunk=512),
        grid_spec=pltpu.PrefetchScalarGridSpec(
            num_scalar_prefetch=1,
            grid=(items,),
            in_specs=[
                item((rows, feats)),
                item((rows, feats)),
                item((rows, feats)),
                whole(gain2.shape),
                whole(proj_w.shape),
                whole(proj_bias.shape),
                whole(fc1_w.shape),
                whole(fc1_bias.shape),
                whole(fc2_w.shape),
                whole(fc2_bias.shape),
                adapter(proj_down),
                adapter(proj_up),
                adapter(fc1_down),
                adapter(fc1_up),
                adapter(fc2_down),
                adapter(fc2_up),
            ],
            out_specs=[
                item((rows, feats)),
                item((rows, feats)),
                item((rows, feats)),
                pl.BlockSpec((1, rank, span), lambda i, ids: (i // per_clip, 0, 0)),
            ],
        ),
        out_shape=[
            jax.ShapeDtypeStruct((items, rows, feats), BF),
            jax.ShapeDtypeStruct((items, rows, feats), F32),
            jax.ShapeDtypeStruct((items, rows, feats), BF),
            jax.ShapeDtypeStruct((clips, rank, span), F32),
        ],
        compiler_params=pltpu.CompilerParams(
            vmem_limit_bytes=VMEM_LIMIT, dimension_semantics=("arbitrary",)
        ),
        name="dense",
    )(
        item_ids, x, attn, dy, gain2, proj_w, proj_bias, fc1_w, fc1_bias, fc2_w, fc2_bias,
        proj_down, proj_up, fc1_down, fc1_up, fc2_down, fc2_up,
    )

    dx, grad_qkv = pl.pallas_call(
        functools.partial(
            attend_back_kernel, scale=scale, per_group=per_group, width=width, per_clip=per_clip
        ),
        grid_spec=pltpu.PrefetchScalarGridSpec(
            num_scalar_prefetch=1,
            grid=(items, groups),
            in_specs=[
                item((rows, feats)),
                whole(gain1.shape),
                whole(qkv_w.shape),
                adapter(qkv_down),
                adapter(qkv_up),
                pl.BlockSpec((1, per_group, rows, rows), lambda i, g, ids: (i, g, 0, 0)),
                item((rows, feats)),
                item((rows, 3 * feats)),
                item((rows, rank)),
                item((rows, feats)),
                item((rows, feats)),
            ],
            out_specs=[
                item((rows, feats)),
                pl.BlockSpec((1, rank, 4 * feats), lambda i, g, ids: (i // per_clip, 0, 0)),
            ],
            scratch_shapes=[
                pltpu.VMEM((rows, 2 * feats), BF),
                pltpu.VMEM((feats, rows), BF),
                pltpu.VMEM((rows, feats), BF),
                pltpu.VMEM((rows, 3 * feats), BF),
                pltpu.VMEM((feats, rows), F32),
            ],
        ),
        out_shape=[
            jax.ShapeDtypeStruct((items, rows, feats), BF),
            jax.ShapeDtypeStruct((clips, rank, 4 * feats), F32),
        ],
        compiler_params=pltpu.CompilerParams(
            vmem_limit_bytes=VMEM_LIMIT, dimension_semantics=("arbitrary", "arbitrary")
        ),
        name="attend_back",
    )(item_ids, x, gain1, qkv_w, qkv_down, qkv_up, probs, attn, qkv, reduced, dattn, dx1)
    return act, dx, grad_qkv, grad_dense


def exchange(x, win_size):
    local = x.shape[1]
    bits = local.bit_length() - 1
    at = jnp.arange(TOK)
    taken = (at // 49 < 4, at // 7 % 7 < 3, at % 7 < 3)
    for bit, rows in zip((2, 1, 0), taken):
        if bit < bits:
            split = x.reshape(x.shape[0], local >> (bit + 1), 2, 1 << bit, TOK, -1)
            other = jnp.flip(split, axis=2).reshape(x.shape)
        elif bit == 2:
            half = lax.ppermute(
                x[:, :, : TOK // 2], "win", [(i, i ^ 1 << bit - bits) for i in range(win_size)]
            )
            x = jnp.concatenate((half, x[:, :, TOK // 2 :]), axis=2)
            continue
        else:
            other = lax.ppermute(x, "win", [(i, i ^ 1 << bit - bits) for i in range(win_size)])
        x = jnp.where(rows[None, None, :, None], other, x)
    return x


def place():
    at = jnp.arange(TOK)
    return at // 49, at // 7 % 7, at % 7


def window_masks(win_index, local):
    depth, height, across = place()
    number = win_index * local + jnp.arange(local)
    label = (
        number[:, None] // 4 % 2 * (depth < 4) * 4
        + number[:, None] // 2 % 2 * (height < 3) * 2
        + number[:, None] % 2 * (across < 3)
    )
    lane = jnp.arange(128)
    same = label[:, :, None] == lane
    return (
        same.astype(BF),
        jnp.where(same | (lane >= 8), 0.0, -FAR).astype(BF),
    )


def bias_by_pair(table):
    heads = table.shape[0]
    side = jnp.arange(49)
    high, wide = (side // 7 + 4) % 7, (side % 7 + 4) % 7
    offset = (high[None, :] - high[:, None] + 6) * 13 + wide[None, :] - wide[:, None] + 6
    pick = (jnp.arange(169)[:, None, None] == offset[None]).astype(BF)
    found = jnp.einsum(
        "mad,dkq->mkaq", table.reshape(heads, 15, 169), pick, preferred_element_type=F32
    )
    found = (found * LOG2E).reshape(heads, 49, 15 * 49)
    blocks = []
    for key_block in range(8):
        t = (key_block + 4) % 8
        blocks.append(
            jnp.concatenate(
                (found[..., (11 - t) * 49 : (15 - t) * 49], found[..., (7 - t) * 49 : (11 - t) * 49]),
                axis=-1,
            )
        )
    return jnp.stack(blocks, axis=1).reshape(heads, TOK, TOK)


def per_device(
    tokens, cotangent, adapter_ids, ln1_gain, qkv_weight, qkv_bias, proj_weight, proj_bias, ln2_gain,
    fc1_weight, fc1_bias, fc2_weight, fc2_bias, bias_table, qkv_down, qkv_up, proj_down, proj_up,
    fc1_down, fc1_up, fc2_down, fc2_up, *, clip_size, win_size,
):
    clips, local, rows, feats = tokens.shape
    items = clips * local
    matrices = (qkv_weight, proj_weight, fc1_weight, fc2_weight)
    downs = (qkv_down, proj_down, fc1_down, fc2_down)
    ups = (qkv_up, proj_up, fc1_up, fc2_up)
    vecs = (ln1_gain, qkv_bias, proj_bias, ln2_gain, fc1_bias, fc2_bias)
    pieces = [*matrices, *downs, *ups]
    flat = jnp.concatenate([p.reshape(-1) for p in pieces])
    got = lax.all_gather(flat, ("clip", "win"))
    got = got.reshape(clip_size, win_size, -1)
    full, at = [], 0
    for n, p in enumerate(pieces):
        part = got[:, :, at : at + p.size].reshape(clip_size, win_size, *p.shape)
        at += p.size
        if n < 4:
            full.append(part.transpose(0, 2, 1, 3).reshape(clip_size * p.shape[0], -1))
        elif n < 8:
            full.append(part.transpose(1, 2, 4, 0, 3).reshape(win_size * p.shape[0], p.shape[2], -1))
        else:
            full.append(part.transpose(1, 2, 3, 0, 4).reshape(win_size * p.shape[0], p.shape[1], -1))
    weights = full[:4]
    adapters = [a for pair in zip(full[4:8], full[8:]) for a in pair]
    flat = lax.all_gather(jnp.concatenate(vecs), "clip")
    vectors, at = [], 0
    for p in vecs:
        vectors.append(flat[:, at : at + p.size].reshape(1, -1).astype(F32))
        at += p.size
    x = exchange(tokens, win_size).reshape(items, rows, feats)
    dy = exchange(cotangent, win_size).reshape(items, rows, feats)
    act, dx, grad_qkv, grad_dense = compute(
        x,
        dy,
        jnp.repeat(adapter_ids, local),
        vectors,
        weights,
        adapters,
        window_masks(lax.axis_index("win"), local),
        bias_by_pair(bias_table),
        local,
    )
    activations = exchange(act.reshape(tokens.shape), win_size)
    input_grad = exchange(dx.reshape(tokens.shape), win_size)
    adapter_count = win_size * qkv_down.shape[0]
    hot = (adapter_ids[:, None] == jnp.arange(adapter_count)[None]).astype(F32)
    hidden = fc1_weight.shape[1] * win_size
    spans = (feats, 3 * feats, feats, feats, feats, hidden, hidden, feats)
    grads = jnp.concatenate((grad_qkv, grad_dense), axis=-1)
    rank = grads.shape[1]
    parts, at = [], 0
    for span in spans:
        part = grads[..., at : at + span].reshape(clips, rank, clip_size, span // clip_size)
        at += span
        parts.append(part)
    mine = jnp.concatenate(parts, axis=-1)
    spread = jnp.sum(hot[:, :, None, None, None] * mine[:, None], axis=0)
    spread = spread.transpose(2, 0, 1, 3).astype(BF)
    total = lax.psum_scatter(spread, "clip", scatter_dimension=0, tiled=True)[0]
    total = lax.psum_scatter(total, "win", scatter_dimension=0, tiled=True).astype(F32)
    outs, at = [], 0
    for n, span in enumerate(spans):
        width = span // clip_size
        part = total[..., at : at + width]
        at += width
        outs.append(part.transpose(0, 2, 1) if n % 2 == 0 else part)
    return (activations, input_grad, *outs)


def solution(mesh):
    split = P("clip", "win", None, None)
    grid2 = P("clip", "win")
    down = P("win", "clip", None)
    up = P("win", None, "clip")
    one = P("clip")
    return jax.shard_map(
        functools.partial(
            per_device, clip_size=mesh.shape["clip"], win_size=mesh.shape["win"]
        ),
        mesh=mesh,
        in_specs=(
            split, split, one, one, grid2, one, grid2, one, one, grid2, one, grid2, one, P(),
            down, up, down, up, down, up, down, up,
        ),
        out_specs=(split, split, down, up, down, up, down, up, down, up),
        check_vma=False,
    )
```

time: 1980 us -> 483 us (0.24)
  blocking collectives: 461 us -> 38.1 us
  matrix products: 400 us -> 1.07 us
  local copies, waits for them, and re-layouts: 573 us -> 184 us
  waiting for transfers between devices: 390 us -> 45 us
  Pallas kernels: 0 us -> 145 us
  other arithmetic: 123 us -> 40 us
    all_gather x22 -> x0, blocking collectives: 438 us -> none  [the longest x1 72.6 us: gather_forward(): lax.all_gather(qkv_up, 'clip', axis=2, tiled=True)]
    dot_general x68 -> x1, matrix products: 400 us -> 1.07 us  [bias_by_pair(): jnp.einsum('mad,dkq->mkaq', table.reshape(heads, 15, 169), pick, preferre...]
    gather x2 -> x0, local copies, waits for them, and re-layouts: 336 us -> none  [window_tables(): pos_bias = jnp.take(table.astype(jnp.float32), relative, axis=1)]
    unnamed x25 -> x3, waiting for transfers between devices: 205 us -> 0.05 us
    reduce_scatter x10 -> x2, waiting for transfers between devices: 157 us -> 8.72 us  [the longest x1 8.71 us: per_device(): lax.psum_scatter(total, 'win', scatter_dimension=0, tiled=True).astype(F32)]
    pallas_call x0 -> x3, Pallas kernels: none -> 145 us  [the longest x1 54.8 us: compute(): pl.pallas_call(functools.partial(dense_kernel, per_clip=per_clip, chunk=5...]
    reshape x11 -> x39, local copies, waits for them, and re-layouts: 64.7 us -> 108 us  [the longest x4 53.4 us: exchange(): other = jnp.flip(split, axis=2).reshape(x.shape)]
    reduce_sum x14 -> x1, other arithmetic: 42.8 us -> 0.82 us  [per_device(): spread = jnp.sum(hot[:, :, None, None, None] * mine[:, None], axis=0)]
  transfers between devices with their start and end apart: 27 -> 11, of which waited for: 14 -> 4; matrix products, arithmetic and copies ran while one was open for 51% -> 32% of each run, Pallas kernels for 0% -> 0%
where the time goes in v1:
time: 483 us; the launch traced here: 475 us
  local copies, waits for them, and re-layouts  184 us (38%)
  Pallas kernels  145 us (30%)
  waiting for transfers between devices  45 us (9%)
  other arithmetic  40 us (8%)
  blocking collectives  38.1 us (8%)
  between operations  15.3 us (3%)
  starting transfers between devices  5.77 us (1%)
    pallas_call x1, Pallas kernels, compute(): pl.pallas_call(functools.partial(dense_kernel, per_clip=per_clip, chunk=5...  54.8 us
    reshape x4, local copies, waits for them, and re-layouts, exchange(): other = jnp.flip(split, axis=2).reshape(x.shape)  53.4 us
    pallas_call x1, Pallas kernels, compute(): pl.pallas_call(functools.partial(attend_back_kernel, scale=scale, per_gro...  49.1 us
    pallas_call x1, Pallas kernels, compute(): pl.pallas_call(functools.partial(attend_kernel, scale=scale, per_group=pe...  41.4 us
    unnamed x1, blocking collectives  38.1 us
    ppermute x4, waiting for transfers between devices, exchange(): lax.ppermute(x[:, :, :TOK // 2], 'win', [(i, i ^ 1 << bit - bits) for i i...  32.8 us
    unnamed x89, local copies, waits for them, and re-layouts  29.4 us
    select_n x4, other arithmetic, exchange(): x = jnp.where(rows[None, None, :, None], other, x)  22.2 us
  transfers between devices with their start and end apart: 11, of which 4 were waited for; matrix products, arithmetic and copies ran while one was open for 32% of the time, Pallas kernels for 0%

profile of v1, /device:TPU:0, one launch (start us, length us, event | category | flops | bytes accessed | tf_op | source)
XLA Modules:
  0.0 474.6 jit_solution(16790009015056277335)
XLA Ops:
  20.0 2.9 collective-permute-start
  27.2 38.1 %all-reduce = bf16[5632]{0:T(1024)(128)(2,1)S(1)} all-reduce(bf16[5632]{0:T(1024)(128)(2,1)S(1)} %dynamic-update-slice), channel_id=2, replica_groups=mesh['clip'=8,'win'=4] {'clip'}, use_global_device_ids=true, to_apply=%add | all-reduce | flops 5632 | bytes 22528
  67.0 5.4 %copy.216 = f32[16,49,15,49]{3,2,0,1:T(8,128)} copy(f32[16,49,15,49]{3,0,2,1:T(8,128)S(1)} %multiply_bitcast_fusion) | data formatting | bytes 4609920 | tf_op jit(solution)/shard_map/mul | solution.py:546
  72.4 5.6 %reshape.743 = f32[16,49,735]{2,0,1:T(8,128)S(1)} reshape(f32[16,49,15,49]{3,2,0,1:T(8,128)} %copy.216) | data formatting | bytes 4609920 | tf_op jit(solution)/shard_map/reshape | solution.py:546
  78.0 4.3 fusion.42
  82.3 2.8 fusion.5
  96.4 1.7 constant_dynamic-update-slice_fusion
  98.9 2.2 constant_dynamic-update-slice_fusion.2
  106.7 17.2 %copy.217.table_ref = f32[16,392,392]{2,1,0:T(8,128)} copy(f32[16,392,392]{2,0,1:T(8,128)} %bitcast.20) | data formatting | bytes 19668992 | tf_op jit(solution)/shard_map/reshape | solution.py:556
  125.9 6.1 %broadcast_select_fusion.2 = (bf16[2,2,392,512]{3,1,2,0:T(2,128)(2,1)S(1)}, bf16[2,2,392,512]{3,1,2,0:T(2,128)(2,1)S(1)}) fusion(bf16[2,2,392,512]{3,1,2,0:T(2,128)(2,1)} %collective-permute-done.3, bf16[2,2,392,512]{3,1,2,0:T(2,128)(2,1)} %copy-done.3, pred[392]{0:T(512)(128)(4,1)S(1)} %fusion.21, bf16[2,2,392,512]{3,1,2,0:T(2,128)(2,1)} %collective-permute-done.1, ...), kind=kLoop, calls=%fused_computation.4 | loop fusion | flops 1605632 | bytes 9634184 | tf_op jit(solution)/shard_map/jit(_where)/select_n | solution.py:512
  132.0 13.3 %reshape.745 = bf16[2,2,392,512]{3,1,2,0:T(2,128)(2,1)} reverse(bf16[2,2,392,512]{3,1,2,0:T(2,128)(2,1)S(1)} %get-tuple-element.121), dimensions={1} | reverse | bytes 3211264 | tf_op jit(solution)/shard_map/reshape | solution.py:503
  145.3 13.3 %reshape.721 = bf16[2,2,392,512]{3,1,2,0:T(2,128)(2,1)} reverse(bf16[2,2,392,512]{3,1,2,0:T(2,128)(2,1)S(1)} %get-tuple-element.122), dimensions={1} | reverse | bytes 3211264 | tf_op jit(solution)/shard_map/reshape | solution.py:503
  158.6 5.9 %broadcast_select_fusion.6 = (bf16[2,2,392,512]{3,1,2,0:T(2,128)(2,1)S(1)}, bf16[2,2,392,512]{3,1,2,0:T(2,128)(2,1)S(1)}) fusion(bf16[2,2,392,512]{3,1,2,0:T(2,128)(2,1)} %reshape.745, bf16[2,2,392,512]{3,1,2,0:T(2,128)(2,1)S(1)} %get-tuple-element.121, pred[392]{0:T(512)(128)(4,1)S(1)} %fusion.19, bf16[2,2,392,512]{3,1,2,0:T(2,128)(2,1)} %reshape.721, ...), kind=kLoop, calls=%fused_computation.8 | loop fusion | flops 1605632 | bytes 9634184 | tf_op jit(solution)/shard_map/jit(_where)/select_n | solution.py:512
  167.4 10.2 %reshape.735 = bf16[8,4,131072]{2,1,0:T(4,128)(2,1)} reshape(bf16[4194304]{0:T(1024)(128)(2,1)} %all-gather.4.cloned.1.call-done) | data formatting | bytes 16777216 | tf_op jit(solution)/shard_map/reshape | solution.py:573
  179.1 3.1 fusion.40
  182.2 4.5 fusion.41
  200.3 1.7 copy.273
  202.6 2.0 copy.258
  207.5 4.5 reshape.761
  212.0 3.6 copy.233
  216.6 41.4 %attend.1 = (bf16[4,16,392,392]{3,2,1,0:T(8,128)(2,1)}, bf16[4,392,512]{2,1,0:T(8,128)(2,1)}, bf16[4,392,1536]{2,1,0:T(8,128)(2,1)}, bf16[4,392,16]{2,1,0:T(8,128)(2,1)}) custom-call(s32[4]{0:T(128)} %reshape.720.ids_ref, bf16[4,392,512]{2,1,0:T(8,128)(2,1)} %bitcast.152, f32[1,512]{1,0:T(1,128)} %reshape.777.gain_ref, bf16[512,1536]{1,0:T(8,128)(2,1)} %bitcast.156, ...), custom_call_target="tpu_custom_call" | custom-call | tf_op jit(solution)/shard_map/attend/pallas_call | solution.py:363
  258.0 54.8 %dense.1 = (bf16[4,392,512]{2,1,0:T(8,128)(2,1)}, f32[4,392,512]{2,1,0:T(8,128)}, bf16[4,392,512]{2,1,0:T(8,128)(2,1)}, f32[2,16,6144]{2,1,0:T(8,128)}) custom-call(s32[4]{0:T(128)} %reshape.720.ids_ref, bf16[4,392,512]{2,1,0:T(8,128)(2,1)} %bitcast.153, bf16[4,392,512]{2,1,0:T(8,128)(2,1)} %get-tuple-element.20.attn_ref, bf16[4,392,512]{2,1,0:T(8,128)(2,1)} %bitcast.163, ...), custom_call_target="tpu_custom_call" | custom-call | tf_op jit(solution)/shard_map/dense/pallas_call | solution.py:406
  312.9 49.1 %attend_back.1 = (bf16[4,392,512]{2,1,0:T(8,128)(2,1)}, f32[2,16,2048]{2,1,0:T(8,128)}) custom-call(s32[4]{0:T(128)} %reshape.720.ids_ref, bf16[4,392,512]{2,1,0:T(8,128)(2,1)} %bitcast.154, f32[1,512]{1,0:T(1,128)} %reshape.777.gain_ref, bf16[512,1536]{1,0:T(8,128)(2,1)} %bitcast.157, bf16[8,16,512]{2,1,0:T(8,128)(2,1)} %reshape.739.down_ref, ...), custom_call_target="tpu_custom_call" | custom-call | tf_op jit(solution)/shard_map/attend_back/pallas_call | solution.py:451
  366.1 2.5 copy.240
  374.1 17.6 %collective-permute-done.4 = bf16[2,2,196,512]{3,1,2,0:T(2,128)(2,1)S(1)} collective-permute-done((bf16[2,2,196,512]{3,1,2,0:T(2,128)(2,1)S(1)}, bf16[2,2,196,512]{3,1,2,0:T(2,128)(2,1)S(1)}, u32[]{:S(2)}, u32[]{:S(2)}) %collective-permute-start.4) | collective-permute-done | bytes 802848 | tf_op jit(solution)/shard_map/ppermute | solution.py:505
  393.0 15.2 %collective-permute-done.6 = bf16[2,2,196,512]{3,1,2,0:T(2,128)(2,1)S(1)} collective-permute-done((bf16[2,2,196,512]{3,1,2,0:T(2,128)(2,1)S(1)}, bf16[2,2,196,512]{3,1,2,0:T(2,128)(2,1)S(1)}, u32[]{:S(2)}, u32[]{:S(2)}) %collective-permute-start.6) | collective-permute-done | bytes 802848 | tf_op jit(solution)/shard_map/ppermute | solution.py:505
  409.5 3.4 collective-permute-done.7
  412.9 4.4 broadcast_select_fusion
  417.3 13.3 %reshape.768 = bf16[2,2,392,512]{3,1,2,0:T(2,128)(2,1)} reverse(bf16[2,2,392,512]{3,1,2,0:T(2,128)(2,1)S(1)} %get-tuple-element.117), dimensions={1} | reverse | bytes 3211264 | tf_op jit(solution)/shard_map/reshape | solution.py:503
  430.7 13.3 %reshape.766 = bf16[2,2,392,512]{3,1,2,0:T(2,128)(2,1)} reverse(bf16[2,2,392,512]{3,1,2,0:T(2,128)(2,1)S(1)} %get-tuple-element.118), dimensions={1} | reverse | bytes 3211264 | tf_op jit(solution)/shard_map/reshape | solution.py:503
  444.0 5.9 %broadcast_select_fusion.4 = (bf16[2,2,392,512]{3,1,2,0:T(2,128)(2,1)S(1)}, bf16[2,2,392,512]{3,1,2,0:T(2,128)(2,1)S(1)}) fusion(bf16[2,2,392,512]{3,1,2,0:T(2,128)(2,1)} %reshape.768, bf16[2,2,392,512]{3,1,2,0:T(2,128)(2,1)S(1)} %get-tuple-element.117, pred[392]{0:T(512)(128)(4,1)S(1)} %fusion.19, bf16[2,2,392,512]{3,1,2,0:T(2,128)(2,1)} %reshape.766, ...), kind=kLoop, calls=%fused_computation.6 | loop fusion | flops 1605632 | bytes 9634184 | tf_op jit(solution)/shard_map/jit(_where)/select_n | solution.py:512
  452.8 8.7 %reduce-scatter.5.cloned.1.call-done = bf16[2,16,1024]{2,1,0:T(8,128)(2,1)} async-done(((bf16[8,16,1024]{2,1,0:T(8,128)(2,1)}), bf16[2,16,1024]{2,1,0:T(8,128)(2,1)}) %reduce-scatter.5.cloned.1.call-update) | async-done | bytes 65552 | tf_op jit(solution)/shard_map/reduce_scatter | solution.py:621
  (210 shorter events, 81.0 us)
Async XLA Ops:
  7.2 11.1 %copy-start.11 = (bf16[2,2,392,512]{3,2,1,0:T(8,128)(2,1)S(1)}, bf16[2,2,392,512]{3,2,1,0:T(8,128)(2,1)}, u32[]{:S(2)}) copy-start(bf16[2,2,392,512]{3,2,1,0:T(8,128)(2,1)} %param.22) | copy-start | bytes 4816900
  7.2 160.2 %all-gather.4.cloned.1.call-start = ((), (), s32[]{:S(2)}) async-start(), calls=%async_computation.4 | async-start | bytes 8650752 | tf_op jit(solution)/shard_map/all_gather | solution.py:572
  18.2 425.8 %reduce-scatter.3.cloned.1.call-start = ((), (), s32[]{:S(2)}) async-start(), calls=%async_computation.2 | async-start | bytes 2359296 | tf_op jit(solution)/shard_map/reduce_scatter | solution.py:620
  18.5 4.5 copy-start.12
  20.0 76.4 %collective-permute-start = (bf16[2,2,196,512]{3,1,2,0:T(2,128)(2,1)}, bf16[2,2,196,512]{3,1,2,0:T(2,128)(2,1)}, u32[]{:S(2)}, u32[]{:S(2)}) collective-permute-start(bf16[2,2,196,512]{3,1,2,0:T(2,128)(2,1)} %copy.246), channel_id=1, source_target_pairs={{0,2},{1,3},{2,0},{3,1},{4,6},{5,7},{6,4},{7,5},{8,10},{9,11},{10,... | collective-permute-start | bytes 2408456 | tf_op jit(solution)/shard_map/ppermute | solution.py:505
  24.1 2.8 copy-start.18
  24.1 2.8 copy-start.19
  24.1 2.8 copy-start.20
  24.1 2.8 copy-start.21
  24.1 2.8 copy-start.22
  24.1 2.8 copy-start.23
  24.1 41.3 %copy-start.17 = (bf16[16,2535]{1,0:T(8,128)(2,1)S(1)}, bf16[16,2535]{1,0:T(8,128)(2,1)}, u32[]{:S(2)}) copy-start(bf16[16,2535]{1,0:T(8,128)(2,1)} %param.35) | copy-start | bytes 243364
  25.6 73.3 %collective-permute-start.2 = (bf16[2,2,196,512]{3,1,2,0:T(2,128)(2,1)}, bf16[2,2,196,512]{3,1,2,0:T(2,128)(2,1)}, u32[]{:S(2)}, u32[]{:S(2)}) collective-permute-start(bf16[2,2,196,512]{3,1,2,0:T(2,128)(2,1)} %copy.248), channel_id=1, source_target_pairs={{0,2},{1,3},{2,0},{3,1},{4,6},{5,7},{6,4},{7,5},{8,10},{9,11},{10,... | collective-permute-start | bytes 2408456 | tf_op jit(solution)/shard_map/ppermute | solution.py:505
  82.3 2.8 copy-start.8
  98.1 3.0 copy-start.4
  98.8 3.0 copy-start.2
  98.8 3.2 copy-start.24
  98.8 27.1 %collective-permute-start.1 = (bf16[2,2,392,512]{3,1,2,0:T(2,128)(2,1)S(1)}, bf16[2,2,392,512]{3,1,2,0:T(2,128)(2,1)}, u32[]{:S(2)}, u32[]{:S(2)}) collective-permute-start(bf16[2,2,392,512]{3,1,2,0:T(2,128)(2,1)S(1)} %copy_dynamic-update-slice_fusion.3), channel_id=1, source_target_pairs={{0,1},{1,0},{2,3},{3,2},{4,5},{5,4},{6,7},{7,6},{8,9},{9,8},{10,11... | collective-permute-start | bytes 4816904 | tf_op jit(solution)/shard_map/ppermute | solution.py:511
  101.8 22.1 %copy-start.3 = (bf16[2,2,392,512]{3,1,2,0:T(2,128)(2,1)}, bf16[2,2,392,512]{3,1,2,0:T(2,128)(2,1)S(1)}, u32[]{:S(2)}) copy-start(bf16[2,2,392,512]{3,1,2,0:T(2,128)(2,1)S(1)} %copy_dynamic-update-slice_fusion.2) | copy-start | bytes 4816900
  101.8 24.1 %collective-permute-start.3 = (bf16[2,2,392,512]{3,1,2,0:T(2,128)(2,1)S(1)}, bf16[2,2,392,512]{3,1,2,0:T(2,128)(2,1)}, u32[]{:S(2)}, u32[]{:S(2)}) collective-permute-start(bf16[2,2,392,512]{3,1,2,0:T(2,128)(2,1)S(1)} %copy_dynamic-update-slice_fusion.2), channel_id=1, source_target_pairs={{0,1},{1,0},{2,3},{3,2},{4,5},{5,4},{6,7},{7,6},{8,9},{9,8},{10,11... | collective-permute-start | bytes 4816904 | tf_op jit(solution)/shard_map/ppermute | solution.py:511
  182.2 4.5 slice-start
  195.2 3.0 slice-start.1
  198.2 2.2 copy-start.1
  200.3 2.2 copy-start
  202.6 2.3 copy-start.9
  312.9 50.9 %copy-start.15 = (f32[2,16,6144]{2,1,0:T(8,128)S(1)}, f32[2,16,6144]{2,1,0:T(8,128)}, u32[]{:S(2)}) copy-start(f32[2,16,6144]{2,1,0:T(8,128)} %get-tuple-element.29) | copy-start | bytes 2359300
  368.6 92.9 %reduce-scatter.5.cloned.1.call-start = ((), (), s32[]{:S(2)}) async-start(), calls=%async_computation.3 | async-start | bytes 327680 | tf_op jit(solution)/shard_map/reduce_scatter | solution.py:621
  370.2 2.2 copy-start.14
  370.9 20.8 %collective-permute-start.4 = (bf16[2,2,196,512]{3,1,2,0:T(2,128)(2,1)S(1)}, bf16[2,2,196,512]{3,1,2,0:T(2,128)(2,1)S(1)}, u32[]{:S(2)}, u32[]{:S(2)}) collective-permute-start(bf16[2,2,196,512]{3,1,2,0:T(2,128)(2,1)S(1)} %copy.250), channel_id=1, source_target_pairs={{0,2},{1,3},{2,0},{3,1},{4,6},{5,7},{6,4},{7,5},{8,10},{9,11},{10,... | collective-permute-start | bytes 2408456 | tf_op jit(solution)/shard_map/ppermute | solution.py:505
  373.3 34.9 %collective-permute-start.6 = (bf16[2,2,196,512]{3,1,2,0:T(2,128)(2,1)S(1)}, bf16[2,2,196,512]{3,1,2,0:T(2,128)(2,1)S(1)}, u32[]{:S(2)}, u32[]{:S(2)}) collective-permute-start(bf16[2,2,196,512]{3,1,2,0:T(2,128)(2,1)S(1)} %copy.252), channel_id=1, source_target_pairs={{0,2},{1,3},{2,0},{3,1},{4,6},{5,7},{6,4},{7,5},{8,10},{9,11},{10,... | collective-permute-start | bytes 2408456 | tf_op jit(solution)/shard_map/ppermute | solution.py:505
  392.9 16.6 %collective-permute-start.5 = (bf16[2,2,392,512]{3,1,2,0:T(2,128)(2,1)S(1)}, bf16[2,2,392,512]{3,1,2,0:T(2,128)(2,1)S(1)}, u32[]{:S(2)}, u32[]{:S(2)}) collective-permute-start(bf16[2,2,392,512]{3,1,2,0:T(2,128)(2,1)S(1)} %copy_dynamic-update-slice_fusion.1), channel_id=1, source_target_pairs={{0,1},{1,0},{2,3},{3,2},{4,5},{5,4},{6,7},{7,6},{8,9},{9,8},{10,11... | collective-permute-start | bytes 4816904 | tf_op jit(solution)/shard_map/ppermute | solution.py:511
  409.4 3.5 collective-permute-start.7
  (7 other events, 10.4 us)
Sparse Core Ops, SparseCore 0:
  18.3 89.2 all-gather.3
  368.7 64.9 reduce-scatter.2
  444.2 17.2 reduce-scatter.4

commit v2 on v1

--- a/solution.py
+++ b/solution.py
@@ -16,6 +16,7 @@
 FAR = 1e9
 VMEM_LIMIT = 60 * 2**20
 TOK = 392
+TOP = 208
 
 
 def dot(left, right, dims):
@@ -137,48 +138,98 @@
         out_ref[0] = out_t[...].T.astype(BF)
 
 
+def row_masks(rows, columns):
+    row = lax.broadcasted_iota(jnp.int32, (rows, columns), 0)
+    return row < TOK // 2, row % 49 < 21, row % 7 < 3
+
+
+def with_top(part, top, early):
+    return jnp.concatenate([jnp.where(early[:TOP], top, part[:TOP]), part[TOP:]], axis=0)
+
+
+def join_pieces(refs, e):
+    own, beside, across, far = refs
+    early, low_h, low_w = row_masks(own.shape[1], own.shape[2])
+
+    def window(n):
+        part = jnp.where(low_h, beside[n], own[n])
+        return with_top(part, jnp.where(low_h[:TOP], far[n], across[n]), early)
+
+    return jnp.where(low_w, window(1 - e), window(e))
+
+
 def dense_kernel(
     ids_ref,
     x_ref,
     attn_ref,
-    dy_ref,
     gain_ref,
-    proj_ref,
     proj_bias_ref,
-    fc1_ref,
     fc1_bias_ref,
-    fc2_ref,
     fc2_bias_ref,
-    proj_down_ref,
-    proj_up_ref,
-    fc1_down_ref,
-    fc1_up_ref,
-    fc2_down_ref,
-    fc2_up_ref,
-    act_ref,
-    dx1_ref,
-    dattn_ref,
-    grad_ref,
-    *,
+    staged_ref,
+    *refs,
     per_clip,
     chunk,
+    pieces,
 ):
+    tiles, refs = refs[:6], refs[6:]
+    dy_refs, refs = refs[:pieces], refs[pieces:]
+    act_ref, dx1_ref, dattn_ref, grad_ref, *refs = refs
+    proj_ref, fc1_ref, fc2_ref, proj_down, proj_up, fc1_down, fc1_up, fc2_down, fc2_up, sem = refs
+
+    @pl.when(pl.program_id(0) == 0)
+    def _():
+        copies = []
+        for n in range(4):
+            moves = [(0, 64, proj_ref, 128 * n), (320, 256, fc2_ref, 128 * n)]
+            moves += [(64 + 64 * t, 64, fc1_ref, 512 * n + 128 * t) for t in range(4)]
+            for start, size, target, lane in moves:
+                copies.append(
+                    pltpu.make_async_copy(
+                        staged_ref.at[:, n, pl.ds(start, size), :],
+                        target.at[:, :, pl.ds(lane, 128)],
+                        sem.at[len(copies)],
+                    )
+                )
+        for copy in copies:
+            copy.start()
+        for copy in copies:
+            copy.wait()
+
+    @pl.when(pl.program_id(0) % per_clip == 0)
+    def _():
+        for n in range(8):
+            short = slice(64 * n, 64 * n + 64)
+            proj_down[:, short] = tiles[0][n, 0, :, 0:64]
+            proj_up[:, short] = tiles[0][n, 0, :, 64:128]
+            fc1_down[:, short] = tiles[1][n, 0, :, 0:64]
+            fc2_up[:, short] = tiles[1][n, 0, :, 64:128]
+            for half in range(2):
+                long = slice(256 * n + 128 * half, 256 * n + 128 * half + 128)
+                fc1_up[:, long] = tiles[2 + half][n, 0]
+                fc2_down[:, long] = tiles[4 + half][n, 0]
+
+    if pieces == 1:
+        dy = dy_refs[0][0]
+    else:
+        dy = join_pieces(dy_refs, pl.program_id(0) % 2)
+    proj_w = proj_ref[...].reshape(proj_ref.shape[0] * proj_ref.shape[1], -1)
+    per_chunk = chunk // fc2_ref.shape[1]
     first = pl.program_id(0) % per_clip == 0
     feats = x_ref.shape[-1]
     hidden = fc1_ref.shape[-1]
     attn = attn_ref[0]
-    reduced_proj = dot(attn, proj_down_ref[0], NT).astype(BF)
+    reduced_proj = dot(attn, proj_down[...], NT).astype(BF)
     middle = (
         x_ref[0].astype(F32)
-        + dot(attn, proj_ref[...], NN)
+        + dot(attn, proj_w, NN)
         + proj_bias_ref[...]
-        + dot(reduced_proj, proj_up_ref[0], NN)
+        + dot(reduced_proj, proj_up[...], NN)
     )
     normed, inverse = norm_stats(middle)
     low = (normed * gain_ref[...]).astype(BF)
-    reduced_fc1 = dot(low, fc1_down_ref[0], NT).astype(BF)
-    dy = dy_ref[0]
-    grad_reduced_fc2 = dot(dy, fc2_up_ref[0], NT).astype(BF)
+    reduced_fc1 = dot(low, fc1_down[...], NT).astype(BF)
+    grad_reduced_fc2 = dot(dy, fc2_up[...], NT).astype(BF)
     fc1_up_at = 3 * feats
     fc2_down_at = fc1_up_at + hidden
     fc2_up_at = fc2_down_at + hidden
@@ -188,10 +239,12 @@
     grad_reduced_fc1 = None
     for j in range(hidden // chunk):
         at = slice(j * chunk, (j + 1) * chunk)
+        fc1_w = fc1_ref[:, :, at].reshape(feats, chunk)
+        fc2_w = fc2_ref[j * per_chunk : (j + 1) * per_chunk].reshape(chunk, feats)
         pre = (
-            dot(low, fc1_ref[:, at], NN)
+            dot(low, fc1_w, NN)
             + fc1_bias_ref[:, at]
-            + dot(reduced_fc1, fc1_up_ref[0, :, at], NN)
+            + dot(reduced_fc1, fc1_up[:, at], NN)
         )
         size = jnp.abs(pre)
         bell = jnp.exp2((pre * pre) * (-0.5 * LOG2E))
@@ -201,32 +254,32 @@
         below = jnp.where(pre >= 0.0, 1.0 - tail, tail)
         act = (pre * below).astype(BF)
         slope = below + pre * bell * 0.3989422804014327
-        partial = dot(act, fc2_ref[at, :], NN)
+        partial = dot(act, fc2_w, NN)
         total = total + partial
-        partial = dot(act, fc2_down_ref[0, :, at], NT)
+        partial = dot(act, fc2_down[:, at], NT)
         reduced_fc2 = partial if reduced_fc2 is None else reduced_fc2 + partial
-        dact = dot(dy, fc2_ref[at, :], NT) + dot(grad_reduced_fc2, fc2_down_ref[0, :, at], NN)
+        dact = dot(dy, fc2_w, NT) + dot(grad_reduced_fc2, fc2_down[:, at], NN)
         dpre = (dact * slope).astype(BF)
-        partial = dot(dpre, fc1_ref[:, at], NT)
+        partial = dot(dpre, fc1_w, NT)
         grad_low = partial if grad_low is None else grad_low + partial
-        partial = dot(dpre, fc1_up_ref[0, :, at], NT)
+        partial = dot(dpre, fc1_up[:, at], NT)
         grad_reduced_fc1 = partial if grad_reduced_fc1 is None else grad_reduced_fc1 + partial
         add_rows(grad_ref, slice(fc1_up_at + j * chunk, fc1_up_at + (j + 1) * chunk), dot(reduced_fc1, dpre, TN), first)
         add_rows(grad_ref, slice(fc2_down_at + j * chunk, fc2_down_at + (j + 1) * chunk), dot(grad_reduced_fc2, act, TN), first)
     reduced_fc2 = reduced_fc2.astype(BF)
-    act_ref[0] = (total + dot(reduced_fc2, fc2_up_ref[0], NN)).astype(BF)
+    act_ref[0] = (total + dot(reduced_fc2, fc2_up[...], NN)).astype(BF)
     add_rows(grad_ref, slice(fc2_up_at, fc2_up_at + feats), dot(reduced_fc2, dy, TN), first)
     grad_reduced_fc1 = grad_reduced_fc1.astype(BF)
-    grad_low = grad_low + dot(grad_reduced_fc1, fc1_down_ref[0], NN)
+    grad_low = grad_low + dot(grad_reduced_fc1, fc1_down[...], NN)
     add_rows(grad_ref, slice(2 * feats, 3 * feats), dot(grad_reduced_fc1, low, TN), first)
     dx1 = dy.astype(F32) + norm_back(grad_low, gain_ref[...], normed, inverse)
     dx1_ref[0] = dx1
     branch = dx1.astype(BF)
-    grad_reduced_proj = dot(branch, proj_up_ref[0], NT).astype(BF)
+    grad_reduced_proj = dot(branch, proj_up[...], NT).astype(BF)
     add_rows(grad_ref, slice(feats, 2 * feats), dot(reduced_proj, branch, TN), first)
     add_rows(grad_ref, slice(0, feats), dot(grad_reduced_proj, attn, TN), first)
     dattn_ref[0] = (
-        dot(branch, proj_ref[...], NT) + dot(grad_reduced_proj, proj_down_ref[0], NN)
+        dot(branch, proj_w, NT) + dot(grad_reduced_proj, proj_down[...], NN)
     ).astype(BF)
 
 
@@ -329,17 +382,7 @@
     return pl.BlockSpec(shape, lambda *at: (0,) * len(shape), pipeline_mode=pl.Buffered(1))
 
 
-def compute(
-    x,
-    dy,
-    item_ids,
-    vectors,
-    weights,
-    adapters,
-    masks,
-    table,
-    per_clip,
-):
+def compute(x, dy, item_ids, vectors, qkv_parts, staged, masks, table, per_clip):
     items, rows, feats = x.shape
     heads = table.shape[0]
     width = feats // heads
@@ -347,11 +390,10 @@
     groups = heads // per_group
     scale = width**-0.5
     gain1, qkv_bias, proj_bias, gain2, fc1_bias, fc2_bias = vectors
-    qkv_w, proj_w, fc1_w, fc2_w = weights
-    qkv_down, qkv_up, proj_down, proj_up, fc1_down, fc1_up, fc2_down, fc2_up = adapters
+    qkv_w, qkv_down, qkv_up = qkv_parts
     key_mask, query_mask = masks
     rank = qkv_down.shape[1]
-    hidden = fc1_w.shape[1]
+    hidden = fc1_bias.shape[1]
     clips = items // per_clip
 
     def item(shape):
@@ -399,38 +441,49 @@
         compiler_params=pltpu.CompilerParams(
             vmem_limit_bytes=VMEM_LIMIT, dimension_semantics=("arbitrary", "arbitrary")
         ),
+        cost_estimate=pl.CostEstimate(flops=4 * 10**10, bytes_accessed=10**7, transcendentals=0),
         name="attend",
     )(item_ids, x, gain1, qkv_w, qkv_bias, qkv_down, qkv_up, key_mask, query_mask, table)
 
     span = 4 * feats + 2 * hidden
+    def tile(n):
+        return pl.BlockSpec(
+            (8, 1, rank, 128), lambda i, ids: (0, ids[i] // 2, 36 + 2 * n + ids[i] % 2, 0)
+        )
+
+    def piece(array):
+        if len(dy) == 1:
+            return item(array.shape[1:])
+        return pl.BlockSpec((per_clip, *array.shape[1:]), lambda i, ids: (i // per_clip, 0, 0))
+
     act, dx1, dattn, grad_dense = pl.pallas_call(
-        functools.partial(dense_kernel, per_clip=per_clip, chunk=512),
+        functools.partial(dense_kernel, per_clip=per_clip, chunk=512, pieces=len(dy)),
         grid_spec=pltpu.PrefetchScalarGridSpec(
             num_scalar_prefetch=1,
             grid=(items,),
             in_specs=[
                 item((rows, feats)),
                 item((rows, feats)),
-                item((rows, feats)),
                 whole(gain2.shape),
-                whole(proj_w.shape),
                 whole(proj_bias.shape),
-                whole(fc1_w.shape),
                 whole(fc1_bias.shape),
-                whole(fc2_w.shape),
                 whole(fc2_bias.shape),
-                adapter(proj_down),
-                adapter(proj_up),
-                adapter(fc1_down),
-                adapter(fc1_up),
-                adapter(fc2_down),
-                adapter(fc2_up),
+                pl.BlockSpec(memory_space=pl.ANY),
+                *[tile(n) for n in range(6)],
+                *[piece(a) for a in dy],
             ],
             out_specs=[
                 item((rows, feats)),
                 item((rows, feats)),
                 item((rows, feats)),
                 pl.BlockSpec((1, rank, span), lambda i, ids: (i // per_clip, 0, 0)),
+            ],
+            scratch_shapes=[
+                pltpu.VMEM((8, feats // 8, feats), BF),
+                pltpu.VMEM((8, feats // 8, hidden), BF),
+                pltpu.VMEM((8, hidden // 8, feats), BF),
+                *[pltpu.VMEM((rank, n), BF) for n in (feats, feats, feats, hidden, hidden, feats)],
+                pltpu.SemaphoreType.DMA((24,)),
             ],
         ),
         out_shape=[
@@ -442,10 +495,10 @@
         compiler_params=pltpu.CompilerParams(
             vmem_limit_bytes=VMEM_LIMIT, dimension_semantics=("arbitrary",)
         ),
+        cost_estimate=pl.CostEstimate(flops=5 * 10**10, bytes_accessed=10**7, transcendentals=0),
         name="dense",
     )(
-        item_ids, x, attn, dy, gain2, proj_w, proj_bias, fc1_w, fc1_bias, fc2_w, fc2_bias,
-        proj_down, proj_up, fc1_down, fc1_up, fc2_down, fc2_up,
+        item_ids, x, attn, gain2, proj_bias, fc1_bias, fc2_bias, staged, *([staged] * 6), *dy
     )
 
     dx, grad_qkv = pl.pallas_call(
@@ -487,9 +540,368 @@
         compiler_params=pltpu.CompilerParams(
             vmem_limit_bytes=VMEM_LIMIT, dimension_semantics=("arbitrary", "arbitrary")
         ),
+        cost_estimate=pl.CostEstimate(flops=5 * 10**10, bytes_accessed=10**7, transcendentals=0),
         name="attend_back",
     )(item_ids, x, gain1, qkv_w, qkv_down, qkv_up, probs, attn, qkv, reduced, dattn, dx1)
     return act, dx, grad_qkv, grad_dense
+
+
+MESH = pl.DeviceIdType.MESH
+
+
+def enter(peers):
+    barrier = pltpu.get_barrier_semaphore()
+    for peer in peers:
+        pl.semaphore_signal(barrier, inc=1, device_id=peer, device_id_type=MESH)
+    pl.semaphore_wait(barrier, len(peers))
+
+
+class Sender:
+    def __init__(self, send_sem, recv_sem):
+        self.send_sem, self.recv_sem, self.count = send_sem, recv_sem, 0
+
+    def copy(self, src, dst, peer):
+        n = self.count
+        self.count += 1
+        made = pltpu.make_async_remote_copy(
+            src_ref=src,
+            dst_ref=dst,
+            send_sem=self.send_sem.at[n],
+            recv_sem=self.recv_sem.at[n],
+            device_id=peer,
+            device_id_type=MESH,
+        )
+        made.start()
+        return made
+
+
+def pack_vectors(vecs, ids):
+    flat = jnp.concatenate([v.astype(F32) for v in vecs] + [ids.astype(F32)])
+    return jnp.pad(flat, (0, 1024 - flat.shape[0])).reshape(8, 128)
+
+
+def spread_kernel(
+    tok_ref, unit_ref, vec_ref, pairs_ref,
+    x_ref, weight_ref, down_ref, up_ref, gain1_ref, qkv_bias_ref, proj_bias_ref, gain2_ref, fc1_bias_ref,
+    fc2_bias_ref, ids_ref, table_ref,
+    units, vecs, beside, mixed, tops, found, wide, select, bias, send_sem, recv_sem, out_sem,
+    *, clip_size,
+):
+    c, w = lax.axis_index("clip"), lax.axis_index("win")
+    z, y = c // 2, c % 2
+    x, k = w // 2, w % 2
+    sibling = (c, x * 2 + 1 - k)
+    across = (c, (1 - x) * 2 + k)
+    zs = clip_size // 2
+
+    def at(z_step, other_y):
+        return (z + z_step + zs) % zs * 2 + (1 - y if other_y else y)
+
+    items, rows, feats = tok_ref.shape
+    enter([sibling, across] + [((c + d) % clip_size, w) for d in range(1, clip_size)])
+    send = Sender(send_sem, recv_sem)
+    waits = []
+    units[k, c, x] = unit_ref[...]
+    vecs[c] = vec_ref[...]
+    to_across = send.copy(unit_ref, units.at[k, c, x], across)
+    tokens_beside = [send.copy(tok_ref.at[i], beside.at[i], sibling) for i in range(items)]
+    from_sibling = [send.copy(unit_ref, units.at[k, c, x], sibling)]
+    vec_copies = [
+        send.copy(vec_ref, vecs.at[c], ((c + d) % clip_size, w)) for d in range(1, clip_size)
+    ]
+    to_across.wait_recv()
+    along_z = [send.copy(units.at[k, c], units.at[k, c], (at(j, False), w)) for j in range(1, zs)]
+    along_y = [send.copy(units.at[k, c], units.at[k, c], (at(0, True), w))]
+    from_sibling.append(send.copy(units.at[k, c, 1 - x], units.at[k, c, 1 - x], sibling))
+    early, low_h, low_w = row_masks(rows, feats)
+    token_tops = []
+    for i in range(items):
+        tokens_beside[i].wait_recv()
+        mixed[i] = jnp.where(low_h, beside[i], tok_ref[i])
+        token_tops.append(send.copy(mixed.at[i, pl.ds(0, TOP)], tops.at[i], across))
+
+    heads = pairs_ref.shape[0] // 15
+    off_lane = lane_ids((pairs_ref.shape[1], 128))
+    off_row = lax.broadcasted_iota(jnp.int32, (pairs_ref.shape[1], 128), 0)
+    query_at = (off_lane // 7 + 4) % 7 * 13 + (off_lane % 7 + 4) % 7
+    wanted = off_row - query_at - 84
+    valid = off_lane < 49
+
+    def one_key(key, carry):
+        key_at = (key // 7 + 4) % 7 * 13 + (key % 7 + 4) % 7
+        pick = jnp.where(valid & (wanted + key_at == 0), 1.0, 0.0).astype(BF)
+        value = dot(pairs_ref[...], pick, NN)
+        for a in range(15):
+            found[a, pl.ds(key, heads, stride=56), :] = value[a * heads : (a + 1) * heads]
+        return carry
+
+    lax.fori_loop(0, 49, one_key, 0)
+
+    from_z = []
+    for j in range(1, zs):
+        along_z[j - 1].wait_recv()
+        slot = at(-j, False)
+        along_y.append(send.copy(units.at[k, slot], units.at[k, slot], (at(0, True), w)))
+        from_sibling.append(send.copy(units.at[k, slot], units.at[k, slot], sibling))
+
+    for a in range(15):
+        wide[:, 128 * a : 128 * a + 128] = found[a].astype(BF)
+    sel_row = lax.broadcasted_iota(jnp.int32, (128, rows), 0)
+    sel_lane = lane_ids((128, rows))
+    for t in range(8):
+        select[128 * t : 128 * t + 128, :] = jnp.where(
+            (sel_lane == sel_row + (t + 4) % 8 * 49) & (sel_row < 49), 1.0, 0.0
+        ).astype(BF)
+
+    for j in range(zs):
+        along_y[j].wait_recv()
+        slot = at(-j, True)
+        from_sibling.append(send.copy(units.at[k, slot], units.at[k, slot], sibling))
+
+    for block in range(8):
+        t = (block + 4) % 8
+        value = dot(wide[:, (7 - t) * 128 : (15 - t) * 128], select[...], NN) * LOG2E
+        for m in range(heads):
+            bias[m, 49 * block : 49 * block + 49, :] = value[56 * m : 56 * m + 49]
+    out = pltpu.make_async_copy(bias, table_ref, out_sem)
+    out.start()
+
+    for copy in vec_copies:
+        copy.wait_recv()
+    for c2 in range(clip_size):
+        v = vecs[c2]
+        gain1_ref[:, 64 * c2 : 64 * c2 + 64] = v[0:1, 0:64]
+        qkv_bias_ref[:, 192 * c2 : 192 * c2 + 64] = v[0:1, 64:128]
+        qkv_bias_ref[:, 192 * c2 + 64 : 192 * c2 + 192] = v[1:2, :]
+        proj_bias_ref[:, 64 * c2 : 64 * c2 + 64] = v[2:3, 0:64]
+        gain2_ref[:, 64 * c2 : 64 * c2 + 64] = v[2:3, 64:128]
+        fc1_bias_ref[:, 256 * c2 : 256 * c2 + 128] = v[3:4, :]
+        fc1_bias_ref[:, 256 * c2 + 128 : 256 * c2 + 256] = v[4:5, :]
+        fc2_bias_ref[:, 64 * c2 : 64 * c2 + 64] = v[5:6, 0:64]
+        for n in range(2):
+            ids_ref[2 * c2 + n : 2 * c2 + n + 1, :] = jnp.broadcast_to(
+                v[5:6, 64 + n : 65 + n], (1, ids_ref.shape[1])
+            )
+
+    for copy in from_sibling:
+        copy.wait_recv()
+    for c2 in range(clip_size):
+        for x2 in range(2):
+            for k2 in range(2):
+                n = 2 * x2 + k2
+                weight_ref[64 * c2 : 64 * c2 + 64, 384 * n : 384 * n + 384] = units[k2, c2, x2, :, 0:384]
+                for a in range(2):
+                    low = units[k2, c2, x2, 16 * a : 16 * a + 16, 384:512]
+                    high = units[k2, c2, x2, 32 + 16 * a : 48 + 16 * a, 384:512]
+                    down_ref[2 * n + a, :, 64 * c2 : 64 * c2 + 64] = low[:, 0:64]
+                    up_ref[2 * n + a, :, 192 * c2 : 192 * c2 + 64] = low[:, 64:128]
+                    up_ref[2 * n + a, :, 192 * c2 + 64 : 192 * c2 + 192] = high
+
+    for i in range(0, items, 2):
+        both = []
+        for e in range(2):
+            token_tops[i + e].wait_recv()
+            both.append(with_top(mixed[i + e], tops[i + e], early))
+        for e in range(2):
+            x_ref[i + e] = jnp.where(low_w, both[1 - e], both[e])
+
+    for copy in [to_across, *tokens_beside, *from_sibling, *vec_copies, *along_z, *along_y, *token_tops]:
+        copy.wait_send()
+    out.wait()
+
+
+def spread(tokens, unit, vec, pairs, clip_size):
+    items, rows, feats = tokens.shape
+    heads = pairs.shape[0] // 15
+    f = functools.partial(jax.ShapeDtypeStruct)
+    vm = pl.BlockSpec(memory_space=pltpu.VMEM)
+    return pl.pallas_call(
+        functools.partial(spread_kernel, clip_size=clip_size),
+        in_specs=[vm] * 4,
+        out_specs=[vm] * 11 + [pl.BlockSpec(memory_space=pl.ANY)],
+        out_shape=[
+            f((items, rows, feats), BF),
+            f((512, 1536), BF),
+            f((8, 16, 512), BF),
+            f((8, 16, 1536), BF),
+            f((1, 512), F32),
+            f((1, 1536), F32),
+            f((1, 512), F32),
+            f((1, 512), F32),
+            f((1, 2048), F32),
+            f((1, 512), F32),
+            f((16, 512), F32),
+            f((heads, rows, rows), F32),
+        ],
+        scratch_shapes=[
+            pltpu.VMEM((2, clip_size, 2, 64, 512), BF),
+            pltpu.VMEM((clip_size, 8, 128), F32),
+            pltpu.VMEM((items, rows, feats), BF),
+            pltpu.VMEM((items, rows, feats), BF),
+            pltpu.VMEM((items, TOP, feats), BF),
+            pltpu.VMEM((15, 56 * heads, 128), F32),
+            pltpu.VMEM((56 * heads, 15 * 128), BF),
+            pltpu.VMEM((8 * 128, rows), BF),
+            pltpu.VMEM((heads, rows, rows), F32),
+            pltpu.SemaphoreType.DMA((32,)),
+            pltpu.SemaphoreType.DMA((32,)),
+            pltpu.SemaphoreType.DMA,
+        ],
+        compiler_params=pltpu.CompilerParams(
+            collective_id=0, has_side_effects=True, vmem_limit_bytes=VMEM_LIMIT
+        ),
+        cost_estimate=pl.CostEstimate(flops=3 * 10**10, bytes_accessed=2 * 10**7, transcendentals=0),
+        name="spread",
+    )(tokens, unit, vec, pairs)
+
+
+PIECES = (("q", 0, 64), ("q", 512, 192), ("d", 0, 64), ("d", 512, 64), ("d", 1024, 64), ("d", 5632, 64), ("d", 1536, 256), ("d", 3584, 256))
+
+
+def finish_kernel(
+    act_ref, act_beside_ref, act_across_ref, act_far_ref, dx_ref, grad_qkv_ref, grad_dense_ref, ids_ref,
+    act_out_ref, dx_out_ref, qd_ref, qu_ref, pd_ref, pu_ref, f1d_ref, f1u_ref, f2d_ref, f2u_ref,
+    beside, mixed, tops, own, other, from_core, half, from_x, shares, from_clips, adapters, from_win, whole_out,
+    send_sem, recv_sem,
+    *, clip_size,
+):
+    c, w = lax.axis_index("clip"), lax.axis_index("win")
+    x, k = w // 2, w % 2
+    sibling = (c, x * 2 + 1 - k)
+    across = (c, (1 - x) * 2 + k)
+    items, rows, feats = dx_ref.shape
+    enter(
+        [(c, (w + d) % 4) for d in range(1, 4)]
+        + [((c + d) % clip_size, w) for d in range(1, clip_size)]
+    )
+    send = Sender(send_sem, recv_sem)
+    dx_beside = [send.copy(dx_ref.at[i], beside.at[i], sibling) for i in range(items)]
+
+    def rows_of(part, j):
+        halves = []
+        for n in range(2):
+            cells = []
+            for name, start, width in PIECES:
+                ref = grad_qkv_ref if name == "q" else grad_dense_ref
+                cells.append(
+                    ref[n, pl.ds(pl.multiple_of(part * 8, 8), 8), start + j * width : start + (j + 1) * width]
+                )
+            halves.append(jnp.concatenate(cells, axis=1))
+        return jnp.concatenate(halves, axis=0)
+
+    for j in range(clip_size):
+        other[j] = rows_of(1 - k, j).astype(BF)
+    core_copy = send.copy(other, from_core, sibling)
+
+    early, low_h, low_w = row_masks(rows, feats)
+    dx_tops = []
+    for i in range(items):
+        dx_beside[i].wait_recv()
+        mixed[i] = jnp.where(low_h, beside[i], dx_ref[i])
+        dx_tops.append(send.copy(mixed.at[i, pl.ds(0, TOP)], tops.at[i], across))
+
+    for j in range(clip_size):
+        own[j] = rows_of(k, j)
+    core_copy.wait_recv()
+    own[...] += from_core[...].astype(F32)
+    half[...] = own[:, :, pl.ds(pl.multiple_of((1 - x) * 512, 512), 512)].astype(BF)
+    x_copy = send.copy(half, from_x, across)
+
+    for i in range(0, items, 2):
+        both = []
+        for e in range(2):
+            part = jnp.where(low_h, act_beside_ref[i + e], act_ref[i + e])
+            top = jnp.where(low_h[:TOP], act_far_ref[i + e], act_across_ref[i + e])
+            both.append(with_top(part, top, early))
+        for e in range(2):
+            act_out_ref[i + e] = jnp.where(low_w, both[1 - e], both[e])
+
+    x_copy.wait_recv()
+    shares[...] = (
+        own[:, :, pl.ds(pl.multiple_of(x * 512, 512), 512)] + from_x[...].astype(F32)
+    ).astype(BF)
+    from_clips[c] = shares[c]
+    clip_copies = []
+    for d in range(1, clip_size):
+        to = (c + d) % clip_size
+        clip_copies.append(send.copy(shares.at[to], from_clips.at[c], (to, w)))
+    for copy in clip_copies:
+        copy.wait_recv()
+    for a in range(8):
+        total = None
+        for n in range(2 * clip_size):
+            value = from_clips[n // 2].astype(F32)[8 * (n % 2) : 8 * (n % 2) + 8]
+            value = jnp.where(ids_ref[n : n + 1, :] == float(a), value, 0.0)
+            total = value if total is None else total + value
+        adapters[a // 2, 8 * (a % 2) : 8 * (a % 2) + 8, :] = total
+    from_win[w] = adapters[w]
+    win_copies = []
+    for d in range(1, 4):
+        to = (w + d) % 4
+        win_copies.append(send.copy(adapters.at[to], from_win.at[w], (c, to)))
+
+    for i in range(0, items, 2):
+        both = []
+        for e in range(2):
+            dx_tops[i + e].wait_recv()
+            both.append(with_top(mixed[i + e], tops[i + e], early))
+        for e in range(2):
+            dx_out_ref[i + e] = jnp.where(low_w, both[1 - e], both[e])
+
+    for copy in win_copies:
+        copy.wait_recv()
+    for x2 in range(2):
+        for k2 in range(2):
+            for a in range(2):
+                whole_out[a, 8 * k2 : 8 * k2 + 8, 512 * x2 : 512 * x2 + 512] = from_win[
+                    2 * x2 + k2, 8 * a : 8 * a + 8, :
+                ]
+    for a in range(2):
+        qd_ref[a] = whole_out[a, :, 0:64]
+        qu_ref[a] = whole_out[a, :, 64:256]
+        pd_ref[a] = whole_out[a, :, 256:320]
+        pu_ref[a] = whole_out[a, :, 320:384]
+        f1d_ref[a] = whole_out[a, :, 384:448]
+        f2u_ref[a] = whole_out[a, :, 448:512]
+        f1u_ref[a] = whole_out[a, :, 512:768]
+        f2d_ref[a] = whole_out[a, :, 768:1024]
+    for copy in [*dx_beside, core_copy, *dx_tops, x_copy, *clip_copies, *win_copies]:
+        copy.wait_send()
+
+
+def finish(act, act_pieces, dx, grad_qkv, grad_dense, ids, clip_size):
+    items, rows, feats = dx.shape
+    f = jax.ShapeDtypeStruct
+    vm = pl.BlockSpec(memory_space=pltpu.VMEM)
+    widths = (64, 192, 64, 64, 64, 256, 256, 64)
+    return pl.pallas_call(
+        functools.partial(finish_kernel, clip_size=clip_size),
+        in_specs=[vm] * 8,
+        out_specs=[vm] * 10,
+        out_shape=[f(dx.shape, BF), f(dx.shape, BF)] + [f((2, 16, n), F32) for n in widths],
+        scratch_shapes=[
+            pltpu.VMEM((items, rows, feats), BF),
+            pltpu.VMEM((items, rows, feats), BF),
+            pltpu.VMEM((items, TOP, feats), BF),
+            pltpu.VMEM((clip_size, 16, 1024), F32),
+            pltpu.VMEM((clip_size, 16, 1024), BF),
+            pltpu.VMEM((clip_size, 16, 1024), BF),
+            pltpu.VMEM((clip_size, 16, 512), BF),
+            pltpu.VMEM((clip_size, 16, 512), BF),
+            pltpu.VMEM((clip_size, 16, 512), BF),
+            pltpu.VMEM((clip_size, 16, 512), BF),
+            pltpu.VMEM((4, 16, 512), F32),
+            pltpu.VMEM((4, 16, 512), F32),
+            pltpu.VMEM((2, 16, 1024), F32),
+            pltpu.SemaphoreType.DMA((20,)),
+            pltpu.SemaphoreType.DMA((20,)),
+        ],
+        compiler_params=pltpu.CompilerParams(
+            collective_id=1, has_side_effects=True, vmem_limit_bytes=VMEM_LIMIT
+        ),
+        cost_estimate=pl.CostEstimate(flops=2 * 10**10, bytes_accessed=2 * 10**7, transcendentals=0),
+        name="finish",
+    )(act, *act_pieces, dx, grad_qkv, grad_dense, ids)
 
 
 def exchange(x, win_size):
@@ -501,16 +913,20 @@
         if bit < bits:
             split = x.reshape(x.shape[0], local >> (bit + 1), 2, 1 << bit, TOK, -1)
             other = jnp.flip(split, axis=2).reshape(x.shape)
-        elif bit == 2:
-            half = lax.ppermute(
-                x[:, :, : TOK // 2], "win", [(i, i ^ 1 << bit - bits) for i in range(win_size)]
-            )
-            x = jnp.concatenate((half, x[:, :, TOK // 2 :]), axis=2)
-            continue
         else:
             other = lax.ppermute(x, "win", [(i, i ^ 1 << bit - bits) for i in range(win_size)])
         x = jnp.where(rows[None, None, :, None], other, x)
     return x
+
+
+def pieces_of(x):
+    top = x[:, :TOP]
+    return (
+        x,
+        lax.ppermute(x, "win", [(i, i ^ 1) for i in range(4)]),
+        lax.ppermute(top, "win", [(i, i ^ 2) for i in range(4)]),
+        lax.ppermute(top, "win", [(i, i ^ 3) for i in range(4)]),
+    )
 
 
 def place():
@@ -556,6 +972,37 @@
     return jnp.stack(blocks, axis=1).reshape(heads, TOK, TOK)
 
 
+def gather(array, spec):
+    for axis, name in enumerate(spec):
+        if name is not None:
+            array = lax.all_gather(array, name, axis=axis, tiled=True)
+    return array
+
+
+def stage_whole(proj_w, fc1_w, fc2_w, maps):
+    proj_down, proj_up, fc1_down, fc1_up, fc2_down, fc2_up = maps
+    count = proj_down.shape[0]
+
+    def short(a):
+        return a.reshape(4, count // 4 * 16, 8, 64).transpose(2, 0, 1, 3)
+
+    def long(a):
+        return a.reshape(4, count // 4 * 16, 8, 2, 128).transpose(2, 0, 3, 1, 4).reshape(8, 4, -1, 128)
+
+    return jnp.concatenate(
+        (
+            proj_w.reshape(8, 64, 4, 128).transpose(0, 2, 1, 3),
+            fc1_w.reshape(8, 64, 4, 4, 128).transpose(0, 2, 3, 1, 4).reshape(8, 4, 256, 128),
+            fc2_w.reshape(8, 256, 4, 128).transpose(0, 2, 1, 3),
+            jnp.concatenate((short(proj_down), short(proj_up)), axis=-1),
+            jnp.concatenate((short(fc1_down), short(fc2_up)), axis=-1),
+            long(fc1_up),
+            long(fc2_down),
+        ),
+        axis=2,
+    )
+
+
 def per_device(
     tokens, cotangent, adapter_ids, ln1_gain, qkv_weight, qkv_bias, proj_weight, proj_bias, ln2_gain,
     fc1_weight, fc1_bias, fc2_weight, fc2_bias, bias_table, qkv_down, qkv_up, proj_down, proj_up,
@@ -563,44 +1010,65 @@
 ):
     clips, local, rows, feats = tokens.shape
     items = clips * local
-    matrices = (qkv_weight, proj_weight, fc1_weight, fc2_weight)
-    downs = (qkv_down, proj_down, fc1_down, fc2_down)
-    ups = (qkv_up, proj_up, fc1_up, fc2_up)
+    heads = bias_table.shape[0]
     vecs = (ln1_gain, qkv_bias, proj_bias, ln2_gain, fc1_bias, fc2_bias)
-    pieces = [*matrices, *downs, *ups]
-    flat = jnp.concatenate([p.reshape(-1) for p in pieces])
-    got = lax.all_gather(flat, ("clip", "win"))
-    got = got.reshape(clip_size, win_size, -1)
-    full, at = [], 0
-    for n, p in enumerate(pieces):
-        part = got[:, :, at : at + p.size].reshape(clip_size, win_size, *p.shape)
-        at += p.size
-        if n < 4:
-            full.append(part.transpose(0, 2, 1, 3).reshape(clip_size * p.shape[0], -1))
-        elif n < 8:
-            full.append(part.transpose(1, 2, 4, 0, 3).reshape(win_size * p.shape[0], p.shape[2], -1))
-        else:
-            full.append(part.transpose(1, 2, 3, 0, 4).reshape(win_size * p.shape[0], p.shape[1], -1))
-    weights = full[:4]
-    adapters = [a for pair in zip(full[4:8], full[8:]) for a in pair]
-    flat = lax.all_gather(jnp.concatenate(vecs), "clip")
-    vectors, at = [], 0
-    for p in vecs:
-        vectors.append(flat[:, at : at + p.size].reshape(1, -1).astype(F32))
-        at += p.size
-    x = exchange(tokens, win_size).reshape(items, rows, feats)
-    dy = exchange(cotangent, win_size).reshape(items, rows, feats)
+    item_ids = jnp.repeat(adapter_ids, local)
+    masks = window_masks(lax.axis_index("win"), local)
+    flat = (items, rows, feats)
+    downs = [a.transpose(0, 2, 1) for a in (qkv_down, proj_down, fc1_down, fc2_down)]
+    own_kernels = (clip_size, win_size, clips, local) == (8, 4, 2, 2)
+    if own_kernels:
+        maps = [a.reshape(32, -1) for a in (downs[1], proj_up, downs[2], fc1_up, downs[3], fc2_up)]
+        later = jnp.concatenate(
+            (
+                proj_weight,
+                fc1_weight.reshape(64, 4, 128).transpose(1, 0, 2).reshape(256, 128),
+                fc2_weight,
+                jnp.concatenate((maps[0], maps[1]), axis=1),
+                jnp.concatenate((maps[2], maps[5]), axis=1),
+                maps[3][:, :128],
+                maps[3][:, 128:],
+                maps[4][:, :128],
+                maps[4][:, 128:],
+            ),
+            axis=0,
+        )
+        staged = lax.all_gather(later, ("clip", "win")).reshape(8, 4, 768, 128)
+        early = jnp.concatenate((downs[0].reshape(32, 64), qkv_up.reshape(32, 192)), axis=1)
+        unit = jnp.concatenate(
+            (qkv_weight, jnp.concatenate((early[:, :128], early[:, 128:]), axis=0)), axis=1
+        )
+        pairs = bias_table.reshape(heads, 15, 169).transpose(1, 0, 2).reshape(15 * heads, 169)
+        pairs = jnp.pad(pairs, ((0, 0), (0, 7)))
+        x, qkv_w, down, up, *vectors, ids, table = spread(
+            tokens.reshape(flat), unit, pack_vectors(vecs, adapter_ids), pairs, clip_size
+        )
+        dy = pieces_of(cotangent.reshape(flat))
+        qkv_parts = (qkv_w, down, up)
+    else:
+        grid2, by_down, by_up = ("clip", "win"), ("win", None, "clip"), ("win", None, "clip")
+        qkv_parts = (gather(qkv_weight, grid2), gather(downs[0], by_down), gather(qkv_up, by_up))
+        maps = (downs[1], proj_up, downs[2], fc1_up, downs[3], fc2_up)
+        staged = stage_whole(
+            *[gather(a, grid2) for a in (proj_weight, fc1_weight, fc2_weight)],
+            [gather(a, by_up) for a in maps],
+        )
+        vectors = [gather(v, ("clip",)).reshape(1, -1).astype(F32) for v in vecs]
+        table = bias_by_pair(bias_table)
+        x = exchange(tokens, win_size).reshape(flat)
+        dy = (exchange(cotangent, win_size).reshape(flat),)
     act, dx, grad_qkv, grad_dense = compute(
-        x,
-        dy,
-        jnp.repeat(adapter_ids, local),
-        vectors,
-        weights,
-        adapters,
-        window_masks(lax.axis_index("win"), local),
-        bias_by_pair(bias_table),
-        local,
+        x, dy, item_ids, vectors, qkv_parts, staged, masks, table, local
     )
+    if own_kernels:
+        act_out, dx_out, qd, qu, pd, pu, f1d, f1u, f2d, f2u = finish(
+            act, pieces_of(act)[1:], dx, grad_qkv, grad_dense, ids, clip_size
+        )
+        turned = [a.transpose(0, 2, 1) for a in (qd, pd, f1d, f2d)]
+        return (
+            act_out.reshape(tokens.shape), dx_out.reshape(tokens.shape),
+            turned[0], qu, turned[1], pu, turned[2], f1u, turned[3], f2u,
+        )
     activations = exchange(act.reshape(tokens.shape), win_size)
     input_grad = exchange(dx.reshape(tokens.shape), win_size)
     adapter_count = win_size * qkv_down.shape[0]
@@ -611,13 +1079,14 @@
     rank = grads.shape[1]
     parts, at = [], 0
     for span in spans:
-        part = grads[..., at : at + span].reshape(clips, rank, clip_size, span // clip_size)
+        parts.append(
+            grads[..., at : at + span].reshape(clips, rank, clip_size, span // clip_size)
+        )
         at += span
-        parts.append(part)
     mine = jnp.concatenate(parts, axis=-1)
-    spread = jnp.sum(hot[:, :, None, None, None] * mine[:, None], axis=0)
-    spread = spread.transpose(2, 0, 1, 3).astype(BF)
-    total = lax.psum_scatter(spread, "clip", scatter_dimension=0, tiled=True)[0]
+    grown = jnp.sum(hot[:, :, None, None, None] * mine[:, None], axis=0)
+    grown = grown.transpose(2, 0, 1, 3).astype(BF)
+    total = lax.psum_scatter(grown, "clip", scatter_dimension=0, tiled=True)[0]
     total = lax.psum_scatter(total, "win", scatter_dimension=0, tiled=True).astype(F32)
     outs, at = [], 0
     for n, span in enumerate(spans):

time: 483 us -> 316 us (0.65); the launches traced: 475 us -> 316 us
  local copies, waits for them, and re-layouts: 184 us -> 20.3 us
  Pallas kernels: 145 us -> 271 us
  waiting for transfers between devices: 45 us -> 0.05 us
  blocking collectives: 38.1 us -> 0 us
  other arithmetic: 40 us -> 4.15 us
    pallas_call x0 -> x2, Pallas kernels: none -> 123 us  [the longest x1 81.1 us: spread(): pl.pallas_call(functools.partial(spread_kernel, clip_size=clip_size), in_...]
    reshape x39 -> x4, local copies, waits for them, and re-layouts: 108 us -> 1.55 us  [the longest x1 0.6 us: pack_vectors(): return jnp.pad(flat, (0, 1024 - flat.shape[0])).reshape(8, 128)]
    unnamed x1 -> x0, blocking collectives: 38.1 us -> none
    ppermute x8 -> x6, waiting for transfers between devices: 36.3 us -> 0.02 us  [the longest x2 0.01 us: pieces_of(): lax.ppermute(top, 'win', [(i, i ^ 3) for i in range(4)])]
    select_n x5 -> x0, other arithmetic: 22.2 us -> none  [the longest x4 22.2 us: exchange(): x = jnp.where(rows[None, None, :, None], other, x)]
    slice x26 -> x3, local copies, waits for them, and re-layouts: 22.3 us -> 2.63 us  [the longest x2 2.55 us: pieces_of(): top = x[:, :TOP]]
    unnamed x89 -> x68, local copies, waits for them, and re-layouts: 29.4 us -> 14.6 us
    unnamed x8 -> x2, other arithmetic: 12.3 us -> 1.6 us
  transfers between devices with their start and end apart: 11 -> 7, of which waited for: 4 -> 0; matrix products, arithmetic and copies ran while one was open for 32% -> 2% of each run, Pallas kernels for 0% -> 54%
where the time goes in v2:
time: 316 us
  Pallas kernels  271 us (86%)
  local copies, waits for them, and re-layouts  20.3 us (6%)
  between operations  14.4 us (5%)
  starting transfers between devices  5.44 us (2%)
  other arithmetic  4.15 us (1%)
    pallas_call x1, Pallas kernels, spread(): pl.pallas_call(functools.partial(spread_kernel, clip_size=clip_size), in_...  81.1 us
    pallas_call x1, Pallas kernels, compute(): pl.pallas_call(functools.partial(dense_kernel, per_clip=per_clip, chunk=5...  58.2 us
    pallas_call x1, Pallas kernels, compute(): pl.pallas_call(functools.partial(attend_back_kernel, scale=scale, per_gro...  48.8 us
    pallas_call x1, Pallas kernels, finish(): pl.pallas_call(functools.partial(finish_kernel, clip_size=clip_size), in_...  42.1 us
    pallas_call x1, Pallas kernels, compute(): pl.pallas_call(functools.partial(attend_kernel, scale=scale, per_group=pe...  41.2 us
    unnamed x68, local copies, waits for them, and re-layouts  14.6 us
  transfers between devices with their start and end apart: 7, of which 0 were waited for; matrix products, arithmetic and copies ran while one was open for 2% of the time, Pallas kernels for 54%

profile of v2, /device:TPU:0, one launch (start us, length us, event | category | flops | bytes accessed | tf_op | source)
XLA Modules:
  0.0 315.7 jit_solution(17553324226193819572)
XLA Ops:
  7.3 0.8 constant_dynamic-update-slice_fusion.8
  8.2 0.9 constant_dynamic-update-slice_fusion.6
  9.1 0.8 constant_dynamic-update-slice_fusion.5
  9.9 0.8 constant_dynamic-update-slice_fusion.4
  10.7 0.7 constant_dynamic-update-slice_fusion.3
  11.4 0.7 constant_dynamic-update-slice_fusion.2
  12.1 0.7 constant_dynamic-update-slice_fusion.1
  12.8 0.7 constant_dynamic-update-slice_fusion
  13.5 0.7 copy-done.5
  14.2 1.2 slice.37
  15.4 3.0 collective-permute-start.1
  19.8 0.7 pad.9.pairs_ref
  21.3 0.7 fusion.3.unit_ref
  22.0 0.9 fusion.1.key_mask_ref
  22.9 0.8 select_convert_fusion.query_mask_ref
  23.7 81.1 %spread.1 = (bf16[4,392,512]{2,1,0:T(8,128)(2,1)}, bf16[512,1536]{1,0:T(8,128)(2,1)}, bf16[8,16,512]{2,1,0:T(8,128)(2,1)}, bf16[8,16,1536]{2,1,0:T(8,128)(2,1)},...) custom-call(bf16[4,392,512]{2,1,0:T(8,128)(2,1)} %bitcast.67, ...), custom_call_target="tpu_custom_call" | custom-call | flops 30000001024 | bytes 20000000 | tf_op jit(solution)/shard_map/spread/pallas_call | solution.py:718
  104.8 41.2 %attend.1 = (bf16[4,16,392,392]{3,2,1,0:T(8,128)(2,1)}, bf16[4,392,512]{2,1,0:T(8,128)(2,1)}, bf16[4,392,1536]{2,1,0:T(8,128)(2,1)}, bf16[4,392,16]{2,1,0:T(8,128)(2,1)}) custom-call(s32[4]{0:T(128)} %reshape.327.ids_ref, bf16[4,392,512]{2,1,0:T(8,128)(2,1)} %get-tuple-element.42.x_ref, f32[1,512]{1,0:T(1,128)} %get-tuple-element.43.gain_ref, ...), custom_call_target="tpu_custom_call" | custom-call | flops 40000000000 | bytes 10000000 | tf_op jit(solution)/shard_map/attend/pallas_call | solution.py:405
  146.0 58.2 %dense.1 = (bf16[4,392,512]{2,1,0:T(8,128)(2,1)}, f32[4,392,512]{2,1,0:T(8,128)}, bf16[4,392,512]{2,1,0:T(8,128)(2,1)}, f32[2,16,6144]{2,1,0:T(8,128)}) custom-call(s32[4]{0:T(128)} %reshape.327.ids_ref, bf16[4,392,512]{2,1,0:T(8,128)(2,1)} %get-tuple-element.42.x_ref, bf16[4,392,512]{2,1,0:T(8,128)(2,1)} %get-tuple-element.49.attn_ref, ...), custom_call_target="tpu_custom_call" | custom-call | flops 49999998976 | bytes 10000000 | tf_op jit(solution)/shard_map/dense/pallas_call | solution.py:459
  204.3 1.3 slice.31
  205.6 1.5 collective-permute-start.4
  207.1 0.7 collective-permute-start.3
  207.8 48.8 %attend_back.1 = (bf16[4,392,512]{2,1,0:T(8,128)(2,1)}, f32[2,16,2048]{2,1,0:T(8,128)}) custom-call(s32[4]{0:T(128)} %reshape.327.ids_ref, bf16[4,392,512]{2,1,0:T(8,128)(2,1)} %get-tuple-element.42.x_ref, f32[1,512]{1,0:T(1,128)} %get-tuple-element.43.gain_ref, bf16[512,1536]{1,0:T(8,128)(2,1)} %get-tuple-element.44.weight_ref, ...), custom_call_target="tpu_custom_call" | custom-call | flops 49999998976 | bytes 10000000 | tf_op jit(solution)/shard_map/attend_back/pallas_call | solution.py:504
  256.7 1.1 copy-done.24
  257.8 42.1 %finish.1 = (bf16[4,392,512]{2,1,0:T(8,128)(2,1)}, bf16[4,392,512]{2,1,0:T(8,128)(2,1)}, f32[2,16,64]{2,1,0:T(8,128)}, f32[2,16,192]{2,1,0:T(8,128)}, f32[2,16,6...) custom-call(bf16[4,392,512]{2,1,0:T(8,128)(2,1)} %get-tuple-element., ...), custom_call_target="tpu_custom_call" | custom-call | flops 20000000000 | bytes 20000000 | tf_op jit(solution)/shard_map/finish/pallas_call | solution.py:877
  299.9 2.8 copy.56
  302.8 1.2 copy.57
  303.9 0.6 copy.58
  304.5 0.6 copy.59
  305.2 0.6 copy.60
  307.0 0.6 copy.63
  307.6 0.6 copy.64
  308.2 0.6 copy.65
  (80 shorter events, 3.6 us)
Async XLA Ops:
  7.2 1.0 copy-start
  7.2 11.2 %copy-start.3 = (bf16[2,2,392,512]{3,2,1,0:T(8,128)(2,1)S(1)}, bf16[2,2,392,512]{3,2,1,0:T(8,128)(2,1)}, u32[]{:S(2)}) copy-start(bf16[2,2,392,512]{3,2,1,0:T(8,128)(2,1)} %param.23) | copy-start | bytes 4816900
  7.2 11.4 %copy-start.8 = (bf16[2,16,192]{2,1,0:T(8,128)(2,1)S(1)}, bf16[2,16,192]{2,1,0:T(8,128)(2,1)}, u32[]{:S(2)}) copy-start(bf16[2,16,192]{2,1,0:T(8,128)(2,1)} %param.37) | copy-start | bytes 36868
  7.2 11.5 %copy-start.6 = (bf16[16,2535]{1,0:T(8,128)(2,1)S(1)}, bf16[16,2535]{1,0:T(8,128)(2,1)}, u32[]{:S(2)}) copy-start(bf16[16,2535]{1,0:T(8,128)(2,1)} %param.35) | copy-start | bytes 243364
  7.2 11.9 %copy-start.25 = (s32[2]{0:T(128)S(1)}, s32[2]{0:T(128)}, u32[]{:S(2)}) copy-start(s32[2]{0:T(128)} %param.24) | copy-start | bytes 28
  7.2 13.2 %copy-start.18 = (bf16[64]{0:T(256)(128)(2,1)S(1)}, bf16[64]{0:T(256)(128)(2,1)}, u32[]{:S(2)}) copy-start(bf16[64]{0:T(256)(128)(2,1)} %param.25) | copy-start | bytes 388
  7.2 13.2 %copy-start.19 = (bf16[192]{0:T(256)(128)(2,1)S(1)}, bf16[192]{0:T(256)(128)(2,1)}, u32[]{:S(2)}) copy-start(bf16[192]{0:T(256)(128)(2,1)} %param.27) | copy-start | bytes 1156
  7.3 13.2 %copy-start.20 = (bf16[64]{0:T(256)(128)(2,1)S(1)}, bf16[64]{0:T(256)(128)(2,1)}, u32[]{:S(2)}) copy-start(bf16[64]{0:T(256)(128)(2,1)} %param.29) | copy-start | bytes 388
  7.3 13.2 %copy-start.21 = (bf16[64]{0:T(256)(128)(2,1)S(1)}, bf16[64]{0:T(256)(128)(2,1)}, u32[]{:S(2)}) copy-start(bf16[64]{0:T(256)(128)(2,1)} %param.30) | copy-start | bytes 388
  7.3 13.2 %copy-start.22 = (bf16[256]{0:T(256)(128)(2,1)S(1)}, bf16[256]{0:T(256)(128)(2,1)}, u32[]{:S(2)}) copy-start(bf16[256]{0:T(256)(128)(2,1)} %param.32) | copy-start | bytes 1540
  7.3 13.2 %copy-start.23 = (bf16[64]{0:T(256)(128)(2,1)S(1)}, bf16[64]{0:T(256)(128)(2,1)}, u32[]{:S(2)}) copy-start(bf16[64]{0:T(256)(128)(2,1)} %param.34) | copy-start | bytes 388
  7.3 138.7 %all-gather.3.cloned.1.call-start = ((), (), s32[]{:S(2)}) async-start(), calls=%async_computation | async-start | bytes 6488064 | tf_op jit(solution)/shard_map/all_gather | solution.py:1036
  8.2 13.1 %copy-start.7 = (bf16[64,384]{1,0:T(8,128)(2,1)S(1)}, bf16[64,384]{1,0:T(8,128)(2,1)}, u32[]{:S(2)}) copy-start(bf16[64,384]{1,0:T(8,128)(2,1)} %param.26) | copy-start | bytes 147460
  8.2 13.1 %copy-start.17 = (bf16[2,64,16]{1,2,0:T(8,128)(2,1)S(1)}, bf16[2,64,16]{1,2,0:T(8,128)(2,1)}, u32[]{:S(2)}) copy-start(bf16[2,64,16]{1,2,0:T(8,128)(2,1)} %param.36) | copy-start | bytes 12292
  15.4 130.6 %collective-permute-start.1 = (bf16[4,208,512]{2,1,0:T(8,128)(2,1)S(1)}, bf16[4,208,512]{2,1,0:T(8,128)(2,1)}, u32[]{:S(2)}, u32[]{:S(2)}) collective-permute-start(bf16[4,208,512]{2,1,0:T(8,128)(2,1)S(1)} %slice.37), channel_id=1, source_target_pairs={{0,2},{1,3},{2,0},{3,1},{4,6},{5,7},{6,4},{7,5},{8,10},{9,11},{10,... | collective-permute-start | bytes 2555912 | tf_op jit(solution)/shard_map/ppermute | solution.py:927
  18.4 127.6 %collective-permute-start.2 = (bf16[4,208,512]{2,1,0:T(8,128)(2,1)S(1)}, bf16[4,208,512]{2,1,0:T(8,128)(2,1)}, u32[]{:S(2)}, u32[]{:S(2)}) collective-permute-start(bf16[4,208,512]{2,1,0:T(8,128)(2,1)S(1)} %slice.37), channel_id=1, source_target_pairs={{0,3},{1,2},{2,1},{3,0},{4,7},{5,6},{6,5},{7,4},{8,11},{9,10},{10,... | collective-permute-start | bytes 2555912 | tf_op jit(solution)/shard_map/ppermute | solution.py:928
  18.4 127.6 %collective-permute-start = (bf16[4,392,512]{2,1,0:T(8,128)(2,1)S(1)}, bf16[4,392,512]{2,1,0:T(8,128)(2,1)}, u32[]{:S(2)}, u32[]{:S(2)}) collective-permute-start(bf16[4,392,512]{2,1,0:T(8,128)(2,1)S(1)} %bitcast.43), channel_id=1, source_target_pairs={{0,1},{1,0},{2,3},{3,2},{4,5},{5,4},{6,7},{7,6},{8,9},{9,8},{10,11... | collective-permute-start | bytes 4816904 | tf_op jit(solution)/shard_map/ppermute | solution.py:926
  204.3 2.8 copy-start.4
  205.6 51.0 %collective-permute-start.4 = (bf16[4,208,512]{2,1,0:T(8,128)(2,1)S(1)}, bf16[4,208,512]{2,1,0:T(8,128)(2,1)}, u32[]{:S(2)}, u32[]{:S(2)}) collective-permute-start(bf16[4,208,512]{2,1,0:T(8,128)(2,1)S(1)} %slice.31), channel_id=1, source_target_pairs={{0,2},{1,3},{2,0},{3,1},{4,6},{5,7},{6,4},{7,5},{8,10},{9,11},{10,... | collective-permute-start | bytes 2555912 | tf_op jit(solution)/shard_map/ppermute | solution.py:927
  207.1 49.6 %collective-permute-start.5 = (bf16[4,208,512]{2,1,0:T(8,128)(2,1)S(1)}, bf16[4,208,512]{2,1,0:T(8,128)(2,1)}, u32[]{:S(2)}, u32[]{:S(2)}) collective-permute-start(bf16[4,208,512]{2,1,0:T(8,128)(2,1)S(1)} %slice.31), channel_id=1, source_target_pairs={{0,3},{1,2},{2,1},{3,0},{4,7},{5,6},{6,5},{7,4},{8,11},{9,10},{10,... | collective-permute-start | bytes 2555912 | tf_op jit(solution)/shard_map/ppermute | solution.py:928
  207.1 49.6 %collective-permute-start.3 = (bf16[4,392,512]{2,1,0:T(8,128)(2,1)S(1)}, bf16[4,392,512]{2,1,0:T(8,128)(2,1)S(1)}, u32[]{:S(2)}, u32[]{:S(2)}) collective-permute-start(bf16[4,392,512]{2,1,0:T(8,128)(2,1)S(1)} %copy-done.4), channel_id=1, source_target_pairs={{0,1},{1,0},{2,3},{3,2},{4,5},{5,4},{6,7},{7,6},{8,9},{9,8},{10,11... | collective-permute-start | bytes 4816904 | tf_op jit(solution)/shard_map/ppermute | solution.py:926
  256.7 1.2 copy-start.24
  299.9 2.8 copy-start.2
  299.9 8.9 %copy-start.1 = (bf16[64,512]{1,0:T(8,128)(2,1)S(1)}, bf16[64,512]{1,0:T(8,128)(2,1)}, u32[]{:S(2)}) copy-start(bf16[64,512]{1,0:T(8,128)(2,1)} %param.31) | copy-start | bytes 196612
  302.7 1.2 copy-start.16
  302.7 1.8 copy-start.11
  302.7 2.4 copy-start.15
  302.7 3.0 copy-start.14
  302.7 3.6 %copy-start.13 = (f32[2,16,64]{2,1,0:T(8,128)S(1)}, f32[2,16,64]{2,1,0:T(8,128)}, u32[]{:S(2)}) copy-start(f32[2,16,64]{2,1,0:T(8,128)} %get-tuple-element.70) | copy-start | bytes 24580
  302.7 4.2 %copy-start.10 = (f32[2,16,256]{2,1,0:T(8,128)S(1)}, f32[2,16,256]{2,1,0:T(8,128)}, u32[]{:S(2)}) copy-start(f32[2,16,256]{2,1,0:T(8,128)} %get-tuple-element.95) | copy-start | bytes 98308
  302.8 4.8 %copy-start.9 = (f32[2,16,256]{2,1,0:T(8,128)S(1)}, f32[2,16,256]{2,1,0:T(8,128)}, u32[]{:S(2)}) copy-start(f32[2,16,256]{2,1,0:T(8,128)} %get-tuple-element.72) | copy-start | bytes 98308
  302.8 5.5 %copy-start.12 = (f32[2,16,64]{2,1,0:T(8,128)S(1)}, f32[2,16,64]{2,1,0:T(8,128)}, u32[]{:S(2)}) copy-start(f32[2,16,64]{2,1,0:T(8,128)} %get-tuple-element.97) | copy-start | bytes 24580
  (1 other events, 0.7 us)
Sparse Core Ops, SparseCore 0:
  14.3 89.3 all-gather.2

commit v3 on v2

--- a/solution.py
+++ b/solution.py
@@ -72,6 +72,8 @@
     values_t,
     out_t,
     scores,
+    table,
+    table_sem,
     *,
     scale,
     per_group,
@@ -80,12 +82,22 @@
     group = pl.program_id(1)
     groups = pl.num_programs(1)
     feats = x_ref.shape[-1]
+    starting = pl.program_id(0) == 0
+
+    def table_copy(g):
+        at = pl.ds(g * per_group, per_group)
+        return pltpu.make_async_copy(table_ref.at[at], table.at[at], table_sem.at[g])
+
+    @pl.when(starting & (group == 0))
+    def _():
+        for g in range(table.shape[0] // per_group):
+            table_copy(g).start()
 
     @pl.when(group == 0)
     def _():
         normed, _ = norm_stats(x_ref[0].astype(F32))
         low = (normed * gain_ref[...]).astype(BF)
-        reduced = dot(low, down_ref[0], NT).astype(BF)
+        reduced = dot(down_ref[0], low, NT).astype(BF)
         reduced_ref[0] = reduced
 
         def columns(part):
@@ -93,7 +105,7 @@
             return (
                 dot(low, weight_ref[:, at], NN)
                 + bias_ref[:, at]
-                + dot(reduced, up_ref[0, :, at], NN)
+                + dot(reduced, up_ref[0, :, at], TN)
             )
 
         query = (columns(0) * (scale * LOG2E)).astype(BF)
@@ -105,8 +117,13 @@
             keys[:, 256 * g : 256 * g + 128] = key[:, 128 * g : 128 * g + 128]
             keys[:, 256 * g + 128 : 256 * g + 256] = key_mask_ref[0]
         value = columns(2)
-        qkv_ref[0, :, 2 * feats :] = value.astype(BF)
-        values_t[...] = value.T.astype(BF)
+        value = value.astype(BF)
+        qkv_ref[0, :, 2 * feats :] = value
+        values_t[...] = value.T
+
+    @pl.when(starting)
+    def _():
+        table_copy(group).wait()
 
     keys_now = keys[:, pl.ds(pl.multiple_of(group * 256, 256), 256)]
     query_now = queries[:, pl.ds(pl.multiple_of(group * 128, 128), 128)]
@@ -115,7 +132,7 @@
     def raw(h):
         own = jnp.where(head_of_lane == h, query_now, jnp.zeros_like(query_now))
         own = jnp.concatenate([own, query_mask_ref[0]], axis=1)
-        return dot(keys_now, own, NT) + table_ref[group * per_group + h]
+        return dot(keys_now, own, NT) + table[group * per_group + h]
 
     def finish(h):
         score = scores[h % 2]
@@ -125,7 +142,7 @@
         probs = (probs * (1.0 / total)).astype(BF)
         probs_ref[0, h] = probs
         at = pl.ds(pl.multiple_of((group * per_group + h) * width, width), width)
-        out_t[at, :] = dot(values_t[at, :], probs, NN)
+        out_t[at, :] = dot(values_t[at, :], probs, NN).astype(BF)
 
     scores[0] = raw(0)
     for h in range(per_group):
@@ -135,7 +152,7 @@
 
     @pl.when(group == groups - 1)
     def _():
-        out_ref[0] = out_t[...].T.astype(BF)
+        out_ref[0] = out_t[...].T
 
 
 def row_masks(rows, columns):
@@ -175,112 +192,131 @@
     tiles, refs = refs[:6], refs[6:]
     dy_refs, refs = refs[:pieces], refs[pieces:]
     act_ref, dx1_ref, dattn_ref, grad_ref, *refs = refs
-    proj_ref, fc1_ref, fc2_ref, proj_down, proj_up, fc1_down, fc1_up, fc2_down, fc2_up, sem = refs
-
-    @pl.when(pl.program_id(0) == 0)
-    def _():
-        copies = []
-        for n in range(4):
-            moves = [(0, 64, proj_ref, 128 * n), (320, 256, fc2_ref, 128 * n)]
-            moves += [(64 + 64 * t, 64, fc1_ref, 512 * n + 128 * t) for t in range(4)]
-            for start, size, target, lane in moves:
-                copies.append(
-                    pltpu.make_async_copy(
-                        staged_ref.at[:, n, pl.ds(start, size), :],
-                        target.at[:, :, pl.ds(lane, 128)],
-                        sem.at[len(copies)],
-                    )
-                )
-        for copy in copies:
-            copy.start()
-        for copy in copies:
-            copy.wait()
-
-    @pl.when(pl.program_id(0) % per_clip == 0)
-    def _():
-        for n in range(8):
-            short = slice(64 * n, 64 * n + 64)
-            proj_down[:, short] = tiles[0][n, 0, :, 0:64]
-            proj_up[:, short] = tiles[0][n, 0, :, 64:128]
-            fc1_down[:, short] = tiles[1][n, 0, :, 0:64]
-            fc2_up[:, short] = tiles[1][n, 0, :, 64:128]
-            for half in range(2):
-                long = slice(256 * n + 128 * half, 256 * n + 128 * half + 128)
-                fc1_up[:, long] = tiles[2 + half][n, 0]
-                fc2_down[:, long] = tiles[4 + half][n, 0]
-
-    if pieces == 1:
-        dy = dy_refs[0][0]
-    else:
-        dy = join_pieces(dy_refs, pl.program_id(0) % 2)
-    proj_w = proj_ref[...].reshape(proj_ref.shape[0] * proj_ref.shape[1], -1)
-    per_chunk = chunk // fc2_ref.shape[1]
-    first = pl.program_id(0) % per_clip == 0
+    proj_ref, fc1_ref, fc2_ref, proj_down, proj_up, fc1_down, fc1_up, fc2_down, fc2_up, *refs = refs
+    pres, acts, dpres, sem = refs
+    starting = pl.program_id(0) == 0
+    count = x_ref.shape[1]
     feats = x_ref.shape[-1]
     hidden = fc1_ref.shape[-1]
-    attn = attn_ref[0]
-    reduced_proj = dot(attn, proj_down[...], NT).astype(BF)
+
+    def moves(first=0, last=24):
+        found = [(0, 64, proj_ref, 128 * n, n) for n in range(4)]
+        found += [(64 + 64 * t, 64, fc1_ref, 512 * n + 128 * t, n) for n in range(4) for t in range(4)]
+        found += [(320, 256, fc2_ref, 128 * n, n) for n in range(4)]
+        return [
+            pltpu.make_async_copy(
+                staged_ref.at[:, n, pl.ds(start, size), :],
+                target.at[:, :, pl.ds(lane, 128)],
+                sem.at[at],
+            )
+            for at, (start, size, target, lane, n) in enumerate(found)
+            if first <= at < last
+        ]
+
+    def arrive(first, last):
+        @pl.when(starting)
+        def _():
+            for copy in moves(first, last):
+                copy.wait()
+
+    @pl.when(starting)
+    def _():
+        for copy in moves():
+            copy.start()
+
+    for n in range(8):
+        short = slice(64 * n, 64 * n + 64)
+        proj_down[:, short] = tiles[0][n, 0, :, 0:64]
+        proj_up[:, short] = tiles[0][n, 0, :, 64:128]
+        fc1_down[:, short] = tiles[1][n, 0, :, 0:64]
+        fc2_up[:, short] = tiles[1][n, 0, :, 64:128]
+        for half in range(2):
+            long = slice(256 * n + 128 * half, 256 * n + 128 * half + 128)
+            fc1_up[:, long] = tiles[2 + half][n, 0]
+            fc2_down[:, long] = tiles[4 + half][n, 0]
+
+    def join(parts):
+        return jnp.concatenate(parts, axis=0) if per_clip > 1 else parts[0]
+
+    if pieces == 1:
+        dy = join([dy_refs[0][e] for e in range(per_clip)])
+    else:
+        dy = join([join_pieces(dy_refs, e) for e in range(per_clip)])
+    attn = join([attn_ref[e] for e in range(per_clip)])
+    reduced_proj = dot(proj_down[...], attn, NT).astype(BF)
+    arrive(0, 4)
+    proj_w = proj_ref[...].reshape(feats, feats)
     middle = (
-        x_ref[0].astype(F32)
+        join([x_ref[e].astype(F32) for e in range(per_clip)])
         + dot(attn, proj_w, NN)
         + proj_bias_ref[...]
-        + dot(reduced_proj, proj_up[...], NN)
+        + dot(reduced_proj, proj_up[...], TN)
     )
     normed, inverse = norm_stats(middle)
     low = (normed * gain_ref[...]).astype(BF)
-    reduced_fc1 = dot(low, fc1_down[...], NT).astype(BF)
-    grad_reduced_fc2 = dot(dy, fc2_up[...], NT).astype(BF)
+    reduced_fc1 = dot(fc1_down[...], low, NT).astype(BF)
+    grad_reduced_fc2 = dot(fc2_up[...], dy, NT).astype(BF)
+    per_chunk = chunk // fc2_ref.shape[1]
+    steps = hidden // chunk
+
+    def pre_of(j):
+        at = slice(j * chunk, (j + 1) * chunk)
+        pres[j % 2] = (
+            dot(low, fc1_ref[:, :, at].reshape(feats, chunk), NN)
+            + fc1_bias_ref[:, at]
+            + dot(reduced_fc1, fc1_up[:, at], TN)
+        )
+
+    arrive(4, 20)
+    pre_of(0)
+    arrive(20, 24)
+    for j in range(steps):
+        at = slice(j * chunk, (j + 1) * chunk)
+        if j + 1 < steps:
+            pre_of(j + 1)
+        fc2_w = fc2_ref[j * per_chunk : (j + 1) * per_chunk].reshape(chunk, feats)
+        dact = dot(dy, fc2_w, NT) + dot(grad_reduced_fc2, fc2_down[:, at], TN)
+        pre = pres[j % 2]
+        bell = jnp.exp2((pre * pre) * (-0.5 * LOG2E))
+        t = 1.0 / (1.0 + jnp.abs(pre) * (0.3275911 * 0.7071067811865476))
+        poly = (
+            (((0.5 * 1.061405429) * t - 0.5 * 1.453152027) * t + 0.5 * 1.421413741) * t
+            - 0.5 * 0.284496736
+        ) * t + 0.5 * 0.254829592
+        tail = poly * t * bell
+        below = jnp.where(pre >= 0.0, 1.0 - tail, tail)
+        acts[:, at] = (pre * below).astype(BF)
+        dpres[:, at] = (dact * (below + pre * bell * 0.3989422804014327)).astype(BF)
+    act = acts[...]
+    dpre = dpres[...]
     fc1_up_at = 3 * feats
     fc2_down_at = fc1_up_at + hidden
     fc2_up_at = fc2_down_at + hidden
-    total = middle + fc2_bias_ref[...]
-    reduced_fc2 = None
-    grad_low = None
-    grad_reduced_fc1 = None
-    for j in range(hidden // chunk):
-        at = slice(j * chunk, (j + 1) * chunk)
-        fc1_w = fc1_ref[:, :, at].reshape(feats, chunk)
-        fc2_w = fc2_ref[j * per_chunk : (j + 1) * per_chunk].reshape(chunk, feats)
-        pre = (
-            dot(low, fc1_w, NN)
-            + fc1_bias_ref[:, at]
-            + dot(reduced_fc1, fc1_up[:, at], NN)
-        )
-        size = jnp.abs(pre)
-        bell = jnp.exp2((pre * pre) * (-0.5 * LOG2E))
-        t = 1.0 / (1.0 + size * (0.3275911 * 0.7071067811865476))
-        poly = ((((0.5 * 1.061405429) * t - 0.5 * 1.453152027) * t + 0.5 * 1.421413741) * t - 0.5 * 0.284496736) * t + 0.5 * 0.254829592
-        tail = poly * t * bell
-        below = jnp.where(pre >= 0.0, 1.0 - tail, tail)
-        act = (pre * below).astype(BF)
-        slope = below + pre * bell * 0.3989422804014327
-        partial = dot(act, fc2_w, NN)
-        total = total + partial
-        partial = dot(act, fc2_down[:, at], NT)
-        reduced_fc2 = partial if reduced_fc2 is None else reduced_fc2 + partial
-        dact = dot(dy, fc2_w, NT) + dot(grad_reduced_fc2, fc2_down[:, at], NN)
-        dpre = (dact * slope).astype(BF)
-        partial = dot(dpre, fc1_w, NT)
-        grad_low = partial if grad_low is None else grad_low + partial
-        partial = dot(dpre, fc1_up[:, at], NT)
-        grad_reduced_fc1 = partial if grad_reduced_fc1 is None else grad_reduced_fc1 + partial
-        add_rows(grad_ref, slice(fc1_up_at + j * chunk, fc1_up_at + (j + 1) * chunk), dot(reduced_fc1, dpre, TN), first)
-        add_rows(grad_ref, slice(fc2_down_at + j * chunk, fc2_down_at + (j + 1) * chunk), dot(grad_reduced_fc2, act, TN), first)
-    reduced_fc2 = reduced_fc2.astype(BF)
-    act_ref[0] = (total + dot(reduced_fc2, fc2_up[...], NN)).astype(BF)
-    add_rows(grad_ref, slice(fc2_up_at, fc2_up_at + feats), dot(reduced_fc2, dy, TN), first)
-    grad_reduced_fc1 = grad_reduced_fc1.astype(BF)
-    grad_low = grad_low + dot(grad_reduced_fc1, fc1_down[...], NN)
-    add_rows(grad_ref, slice(2 * feats, 3 * feats), dot(grad_reduced_fc1, low, TN), first)
-    dx1 = dy.astype(F32) + norm_back(grad_low, gain_ref[...], normed, inverse)
-    dx1_ref[0] = dx1
+    fc1_w = fc1_ref[...].reshape(feats, hidden)
+    fc2_w = fc2_ref[...].reshape(hidden, feats)
+    grad_reduced_fc1 = dot(fc1_up[...], dpre, NT).astype(BF)
+    dlow = dot(dpre, fc1_w, NT) + dot(grad_reduced_fc1, fc1_down[...], TN)
+    dx1 = dy.astype(F32) + norm_back(dlow, gain_ref[...], normed, inverse)
     branch = dx1.astype(BF)
-    grad_reduced_proj = dot(branch, proj_up[...], NT).astype(BF)
-    add_rows(grad_ref, slice(feats, 2 * feats), dot(reduced_proj, branch, TN), first)
-    add_rows(grad_ref, slice(0, feats), dot(grad_reduced_proj, attn, TN), first)
-    dattn_ref[0] = (
-        dot(branch, proj_w, NT) + dot(grad_reduced_proj, proj_down[...], NN)
+    reduced_fc2 = dot(fc2_down[...], act, NT).astype(BF)
+    total = (
+        middle + fc2_bias_ref[...] + dot(act, fc2_w, NN) + dot(reduced_fc2, fc2_up[...], TN)
     ).astype(BF)
+    grad_reduced_proj = dot(proj_up[...], branch, NT).astype(BF)
+    dattn = (
+        dot(branch, proj_w, NT) + dot(grad_reduced_proj, proj_down[...], TN)
+    ).astype(BF)
+    for e in range(per_clip):
+        rows = slice(e * count, (e + 1) * count)
+        act_ref[e] = total[rows]
+        dx1_ref[e] = dx1[rows]
+        dattn_ref[e] = dattn[rows]
+    grad_ref[0, :, :feats] = dot(grad_reduced_proj, attn, NN)
+    grad_ref[0, :, feats : 2 * feats] = dot(reduced_proj, branch, NN)
+    grad_ref[0, :, 2 * feats : fc1_up_at] = dot(grad_reduced_fc1, low, NN)
+    grad_ref[0, :, fc1_up_at:fc2_down_at] = dot(reduced_fc1, dpre, NN)
+    grad_ref[0, :, fc2_down_at:fc2_up_at] = dot(grad_reduced_fc2, act, NN)
+    grad_ref[0, :, fc2_up_at:] = dot(reduced_fc2, dy, NN)
 
 
 def attend_back_kernel(
@@ -316,7 +352,7 @@
 
     @pl.when(group == 0)
     def _():
-        keys_t[...] = qkv_ref[0, :, feats : 2 * feats].astype(F32).T.astype(BF)
+        keys_t[...] = qkv_ref[0, :, feats : 2 * feats].T
         lane = lane_ids((rows, 128))
         ones = jnp.where(lane % width < 2, 1.0, 0.0).astype(BF)
         source = lax.broadcasted_iota(jnp.int32, (128, 128), 0)
@@ -358,21 +394,21 @@
         partial = dot(dscore, query_own, NN)
         dkey = partial if dkey is None else dkey + partial
         at = pl.ds(pl.multiple_of((group * per_group + h) * width, width), width)
-        dquery_t[at, :] = dot(keys_t[at, :], dscore, NN)
+        dquery_t[at, :] = (dot(keys_t[at, :], dscore, NN) * scale).astype(BF)
     dqkv[:, pl.ds(pl.multiple_of(2 * feats + group * 128, 128), 128)] = dvalue.astype(BF)
     dqkv[:, pl.ds(pl.multiple_of(feats + group * 128, 128), 128)] = (dkey * LN2).astype(BF)
 
     @pl.when(group == groups - 1)
     def _():
         first = pl.program_id(0) % per_clip == 0
-        dqkv[:, :feats] = (dquery_t[...].T * scale).astype(BF)
+        dqkv[:, :feats] = dquery_t[...].T
         dall = dqkv[...]
         normed, inverse = norm_stats(x_ref[0].astype(F32))
         low = (normed * gain_ref[...]).astype(BF)
-        grad_reduced = dot(dall, up_ref[0], NT).astype(BF)
-        add_rows(grad_ref, slice(feats, 4 * feats), dot(reduced_ref[0], dall, TN), first)
-        add_rows(grad_ref, slice(0, feats), dot(grad_reduced, low, TN), first)
-        dlow = (dot(dall, weight_ref[...], NT) + dot(grad_reduced, down_ref[0], NN)).astype(BF)
+        grad_reduced = dot(up_ref[0], dall, NT).astype(BF)
+        add_rows(grad_ref, slice(feats, 4 * feats), dot(reduced_ref[0], dall, NN), first)
+        add_rows(grad_ref, slice(0, feats), dot(grad_reduced, low, NN), first)
+        dlow = (dot(dall, weight_ref[...], NT) + dot(grad_reduced, down_ref[0], TN)).astype(BF)
         dx_ref[0] = (
             dx1_ref[0] + norm_back(dlow.astype(F32), gain_ref[...], normed, inverse)
         ).astype(BF)
@@ -416,27 +452,29 @@
                 adapter(qkv_up),
                 pl.BlockSpec((1, rows, 128), lambda i, g, ids: (i % per_clip, 0, 0)),
                 pl.BlockSpec((1, rows, 128), lambda i, g, ids: (i % per_clip, 0, 0)),
-                whole(table.shape),
+                pl.BlockSpec(memory_space=pl.ANY),
             ],
             out_specs=[
                 pl.BlockSpec((1, per_group, rows, rows), lambda i, g, ids: (i, g, 0, 0)),
                 item((rows, feats)),
                 item((rows, 3 * feats)),
-                item((rows, rank)),
+                item((rank, rows)),
             ],
             scratch_shapes=[
                 pltpu.VMEM((rows, 2 * feats), BF),
                 pltpu.VMEM((rows, feats), BF),
                 pltpu.VMEM((feats, rows), BF),
-                pltpu.VMEM((feats, rows), F32),
+                pltpu.VMEM((feats, rows), BF),
                 pltpu.VMEM((2, rows, rows), F32),
+                pltpu.VMEM(table.shape, F32),
+                pltpu.SemaphoreType.DMA((groups,)),
             ],
         ),
         out_shape=[
             jax.ShapeDtypeStruct((items, heads, rows, rows), BF),
             jax.ShapeDtypeStruct((items, rows, feats), BF),
             jax.ShapeDtypeStruct((items, rows, 3 * feats), BF),
-            jax.ShapeDtypeStruct((items, rows, rank), BF),
+            jax.ShapeDtypeStruct((items, rank, rows), BF),
         ],
         compiler_params=pltpu.CompilerParams(
             vmem_limit_bytes=VMEM_LIMIT, dimension_semantics=("arbitrary", "arbitrary")
@@ -448,41 +486,44 @@
     span = 4 * feats + 2 * hidden
     def tile(n):
         return pl.BlockSpec(
-            (8, 1, rank, 128), lambda i, ids: (0, ids[i] // 2, 36 + 2 * n + ids[i] % 2, 0)
+            (8, 1, rank, 128),
+            lambda c, ids: (0, ids[c * per_clip] // 2, 36 + 2 * n + ids[c * per_clip] % 2, 0),
         )
 
-    def piece(array):
-        if len(dy) == 1:
-            return item(array.shape[1:])
-        return pl.BlockSpec((per_clip, *array.shape[1:]), lambda i, ids: (i // per_clip, 0, 0))
-
+    def clip(array_shape):
+        return pl.BlockSpec((per_clip, *array_shape[1:]), lambda c, ids: (c, 0, 0))
+
+    chunk = 512
     act, dx1, dattn, grad_dense = pl.pallas_call(
-        functools.partial(dense_kernel, per_clip=per_clip, chunk=512, pieces=len(dy)),
+        functools.partial(dense_kernel, per_clip=per_clip, chunk=chunk, pieces=len(dy)),
         grid_spec=pltpu.PrefetchScalarGridSpec(
             num_scalar_prefetch=1,
-            grid=(items,),
+            grid=(clips,),
             in_specs=[
-                item((rows, feats)),
-                item((rows, feats)),
+                clip(x.shape),
+                clip(x.shape),
                 whole(gain2.shape),
                 whole(proj_bias.shape),
                 whole(fc1_bias.shape),
                 whole(fc2_bias.shape),
                 pl.BlockSpec(memory_space=pl.ANY),
                 *[tile(n) for n in range(6)],
-                *[piece(a) for a in dy],
+                *[clip(a.shape) for a in dy],
             ],
             out_specs=[
-                item((rows, feats)),
-                item((rows, feats)),
-                item((rows, feats)),
-                pl.BlockSpec((1, rank, span), lambda i, ids: (i // per_clip, 0, 0)),
+                clip(x.shape),
+                clip(x.shape),
+                clip(x.shape),
+                pl.BlockSpec((1, rank, span), lambda c, ids: (c, 0, 0)),
             ],
             scratch_shapes=[
                 pltpu.VMEM((8, feats // 8, feats), BF),
                 pltpu.VMEM((8, feats // 8, hidden), BF),
                 pltpu.VMEM((8, hidden // 8, feats), BF),
                 *[pltpu.VMEM((rank, n), BF) for n in (feats, feats, feats, hidden, hidden, feats)],
+                pltpu.VMEM((2, per_clip * rows, chunk), F32),
+                pltpu.VMEM((per_clip * rows, hidden), BF),
+                pltpu.VMEM((per_clip * rows, hidden), BF),
                 pltpu.SemaphoreType.DMA((24,)),
             ],
         ),
@@ -517,7 +558,7 @@
                 pl.BlockSpec((1, per_group, rows, rows), lambda i, g, ids: (i, g, 0, 0)),
                 item((rows, feats)),
                 item((rows, 3 * feats)),
-                item((rows, rank)),
+                item((rank, rows)),
                 item((rows, feats)),
                 item((rows, feats)),
             ],
@@ -530,7 +571,7 @@
                 pltpu.VMEM((feats, rows), BF),
                 pltpu.VMEM((rows, feats), BF),
                 pltpu.VMEM((rows, 3 * feats), BF),
-                pltpu.VMEM((feats, rows), F32),
+                pltpu.VMEM((feats, rows), BF),
             ],
         ),
         out_shape=[
@@ -1043,7 +1084,8 @@
         x, qkv_w, down, up, *vectors, ids, table = spread(
             tokens.reshape(flat), unit, pack_vectors(vecs, adapter_ids), pairs, clip_size
         )
-        dy = pieces_of(cotangent.reshape(flat))
+        later_dy, table = lax.optimization_barrier((cotangent, table))
+        dy = pieces_of(later_dy.reshape(flat))
         qkv_parts = (qkv_w, down, up)
     else:
         grid2, by_down, by_up = ("clip", "win"), ("win", None, "clip"), ("win", None, "clip")

time: 316 us -> 269 us (0.85)
  Pallas kernels: 271 us -> 216 us
  local copies, waits for them, and re-layouts: 20.3 us -> 24.7 us
  waiting for transfers between devices: 0.05 us -> 3.26 us
    pallas_call x1, Pallas kernels: 81.1 us -> 48.7 us  [spread(): pl.pallas_call(functools.partial(spread_kernel, clip_size=clip_size), in_...]
    pallas_call x1, Pallas kernels: 58.2 us -> 41.4 us  [compute(): pl.pallas_call(functools.partial(dense_kernel, per_clip=per_clip, chunk=c...]
    concatenate x1, local copies, waits for them, and re-layouts: 0.09 us -> 4.08 us  [pack_vectors(): flat = jnp.concatenate([v.astype(F32) for v in vecs] + [ids.astype(F32)])]
    pallas_call x1, Pallas kernels: 41.2 us -> 37.6 us  [compute(): pl.pallas_call(functools.partial(attend_kernel, scale=scale, per_group=pe...]
    ppermute x2, waiting for transfers between devices: 0.01 us -> 3.23 us  [pieces_of(): lax.ppermute(top, 'win', [(i, i ^ 3) for i in range(4)])]
    unnamed x68 -> x50, local copies, waits for them, and re-layouts: 14.6 us -> 14.5 us
  transfers between devices with their start and end apart: 7 -> 7, of which waited for: 0 -> 1; matrix products, arithmetic and copies ran while one was open for 2% -> 5% of each run, Pallas kernels for 54% -> 50%
where the time goes in v3:
time: 269 us; the launch traced here: 268 us
  Pallas kernels  216 us (80%)
  local copies, waits for them, and re-layouts  24.7 us (9%)
  between operations  14.3 us (5%)
  other arithmetic  5.65 us (2%)
  starting transfers between devices  4.45 us (2%)
  waiting for transfers between devices  3.26 us (1%)
    pallas_call x1, Pallas kernels, spread(): pl.pallas_call(functools.partial(spread_kernel, clip_size=clip_size), in_...  48.7 us
    pallas_call x1, Pallas kernels, compute(): pl.pallas_call(functools.partial(attend_back_kernel, scale=scale, per_gro...  47.3 us
    pallas_call x1, Pallas kernels, compute(): pl.pallas_call(functools.partial(dense_kernel, per_clip=per_clip, chunk=c...  41.4 us
    pallas_call x1, Pallas kernels, finish(): pl.pallas_call(functools.partial(finish_kernel, clip_size=clip_size), in_...  41.2 us
    pallas_call x1, Pallas kernels, compute(): pl.pallas_call(functools.partial(attend_kernel, scale=scale, per_group=pe...  37.6 us
    unnamed x50, local copies, waits for them, and re-layouts  14.5 us
  transfers between devices with their start and end apart: 7, of which 1 were waited for; matrix products, arithmetic and copies ran while one was open for 5% of the time, Pallas kernels for 50%

profile of v3, /device:TPU:0, one launch (start us, length us, event | category | flops | bytes accessed | tf_op | source)
XLA Modules:
  0.0 268.4 jit_solution(5081845745982665234)
XLA Ops:
  7.2 0.7 constant_dynamic-update-slice_fusion.8
  8.1 0.9 constant_dynamic-update-slice_fusion.6
  8.9 0.8 constant_dynamic-update-slice_fusion.5
  9.7 0.8 constant_dynamic-update-slice_fusion.4
  10.5 0.7 constant_dynamic-update-slice_fusion.3
  11.2 0.7 constant_dynamic-update-slice_fusion.2
  11.9 0.7 constant_dynamic-update-slice_fusion.1
  12.6 0.7 constant_dynamic-update-slice_fusion
  13.3 0.7 copy-done.5
  14.0 0.8 slice.32
  14.8 1.2 reshape.332
  16.1 0.7 convert_element_type.58
  16.8 0.7 pad.9.pairs_ref
  17.5 4.1 %concatenate.24 = f32[706]{0:T(1024)S(1)} concatenate(bf16[64]{0:T(256)(128)(2,1)} %param.25, bf16[192]{0:T(256)(128)(2,1)} %param.27, bf16[64]{0:T(256)(128)(2,1)} %param.29, bf16[64]{0:T(256)(128)(2,1)} %param.30, bf16[256]{0:T(256)(128)(2,1)} %param.32, bf16[64]{0:T(256)(128)(2,1)} %param.34, f32[2]{0:T(128)S(1)} %convert_element_type.58), dimensions={0} | concatenate | bytes 4240 | tf_op jit(solution)/shard_map/concatenate | solution.py:620
  22.1 1.5 fusion.3.unit_ref
  23.7 48.7 %spread.1 = (bf16[4,392,512]{2,1,0:T(8,128)(2,1)}, bf16[512,1536]{1,0:T(8,128)(2,1)}, bf16[8,16,512]{2,1,0:T(8,128)(2,1)}, bf16[8,16,1536]{2,1,0:T(8,128)(2,1)},...) custom-call(bf16[4,392,512]{2,1,0:T(8,128)(2,1)} %bitcast.67, ...), custom_call_target="tpu_custom_call" | custom-call | flops 30000001024 | bytes 20000000 | tf_op jit(solution)/shard_map/spread/pallas_call | solution.py:759
  72.4 1.5 collective-permute-start.1
  74.0 0.7 collective-permute-start
  75.5 0.9 fusion.1.key_mask_ref
  76.3 0.8 select_convert_fusion.query_mask_ref
  77.2 37.6 %attend.1 = (bf16[4,16,392,392]{3,2,1,0:T(8,128)(2,1)}, bf16[4,392,512]{2,1,0:T(8,128)(2,1)}, bf16[4,392,1536]{2,1,0:T(8,128)(2,1)}, bf16[4,16,392]{2,1,0:T(8,128)(2,1)}) custom-call(s32[4]{0:T(128)} %reshape.327.ids_ref, bf16[4,392,512]{2,1,0:T(8,128)(2,1)} %get-tuple-element.44.x_ref, f32[1,512]{1,0:T(1,128)} %get-tuple-element.45.gain_ref, ...), custom_call_target="tpu_custom_call" | custom-call | flops 40000000000 | bytes 10000000 | tf_op jit(solution)/shard_map/attend/pallas_call | solution.py:441
  114.8 3.2 %collective-permute-done.2.refs_9_ = bf16[4,208,512]{2,1,0:T(8,128)(2,1)} collective-permute-done((bf16[4,208,512]{2,1,0:T(8,128)(2,1)S(1)}, bf16[4,208,512]{2,1,0:T(8,128)(2,1)}, u32[]{:S(2)}, u32[]{:S(2)}) %collective-permute-start.2) | collective-permute-done | bytes 852000 | tf_op jit(solution)/shard_map/ppermute | solution.py:969
  118.0 41.4 %dense.1 = (bf16[4,392,512]{2,1,0:T(8,128)(2,1)}, f32[4,392,512]{2,1,0:T(8,128)}, bf16[4,392,512]{2,1,0:T(8,128)(2,1)}, f32[2,16,6144]{2,1,0:T(8,128)}) custom-call(s32[4]{0:T(128)} %reshape.327.ids_ref, bf16[4,392,512]{2,1,0:T(8,128)(2,1)} %get-tuple-element.44.x_ref, bf16[4,392,512]{2,1,0:T(8,128)(2,1)} %get-tuple-element.52.attn_ref, ...), custom_call_target="tpu_custom_call" | custom-call | flops 49999998976 | bytes 10000000 | tf_op jit(solution)/shard_map/dense/pallas_call | solution.py:497
  159.4 1.3 slice.31
  161.2 1.4 collective-permute-start.5
  162.9 47.3 %attend_back.1 = (bf16[4,392,512]{2,1,0:T(8,128)(2,1)}, f32[2,16,2048]{2,1,0:T(8,128)}) custom-call(s32[4]{0:T(128)} %reshape.327.ids_ref, bf16[4,392,512]{2,1,0:T(8,128)(2,1)} %get-tuple-element.44.x_ref, f32[1,512]{1,0:T(1,128)} %get-tuple-element.45.gain_ref, bf16[512,1536]{1,0:T(8,128)(2,1)} %get-tuple-element.46.weight_ref, ...), custom_call_target="tpu_custom_call" | custom-call | flops 49999998976 | bytes 10000000 | tf_op jit(solution)/shard_map/attend_back/pallas_call | solution.py:545
  210.3 1.1 copy-done.14
  211.5 41.2 %finish.1 = (bf16[4,392,512]{2,1,0:T(8,128)(2,1)}, bf16[4,392,512]{2,1,0:T(8,128)(2,1)}, f32[2,16,64]{2,1,0:T(8,128)}, f32[2,16,192]{2,1,0:T(8,128)}, f32[2,16,6...) custom-call(bf16[4,392,512]{2,1,0:T(8,128)(2,1)} %get-tuple-element., ...), custom_call_target="tpu_custom_call" | custom-call | flops 20000000000 | bytes 20000000 | tf_op jit(solution)/shard_map/finish/pallas_call | solution.py:918
  252.7 2.8 %copy.56 = bf16[2,2,392,512]{3,2,1,0:T(8,128)(2,1)} copy(bf16[2,2,392,512]{3,2,1,0:T(8,128)(2,1)} %bitcast.38) | data formatting | bytes 3211264
  255.5 1.2 copy.57
  257.3 0.6 copy.59
  259.8 0.6 copy.63
  (62 shorter events, 6.2 us)
Async XLA Ops:
  7.2 0.8 copy-start
  7.2 110.8 %all-gather.3.cloned.1.call-start = ((), (), s32[]{:S(2)}) async-start(), calls=%async_computation | async-start | bytes 6488064 | tf_op jit(solution)/shard_map/all_gather | solution.py:1077
  13.3 0.7 copy-start.5
  23.7 48.7 %copy-start.3 = (bf16[2,2,392,512]{3,2,1,0:T(8,128)(2,1)S(1)}, bf16[2,2,392,512]{3,2,1,0:T(8,128)(2,1)}, u32[]{:S(2)}) copy-start(bf16[2,2,392,512]{3,2,1,0:T(8,128)(2,1)} %param.23) | copy-start | bytes 4816900
  72.3 2.3 copy-start.16
  72.4 42.3 %collective-permute-start.1 = (bf16[4,208,512]{2,1,0:T(8,128)(2,1)S(1)}, bf16[4,208,512]{2,1,0:T(8,128)(2,1)S(1)}, u32[]{:S(2)}, u32[]{:S(2)}) collective-permute-start(bf16[4,208,512]{2,1,0:T(8,128)(2,1)S(1)} %slice.37), channel_id=1, source_target_pairs={{0,2},{1,3},{2,0},{3,1},{4,6},{5,7},{6,4},{7,5},{8,10},{9,11},{10,... | collective-permute-start | bytes 2555912 | tf_op jit(solution)/shard_map/ppermute | solution.py:968
  74.0 44.0 %collective-permute-start.2 = (bf16[4,208,512]{2,1,0:T(8,128)(2,1)S(1)}, bf16[4,208,512]{2,1,0:T(8,128)(2,1)}, u32[]{:S(2)}, u32[]{:S(2)}) collective-permute-start(bf16[4,208,512]{2,1,0:T(8,128)(2,1)S(1)} %slice.37), channel_id=1, source_target_pairs={{0,3},{1,2},{2,1},{3,0},{4,7},{5,6},{6,5},{7,4},{8,11},{9,10},{10,... | collective-permute-start | bytes 2555912 | tf_op jit(solution)/shard_map/ppermute | solution.py:969
  74.0 44.0 %collective-permute-start = (bf16[4,392,512]{2,1,0:T(8,128)(2,1)S(1)}, bf16[4,392,512]{2,1,0:T(8,128)(2,1)}, u32[]{:S(2)}, u32[]{:S(2)}) collective-permute-start(bf16[4,392,512]{2,1,0:T(8,128)(2,1)S(1)} %bitcast.43), channel_id=1, source_target_pairs={{0,1},{1,0},{2,3},{3,2},{4,5},{5,4},{6,7},{7,6},{8,9},{9,8},{10,11... | collective-permute-start | bytes 4816904 | tf_op jit(solution)/shard_map/ppermute | solution.py:967
  114.8 3.2 %copy-start.15 = (bf16[4,208,512]{2,1,0:T(8,128)(2,1)}, bf16[4,208,512]{2,1,0:T(8,128)(2,1)S(1)}, u32[]{:S(2)}) copy-start(bf16[4,208,512]{2,1,0:T(8,128)(2,1)S(1)} %collective-permute-done.1.refs_8_) | copy-start | bytes 2555908
  159.4 3.2 %copy-start.4 = (bf16[4,392,512]{2,1,0:T(8,128)(2,1)S(1)}, bf16[4,392,512]{2,1,0:T(8,128)(2,1)}, u32[]{:S(2)}) copy-start(bf16[4,392,512]{2,1,0:T(8,128)(2,1)} %get-tuple-element.58.act_ref) | copy-start | bytes 4816900
  160.7 49.6 %collective-permute-start.4 = (bf16[4,208,512]{2,1,0:T(8,128)(2,1)S(1)}, bf16[4,208,512]{2,1,0:T(8,128)(2,1)}, u32[]{:S(2)}, u32[]{:S(2)}) collective-permute-start(bf16[4,208,512]{2,1,0:T(8,128)(2,1)S(1)} %slice.31), channel_id=1, source_target_pairs={{0,2},{1,3},{2,0},{3,1},{4,6},{5,7},{6,4},{7,5},{8,10},{9,11},{10,... | collective-permute-start | bytes 2555912 | tf_op jit(solution)/shard_map/ppermute | solution.py:968
  161.2 49.1 %collective-permute-start.5 = (bf16[4,208,512]{2,1,0:T(8,128)(2,1)S(1)}, bf16[4,208,512]{2,1,0:T(8,128)(2,1)}, u32[]{:S(2)}, u32[]{:S(2)}) collective-permute-start(bf16[4,208,512]{2,1,0:T(8,128)(2,1)S(1)} %slice.31), channel_id=1, source_target_pairs={{0,3},{1,2},{2,1},{3,0},{4,7},{5,6},{6,5},{7,4},{8,11},{9,10},{10,... | collective-permute-start | bytes 2555912 | tf_op jit(solution)/shard_map/ppermute | solution.py:969
  162.6 47.7 %collective-permute-start.3 = (bf16[4,392,512]{2,1,0:T(8,128)(2,1)S(1)}, bf16[4,392,512]{2,1,0:T(8,128)(2,1)S(1)}, u32[]{:S(2)}, u32[]{:S(2)}) collective-permute-start(bf16[4,392,512]{2,1,0:T(8,128)(2,1)S(1)} %copy-done.4), channel_id=1, source_target_pairs={{0,1},{1,0},{2,3},{3,2},{4,5},{5,4},{6,7},{7,6},{8,9},{9,8},{10,11... | collective-permute-start | bytes 4816904 | tf_op jit(solution)/shard_map/ppermute | solution.py:967
  210.3 1.2 copy-start.14
  252.7 2.8 %copy-start.2 = (bf16[4,392,512]{2,1,0:T(8,128)(2,1)S(1)}, bf16[4,392,512]{2,1,0:T(8,128)(2,1)}, u32[]{:S(2)}) copy-start(bf16[4,392,512]{2,1,0:T(8,128)(2,1)} %get-tuple-element.69) | copy-start | bytes 4816900
  252.7 8.9 %copy-start.1 = (bf16[64,512]{1,0:T(8,128)(2,1)S(1)}, bf16[64,512]{1,0:T(8,128)(2,1)}, u32[]{:S(2)}) copy-start(bf16[64,512]{1,0:T(8,128)(2,1)} %param.31) | copy-start | bytes 196612
  255.5 1.2 copy-start.13
  255.5 1.8 copy-start.8
  255.5 2.4 copy-start.12
  255.5 3.0 %copy-start.11 = (f32[2,16,64]{2,1,0:T(8,128)S(1)}, f32[2,16,64]{2,1,0:T(8,128)}, u32[]{:S(2)}) copy-start(f32[2,16,64]{2,1,0:T(8,128)} %get-tuple-element.97) | copy-start | bytes 24580
  255.5 3.6 %copy-start.10 = (f32[2,16,64]{2,1,0:T(8,128)S(1)}, f32[2,16,64]{2,1,0:T(8,128)}, u32[]{:S(2)}) copy-start(f32[2,16,64]{2,1,0:T(8,128)} %get-tuple-element.74) | copy-start | bytes 24580
  255.5 4.2 %copy-start.7 = (f32[2,16,256]{2,1,0:T(8,128)S(1)}, f32[2,16,256]{2,1,0:T(8,128)}, u32[]{:S(2)}) copy-start(f32[2,16,256]{2,1,0:T(8,128)} %get-tuple-element.99) | copy-start | bytes 98308
  255.5 4.8 %copy-start.6 = (f32[2,16,256]{2,1,0:T(8,128)S(1)}, f32[2,16,256]{2,1,0:T(8,128)}, u32[]{:S(2)}) copy-start(f32[2,16,256]{2,1,0:T(8,128)} %get-tuple-element.76) | copy-start | bytes 98308
  255.5 5.5 %copy-start.9 = (f32[2,16,64]{2,1,0:T(8,128)S(1)}, f32[2,16,64]{2,1,0:T(8,128)}, u32[]{:S(2)}) copy-start(f32[2,16,64]{2,1,0:T(8,128)} %get-tuple-element.101) | copy-start | bytes 24580
Sparse Core Ops, SparseCore 0:
  14.1 89.1 all-gather.2

commit v4 on v3

--- a/solution.py
+++ b/solution.py
@@ -52,52 +52,306 @@
         ref[0, :, at] += value
 
 
+MESH = pl.DeviceIdType.MESH
+
+
+def enter(peers):
+    barrier = pltpu.get_barrier_semaphore()
+    for peer in peers:
+        pl.semaphore_signal(barrier, inc=1, device_id=peer, device_id_type=MESH)
+    pl.semaphore_wait(barrier, len(peers))
+
+
+def remote(src, dst, send_sem, recv_sem, peer):
+    return pltpu.make_async_remote_copy(
+        src_ref=src,
+        dst_ref=dst,
+        send_sem=send_sem,
+        recv_sem=recv_sem,
+        device_id=peer,
+        device_id_type=MESH,
+    )
+
+
+class Sender:
+    def __init__(self, send_sem, recv_sem):
+        self.send_sem, self.recv_sem, self.count = send_sem, recv_sem, 0
+
+    def copy(self, src, dst, peer):
+        n = self.count
+        self.count += 1
+        made = remote(src, dst, self.send_sem.at[n], self.recv_sem.at[n], peer)
+        made.start()
+        return made
+
+
+def row_masks(rows, columns):
+    row = lax.broadcasted_iota(jnp.int32, (rows, columns), 0)
+    return row < TOK // 2, row % 49 < 21, row % 7 < 3
+
+
+def with_top(part, top, early):
+    return jnp.concatenate([jnp.where(early[:TOP], top, part[:TOP]), part[TOP:]], axis=0)
+
+
+class Place:
+    def __init__(self, clip_size):
+        self.c, self.w = lax.axis_index("clip"), lax.axis_index("win")
+        self.z, self.y = self.c // 2, self.c % 2
+        self.x, self.k = self.w // 2, self.w % 2
+        self.zs = clip_size // 2
+        self.sibling = (self.c, self.x * 2 + 1 - self.k)
+        self.across = (self.c, (1 - self.x) * 2 + self.k)
+
+    def clip_at(self, z_step, other_y):
+        return (self.z + z_step + self.zs) % self.zs * 2 + (1 - self.y if other_y else self.y)
+
+    def along_z(self, step):
+        return (self.clip_at(step, False), self.w)
+
+    def along_y(self):
+        return (self.clip_at(0, True), self.w)
+
+
+class Gather:
+    COPIES = 29
+
+    def __init__(self, place, unit, units, send_sem, recv_sem):
+        self.place, self.unit, self.units = place, unit, units
+        self.send_sem, self.recv_sem = send_sem, recv_sem
+        self.hops = range(place.zs - 1)
+
+    def make(self, kind, t=0):
+        p, units = self.place, self.units
+        kinds = ("up", "down", "y_up", "y_down", "s_up", "s_down", "sy_up", "sy_down")
+        single = ("across", "own", "theirs", "y", "s_y")
+        n = single.index(kind) if kind in single else 5 + 8 * t + kinds.index(kind)
+        sems = self.send_sem.at[n], self.recv_sem.at[n]
+        mine = units.at[p.k, p.c, p.x]
+        if kind == "across":
+            return remote(self.unit, mine, *sems, p.across)
+        if kind == "own":
+            return remote(self.unit, mine, *sems, p.sibling)
+        if kind == "theirs":
+            part = units.at[p.k, p.c, 1 - p.x]
+        elif kind == "y":
+            part = units.at[p.k, p.c]
+        elif kind == "s_y":
+            part = units.at[p.k, p.z * 2 + 1 - p.y]
+        else:
+            sign = -1 if kind.endswith("up") else 1
+            far = p.z + sign * (t if kind in ("up", "down") else t + 1)
+            part = units.at[p.k, far * 2 + (1 - p.y if kind.startswith("sy") else p.y)]
+        if kind in ("up", "down"):
+            peer = (p.c - 2 * sign, p.w)
+        else:
+            peer = p.along_y() if kind.startswith("y") else p.sibling
+        return remote(part, part, *sems, peer)
+
+    def when(self, kind, t, sending, act):
+        p, last = self.place, self.place.zs - 1
+        if kind.endswith("up"):
+            holds = (p.z >= t) & (p.z < last) if sending and kind == "up" else p.z >= t + 1
+        elif kind.endswith("down"):
+            holds = (p.z <= last - t) & (p.z > 0) if sending and kind == "down" else p.z <= last - 1 - t
+        else:
+            act()
+            return
+        pl.when(holds)(act)
+
+    def start(self, kind, t=0):
+        self.when(kind, t, True, lambda: self.make(kind, t).start())
+
+    def wait_recv(self, kind, t=0):
+        self.when(kind, t, False, lambda: self.make(kind, t).wait_recv())
+
+    def wait_send(self, kind, t=0):
+        self.when(kind, t, True, lambda: self.make(kind, t).wait_send())
+
+    def begin(self):
+        self.start("across")
+        self.start("own")
+
+    def second(self):
+        self.wait_recv("across")
+        for kind in ("up", "down", "y", "theirs"):
+            self.start(kind)
+
+    def from_z(self, t):
+        for way in ("up", "down"):
+            self.wait_recv(way, t)
+            if t + 1 in self.hops:
+                self.start(way, t + 1)
+            self.start("y_" + way, t)
+            self.start("s_" + way, t)
+
+    def from_y(self, t):
+        if t < 0:
+            self.wait_recv("y")
+            self.start("s_y")
+        else:
+            for way in ("up", "down"):
+                self.wait_recv("y_" + way, t)
+                self.start("sy_" + way, t)
+
+    def finish(self):
+        for kind in ("own", "theirs", "s_y"):
+            self.wait_recv(kind)
+        for t in self.hops:
+            for kind in ("s_up", "s_down", "sy_up", "sy_down"):
+                self.wait_recv(kind, t)
+        for kind in ("across", "own", "theirs", "y", "s_y"):
+            self.wait_send(kind)
+        for t in self.hops:
+            for kind in ("up", "down", "y_up", "y_down", "s_up", "s_down", "sy_up", "sy_down"):
+                self.wait_send(kind, t)
+
+
 def attend_kernel(
-    ids_ref,
     x_ref,
     gain_ref,
     weight_ref,
     bias_ref,
+    ids_ref,
     down_ref,
     up_ref,
-    key_mask_ref,
-    query_mask_ref,
     table_ref,
-    probs_ref,
-    out_ref,
-    qkv_ref,
-    reduced_ref,
-    keys,
-    queries,
-    values_t,
-    out_t,
-    scores,
-    table,
-    table_sem,
-    *,
+    *refs,
     scale,
     per_group,
     width,
+    per_clip,
+    remote_size,
 ):
+    if remote_size:
+        (dy_ref, proj_ref, fc1_ref, fc2_ref, pd_ref, pu_ref, f1d_ref, f1u_ref, f2d_ref, f2u_ref, *refs) = refs
+    probs_ref, out_ref, qkv_ref, reduced_ref, down_own, up_own, *refs = refs
+    if remote_size:
+        dy_out_ref, units_ref, *refs = refs
+    keys, queries, values_t, out_t, scores, table, table_sem, query_mask, *refs = refs
     group = pl.program_id(1)
     groups = pl.num_programs(1)
+    item = pl.program_id(0)
+    step = item * groups + group
     feats = x_ref.shape[-1]
-    starting = pl.program_id(0) == 0
+    rows = x_ref.shape[1]
+    starting = item == 0
 
     def table_copy(g):
         at = pl.ds(g * per_group, per_group)
         return pltpu.make_async_copy(table_ref.at[at], table.at[at], table_sem.at[g])
 
-    @pl.when(starting & (group == 0))
+    @pl.when(step == 0)
     def _():
         for g in range(table.shape[0] // per_group):
             table_copy(g).start()
 
+    if remote_size:
+        unit, beside, mixed, tops, send_sem, recv_sem, dy_send, dy_recv, own_sem = refs
+        place = Place(remote_size)
+        gather_units = Gather(place, unit, units_ref, send_sem, recv_sem)
+        items = dy_ref.shape[0]
+
+        def dy_copy(kind, i):
+            n = kind * items + i
+            sems = dy_send.at[n], dy_recv.at[n]
+            if kind == 0:
+                return remote(dy_ref.at[i], beside.at[i], *sems, place.sibling)
+            return remote(mixed.at[i, pl.ds(0, TOP)], tops.at[i], *sems, place.across)
+
+        @pl.when(step == 0)
+        def _():
+            unit[0:64] = proj_ref[...]
+            for t in range(4):
+                unit[64 + 64 * t : 128 + 64 * t] = fc1_ref[:, 128 * t : 128 * t + 128]
+            unit[320:576] = fc2_ref[...]
+            for a in range(2):
+                at = 576 + 16 * a
+                unit[at : at + 16, 0:64] = pd_ref[a]
+                unit[at : at + 16, 64:128] = pu_ref[a]
+                unit[at + 32 : at + 48, 0:64] = f1d_ref[a]
+                unit[at + 32 : at + 48, 64:128] = f2u_ref[a]
+                for half in range(2):
+                    lanes = slice(128 * half, 128 * half + 128)
+                    unit[at + 64 + 32 * half : at + 80 + 32 * half] = f1u_ref[a, :, lanes]
+                    unit[at + 128 + 32 * half : at + 144 + 32 * half] = f2d_ref[a, :, lanes]
+            own = pltpu.make_async_copy(unit, units_ref.at[place.k, place.c, place.x], own_sem)
+            own.start()
+            enter(
+                [place.sibling, place.across, place.along_y()]
+                + [place.along_z(j) for j in range(1, place.zs)]
+            )
+            gather_units.begin()
+            for i in range(items):
+                dy_copy(0, i).start()
+            own.wait()
+
+        @pl.when(step == 1)
+        def _():
+            gather_units.second()
+
+        @pl.when(step == 2)
+        def _():
+            low_h = row_masks(rows, feats)[1]
+            for i in range(items):
+                dy_copy(0, i).wait_recv()
+                mixed[i] = jnp.where(low_h, beside[i], dy_ref[i])
+                dy_copy(1, i).start()
+
+        for t, at in enumerate((4, 8, 11)):
+
+            @pl.when(step == at)
+            def _():
+                gather_units.from_z(t)
+
+        for t, at in ((-1, 5), (0, 9), (1, 12), (2, 15)):
+
+            @pl.when(step == at)
+            def _():
+                gather_units.from_y(t)
+
+        @pl.when(step == 4 * items - 1)
+        def _():
+            early, _, low_w = row_masks(rows, feats)
+            for i in range(0, items, 2):
+                both = []
+                for e in range(2):
+                    dy_copy(1, i + e).wait_recv()
+                    both.append(with_top(mixed[i + e], tops[i + e], early))
+                for e in range(2):
+                    dy_out_ref[i + e] = jnp.where(low_w, both[1 - e], both[e])
+            gather_units.finish()
+            for i in range(items):
+                dy_copy(0, i).wait_send()
+                dy_copy(1, i).wait_send()
+
+    @pl.when((group == 0) & (item % per_clip == 0))
+    def _():
+        clip = item // per_clip
+        for ref, target in ((down_ref, down_own), (up_ref, up_own)):
+            total = jnp.zeros(ref.shape[1:], F32)
+            for a in range(ref.shape[0]):
+                total = total + jnp.where(
+                    ids_ref[pl.ds(clip, 1), 0:1] == float(a), ref[a].astype(F32), 0.0
+                )
+            target[0] = total.astype(BF)
+
     @pl.when(group == 0)
     def _():
+        number = lax.axis_index("win") * per_clip + item % per_clip
+        early, low_h, low_w = row_masks(rows, 128)
+        label = (
+            jnp.where(early, number // 4 % 2 * 4, 0)
+            + jnp.where(low_h, number // 2 % 2 * 2, 0)
+            + jnp.where(low_w, number % 2, 0)
+        )
+        lane = lane_ids((rows, 128))
+        same = label == lane
+        key_mask = jnp.where(same, 1.0, 0.0).astype(BF)
+        query_mask[...] = jnp.where(same | (lane >= 8), 0.0, -FAR).astype(BF)
         normed, _ = norm_stats(x_ref[0].astype(F32))
         low = (normed * gain_ref[...]).astype(BF)
-        reduced = dot(down_ref[0], low, NT).astype(BF)
+        reduced = dot(down_own[0], low, NT).astype(BF)
         reduced_ref[0] = reduced
 
         def columns(part):
@@ -105,7 +359,7 @@
             return (
                 dot(low, weight_ref[:, at], NN)
                 + bias_ref[:, at]
-                + dot(reduced, up_ref[0, :, at], TN)
+                + dot(reduced, up_own[0, :, at], TN)
             )
 
         query = (columns(0) * (scale * LOG2E)).astype(BF)
@@ -115,9 +369,8 @@
         qkv_ref[0, :, feats : 2 * feats] = key
         for g in range(feats // 128):
             keys[:, 256 * g : 256 * g + 128] = key[:, 128 * g : 128 * g + 128]
-            keys[:, 256 * g + 128 : 256 * g + 256] = key_mask_ref[0]
-        value = columns(2)
-        value = value.astype(BF)
+            keys[:, 256 * g + 128 : 256 * g + 256] = key_mask
+        value = columns(2).astype(BF)
         qkv_ref[0, :, 2 * feats :] = value
         values_t[...] = value.T
 
@@ -131,7 +384,7 @@
 
     def raw(h):
         own = jnp.where(head_of_lane == h, query_now, jnp.zeros_like(query_now))
-        own = jnp.concatenate([own, query_mask_ref[0]], axis=1)
+        own = jnp.concatenate([own, query_mask[...]], axis=1)
         return dot(keys_now, own, NT) + table[group * per_group + h]
 
     def finish(h):
@@ -155,26 +408,6 @@
         out_ref[0] = out_t[...].T
 
 
-def row_masks(rows, columns):
-    row = lax.broadcasted_iota(jnp.int32, (rows, columns), 0)
-    return row < TOK // 2, row % 49 < 21, row % 7 < 3
-
-
-def with_top(part, top, early):
-    return jnp.concatenate([jnp.where(early[:TOP], top, part[:TOP]), part[TOP:]], axis=0)
-
-
-def join_pieces(refs, e):
-    own, beside, across, far = refs
-    early, low_h, low_w = row_masks(own.shape[1], own.shape[2])
-
-    def window(n):
-        part = jnp.where(low_h, beside[n], own[n])
-        return with_top(part, jnp.where(low_h[:TOP], far[n], across[n]), early)
-
-    return jnp.where(low_w, window(1 - e), window(e))
-
-
 def dense_kernel(
     ids_ref,
     x_ref,
@@ -183,14 +416,13 @@
     proj_bias_ref,
     fc1_bias_ref,
     fc2_bias_ref,
+    dy_ref,
     staged_ref,
     *refs,
     per_clip,
     chunk,
-    pieces,
 ):
     tiles, refs = refs[:6], refs[6:]
-    dy_refs, refs = refs[:pieces], refs[pieces:]
     act_ref, dx1_ref, dattn_ref, grad_ref, *refs = refs
     proj_ref, fc1_ref, fc2_ref, proj_down, proj_up, fc1_down, fc1_up, fc2_down, fc2_up, *refs = refs
     pres, acts, dpres, sem = refs
@@ -205,7 +437,7 @@
         found += [(320, 256, fc2_ref, 128 * n, n) for n in range(4)]
         return [
             pltpu.make_async_copy(
-                staged_ref.at[:, n, pl.ds(start, size), :],
+                staged_ref.at[n % 2, :, n // 2, pl.ds(start, size), :],
                 target.at[:, :, pl.ds(lane, 128)],
                 sem.at[at],
             )
@@ -226,22 +458,19 @@
 
     for n in range(8):
         short = slice(64 * n, 64 * n + 64)
-        proj_down[:, short] = tiles[0][n, 0, :, 0:64]
-        proj_up[:, short] = tiles[0][n, 0, :, 64:128]
-        fc1_down[:, short] = tiles[1][n, 0, :, 0:64]
-        fc2_up[:, short] = tiles[1][n, 0, :, 64:128]
+        proj_down[:, short] = tiles[0][0, n, 0, :, 0:64]
+        proj_up[:, short] = tiles[0][0, n, 0, :, 64:128]
+        fc1_down[:, short] = tiles[1][0, n, 0, :, 0:64]
+        fc2_up[:, short] = tiles[1][0, n, 0, :, 64:128]
         for half in range(2):
             long = slice(256 * n + 128 * half, 256 * n + 128 * half + 128)
-            fc1_up[:, long] = tiles[2 + half][n, 0]
-            fc2_down[:, long] = tiles[4 + half][n, 0]
+            fc1_up[:, long] = tiles[2 + half][0, n, 0]
+            fc2_down[:, long] = tiles[4 + half][0, n, 0]
 
     def join(parts):
         return jnp.concatenate(parts, axis=0) if per_clip > 1 else parts[0]
 
-    if pieces == 1:
-        dy = join([dy_refs[0][e] for e in range(per_clip)])
-    else:
-        dy = join([join_pieces(dy_refs, e) for e in range(per_clip)])
+    dy = join([dy_ref[e] for e in range(per_clip)])
     attn = join([attn_ref[e] for e in range(per_clip)])
     reduced_proj = dot(proj_down[...], attn, NT).astype(BF)
     arrive(0, 4)
@@ -292,10 +521,9 @@
     fc1_up_at = 3 * feats
     fc2_down_at = fc1_up_at + hidden
     fc2_up_at = fc2_down_at + hidden
-    fc1_w = fc1_ref[...].reshape(feats, hidden)
     fc2_w = fc2_ref[...].reshape(hidden, feats)
     grad_reduced_fc1 = dot(fc1_up[...], dpre, NT).astype(BF)
-    dlow = dot(dpre, fc1_w, NT) + dot(grad_reduced_fc1, fc1_down[...], TN)
+    dlow = dot(dpre, fc1_ref[...].reshape(feats, hidden), NT) + dot(grad_reduced_fc1, fc1_down[...], TN)
     dx1 = dy.astype(F32) + norm_back(dlow, gain_ref[...], normed, inverse)
     branch = dx1.astype(BF)
     reduced_fc2 = dot(fc2_down[...], act, NT).astype(BF)
@@ -320,7 +548,6 @@
 
 
 def attend_back_kernel(
-    ids_ref,
     x_ref,
     gain_ref,
     weight_ref,
@@ -418,7 +645,7 @@
     return pl.BlockSpec(shape, lambda *at: (0,) * len(shape), pipeline_mode=pl.Buffered(1))
 
 
-def compute(x, dy, item_ids, vectors, qkv_parts, staged, masks, table, per_clip):
+def compute(x, dy, adapter_ids, vectors, qkv_parts, later, table, per_clip, remote_size):
     items, rows, feats = x.shape
     heads = table.shape[0]
     width = feats // heads
@@ -427,7 +654,6 @@
     scale = width**-0.5
     gain1, qkv_bias, proj_bias, gain2, fc1_bias, fc2_bias = vectors
     qkv_w, qkv_down, qkv_up = qkv_parts
-    key_mask, query_mask = masks
     rank = qkv_down.shape[1]
     hidden = fc1_bias.shape[1]
     clips = items // per_clip
@@ -435,67 +661,109 @@
     def item(shape):
         return pl.BlockSpec((1, *shape), lambda i, *rest: (i,) + (0,) * len(shape))
 
-    def adapter(array):
-        return pl.BlockSpec((1, *array.shape[1:]), lambda i, *rest: (rest[-1][i], 0, 0))
-
-    probs, attn, qkv, reduced = pl.pallas_call(
-        functools.partial(attend_kernel, scale=scale, per_group=per_group, width=width),
-        grid_spec=pltpu.PrefetchScalarGridSpec(
-            num_scalar_prefetch=1,
-            grid=(items, groups),
-            in_specs=[
-                item((rows, feats)),
-                whole(gain1.shape),
-                whole(qkv_w.shape),
-                whole(qkv_bias.shape),
-                adapter(qkv_down),
-                adapter(qkv_up),
-                pl.BlockSpec((1, rows, 128), lambda i, g, ids: (i % per_clip, 0, 0)),
-                pl.BlockSpec((1, rows, 128), lambda i, g, ids: (i % per_clip, 0, 0)),
-                pl.BlockSpec(memory_space=pl.ANY),
-            ],
-            out_specs=[
-                pl.BlockSpec((1, per_group, rows, rows), lambda i, g, ids: (i, g, 0, 0)),
-                item((rows, feats)),
-                item((rows, 3 * feats)),
-                item((rank, rows)),
-            ],
-            scratch_shapes=[
-                pltpu.VMEM((rows, 2 * feats), BF),
-                pltpu.VMEM((rows, feats), BF),
-                pltpu.VMEM((feats, rows), BF),
-                pltpu.VMEM((feats, rows), BF),
-                pltpu.VMEM((2, rows, rows), F32),
-                pltpu.VMEM(table.shape, F32),
-                pltpu.SemaphoreType.DMA((groups,)),
-            ],
+    clip_ids = jnp.broadcast_to(adapter_ids.astype(F32)[:, None], (clips, 128))
+    item_ids = adapter_ids
+    any_space = pl.BlockSpec(memory_space=pl.ANY)
+
+    def of_clip(shape):
+        return pl.BlockSpec((1, *shape), lambda i, *rest: (i // per_clip, 0, 0))
+
+    if remote_size:
+        unit_shape = (768, 128)
+        sent = (dy, *later)
+        sent_out = [
+            jax.ShapeDtypeStruct(dy.shape, BF),
+            jax.ShapeDtypeStruct((2, remote_size, 2, *unit_shape), BF),
+        ]
+        sent_scratch = [
+            pltpu.VMEM(unit_shape, BF),
+            pltpu.VMEM(dy.shape, BF),
+            pltpu.VMEM(dy.shape, BF),
+            pltpu.VMEM((items, TOP, feats), BF),
+            pltpu.SemaphoreType.DMA((Gather.COPIES,)),
+            pltpu.SemaphoreType.DMA((Gather.COPIES,)),
+            pltpu.SemaphoreType.DMA((2 * items,)),
+            pltpu.SemaphoreType.DMA((2 * items,)),
+            pltpu.SemaphoreType.DMA,
+        ]
+    else:
+        sent, sent_out, sent_scratch = (), [], []
+    probs, attn, qkv, reduced, down_own, up_own, *arrived = pl.pallas_call(
+        functools.partial(
+            attend_kernel,
+            scale=scale,
+            per_group=per_group,
+            width=width,
+            per_clip=per_clip,
+            remote_size=remote_size,
         ),
+        grid=(items, groups),
+        in_specs=[
+            item((rows, feats)),
+            whole(gain1.shape),
+            whole(qkv_w.shape),
+            whole(qkv_bias.shape),
+            whole(clip_ids.shape),
+            whole(qkv_down.shape),
+            whole(qkv_up.shape),
+            any_space,
+            *[whole(a.shape) for a in sent],
+        ],
+        out_specs=[
+            pl.BlockSpec((1, per_group, rows, rows), lambda i, g: (i, g, 0, 0)),
+            item((rows, feats)),
+            item((rows, 3 * feats)),
+            item((rank, rows)),
+            of_clip((rank, feats)),
+            of_clip((rank, 3 * feats)),
+            *([whole(dy.shape), any_space] if remote_size else []),
+        ],
+        scratch_shapes=[
+            pltpu.VMEM((rows, 2 * feats), BF),
+            pltpu.VMEM((rows, feats), BF),
+            pltpu.VMEM((feats, rows), BF),
+            pltpu.VMEM((feats, rows), BF),
+            pltpu.VMEM((2, rows, rows), F32),
+            pltpu.VMEM(table.shape, F32),
+            pltpu.SemaphoreType.DMA((groups,)),
+            pltpu.VMEM((rows, 128), BF),
+            *sent_scratch,
+        ],
         out_shape=[
             jax.ShapeDtypeStruct((items, heads, rows, rows), BF),
             jax.ShapeDtypeStruct((items, rows, feats), BF),
             jax.ShapeDtypeStruct((items, rows, 3 * feats), BF),
             jax.ShapeDtypeStruct((items, rank, rows), BF),
+            jax.ShapeDtypeStruct((clips, rank, feats), BF),
+            jax.ShapeDtypeStruct((clips, rank, 3 * feats), BF),
+            *sent_out,
         ],
         compiler_params=pltpu.CompilerParams(
-            vmem_limit_bytes=VMEM_LIMIT, dimension_semantics=("arbitrary", "arbitrary")
+            vmem_limit_bytes=VMEM_LIMIT,
+            dimension_semantics=("arbitrary", "arbitrary"),
+            **({"collective_id": 2, "has_side_effects": True} if remote_size else {}),
         ),
         cost_estimate=pl.CostEstimate(flops=4 * 10**10, bytes_accessed=10**7, transcendentals=0),
         name="attend",
-    )(item_ids, x, gain1, qkv_w, qkv_bias, qkv_down, qkv_up, key_mask, query_mask, table)
+    )(x, gain1, qkv_w, qkv_bias, clip_ids, qkv_down, qkv_up, table, *sent)
+    if remote_size:
+        dy, staged = arrived
+    else:
+        (staged,) = later
 
     span = 4 * feats + 2 * hidden
     def tile(n):
-        return pl.BlockSpec(
-            (8, 1, rank, 128),
-            lambda c, ids: (0, ids[c * per_clip] // 2, 36 + 2 * n + ids[c * per_clip] % 2, 0),
-        )
+        def index(c, ids):
+            return ids[c] // 2 % 2, 0, ids[c] // 4, 36 + 2 * n + ids[c] % 2, 0
+
+        return pl.BlockSpec((1, 8, 1, rank, 128), index)
 
     def clip(array_shape):
         return pl.BlockSpec((per_clip, *array_shape[1:]), lambda c, ids: (c, 0, 0))
 
     chunk = 512
     act, dx1, dattn, grad_dense = pl.pallas_call(
-        functools.partial(dense_kernel, per_clip=per_clip, chunk=chunk, pieces=len(dy)),
+        functools.partial(dense_kernel, per_clip=per_clip, chunk=chunk),
         grid_spec=pltpu.PrefetchScalarGridSpec(
             num_scalar_prefetch=1,
             grid=(clips,),
@@ -506,9 +774,9 @@
                 whole(proj_bias.shape),
                 whole(fc1_bias.shape),
                 whole(fc2_bias.shape),
-                pl.BlockSpec(memory_space=pl.ANY),
+                clip(x.shape),
+                any_space,
                 *[tile(n) for n in range(6)],
-                *[clip(a.shape) for a in dy],
             ],
             out_specs=[
                 clip(x.shape),
@@ -539,41 +807,38 @@
         cost_estimate=pl.CostEstimate(flops=5 * 10**10, bytes_accessed=10**7, transcendentals=0),
         name="dense",
     )(
-        item_ids, x, attn, gain2, proj_bias, fc1_bias, fc2_bias, staged, *([staged] * 6), *dy
+        item_ids, x, attn, gain2, proj_bias, fc1_bias, fc2_bias, dy, staged, *([staged] * 6)
     )
 
     dx, grad_qkv = pl.pallas_call(
         functools.partial(
             attend_back_kernel, scale=scale, per_group=per_group, width=width, per_clip=per_clip
         ),
-        grid_spec=pltpu.PrefetchScalarGridSpec(
-            num_scalar_prefetch=1,
-            grid=(items, groups),
-            in_specs=[
-                item((rows, feats)),
-                whole(gain1.shape),
-                whole(qkv_w.shape),
-                adapter(qkv_down),
-                adapter(qkv_up),
-                pl.BlockSpec((1, per_group, rows, rows), lambda i, g, ids: (i, g, 0, 0)),
-                item((rows, feats)),
-                item((rows, 3 * feats)),
-                item((rank, rows)),
-                item((rows, feats)),
-                item((rows, feats)),
-            ],
-            out_specs=[
-                item((rows, feats)),
-                pl.BlockSpec((1, rank, 4 * feats), lambda i, g, ids: (i // per_clip, 0, 0)),
-            ],
-            scratch_shapes=[
-                pltpu.VMEM((rows, 2 * feats), BF),
-                pltpu.VMEM((feats, rows), BF),
-                pltpu.VMEM((rows, feats), BF),
-                pltpu.VMEM((rows, 3 * feats), BF),
-                pltpu.VMEM((feats, rows), BF),
-            ],
-        ),
+        grid=(items, groups),
+        in_specs=[
+            item((rows, feats)),
+            whole(gain1.shape),
+            whole(qkv_w.shape),
+            of_clip((rank, feats)),
+            of_clip((rank, 3 * feats)),
+            pl.BlockSpec((1, per_group, rows, rows), lambda i, g: (i, g, 0, 0)),
+            item((rows, feats)),
+            item((rows, 3 * feats)),
+            item((rank, rows)),
+            item((rows, feats)),
+            item((rows, feats)),
+        ],
+        out_specs=[
+            item((rows, feats)),
+            pl.BlockSpec((1, rank, 4 * feats), lambda i, g: (i // per_clip, 0, 0)),
+        ],
+        scratch_shapes=[
+            pltpu.VMEM((rows, 2 * feats), BF),
+            pltpu.VMEM((feats, rows), BF),
+            pltpu.VMEM((rows, feats), BF),
+            pltpu.VMEM((rows, 3 * feats), BF),
+            pltpu.VMEM((feats, rows), BF),
+        ],
         out_shape=[
             jax.ShapeDtypeStruct((items, rows, feats), BF),
             jax.ShapeDtypeStruct((clips, rank, 4 * feats), F32),
@@ -583,77 +848,50 @@
         ),
         cost_estimate=pl.CostEstimate(flops=5 * 10**10, bytes_accessed=10**7, transcendentals=0),
         name="attend_back",
-    )(item_ids, x, gain1, qkv_w, qkv_down, qkv_up, probs, attn, qkv, reduced, dattn, dx1)
+    )(x, gain1, qkv_w, down_own, up_own, probs, attn, qkv, reduced, dattn, dx1)
     return act, dx, grad_qkv, grad_dense
 
 
-MESH = pl.DeviceIdType.MESH
-
-
-def enter(peers):
-    barrier = pltpu.get_barrier_semaphore()
-    for peer in peers:
-        pl.semaphore_signal(barrier, inc=1, device_id=peer, device_id_type=MESH)
-    pl.semaphore_wait(barrier, len(peers))
-
-
-class Sender:
-    def __init__(self, send_sem, recv_sem):
-        self.send_sem, self.recv_sem, self.count = send_sem, recv_sem, 0
-
-    def copy(self, src, dst, peer):
-        n = self.count
-        self.count += 1
-        made = pltpu.make_async_remote_copy(
-            src_ref=src,
-            dst_ref=dst,
-            send_sem=self.send_sem.at[n],
-            recv_sem=self.recv_sem.at[n],
-            device_id=peer,
-            device_id_type=MESH,
-        )
-        made.start()
-        return made
-
-
-def pack_vectors(vecs, ids):
-    flat = jnp.concatenate([v.astype(F32) for v in vecs] + [ids.astype(F32)])
-    return jnp.pad(flat, (0, 1024 - flat.shape[0])).reshape(8, 128)
-
-
 def spread_kernel(
-    tok_ref, unit_ref, vec_ref, pairs_ref,
+    tok_ref, table_in_ref, qkv_ref, qd_ref, qu_ref, ids_in_ref,
+    g1_ref, qb_ref, pb_ref, g2_ref, f1b_ref, f2b_ref,
     x_ref, weight_ref, down_ref, up_ref, gain1_ref, qkv_bias_ref, proj_bias_ref, gain2_ref, fc1_bias_ref,
     fc2_bias_ref, ids_ref, table_ref,
-    units, vecs, beside, mixed, tops, found, wide, select, bias, send_sem, recv_sem, out_sem,
+    unit_ref, vec_ref, pairs_ref,
+    units, vecs, beside, mixed, tops, found, wide, select, bias,
+    send_sem, recv_sem, unit_send, unit_recv, out_sem,
     *, clip_size,
 ):
-    c, w = lax.axis_index("clip"), lax.axis_index("win")
-    z, y = c // 2, c % 2
-    x, k = w // 2, w % 2
-    sibling = (c, x * 2 + 1 - k)
-    across = (c, (1 - x) * 2 + k)
-    zs = clip_size // 2
-
-    def at(z_step, other_y):
-        return (z + z_step + zs) % zs * 2 + (1 - y if other_y else y)
-
+    place = Place(clip_size)
+    c, w, x, k = place.c, place.w, place.x, place.k
+    sibling, across = place.sibling, place.across
+    gather_units = Gather(place, unit_ref, units, unit_send, unit_recv)
     items, rows, feats = tok_ref.shape
+    unit_ref[:, 0:384] = qkv_ref[...]
+    for a in range(2):
+        unit_ref[16 * a : 16 * a + 16, 384:448] = qd_ref[a]
+        unit_ref[16 * a : 16 * a + 16, 448:512] = qu_ref[a, :, 0:64]
+        unit_ref[32 + 16 * a : 48 + 16 * a, 384:512] = qu_ref[a, :, 64:192]
+    vec_ref[0:1, 0:64] = g1_ref[...].astype(F32)
+    vec_ref[0:1, 64:128] = qb_ref[:, 0:64].astype(F32)
+    vec_ref[1:2, :] = qb_ref[:, 64:192].astype(F32)
+    vec_ref[2:3, 0:64] = pb_ref[...].astype(F32)
+    vec_ref[2:3, 64:128] = g2_ref[...].astype(F32)
+    vec_ref[3:4, :] = f1b_ref[:, 0:128].astype(F32)
+    vec_ref[4:5, :] = f1b_ref[:, 128:256].astype(F32)
+    vec_ref[5:6, 0:64] = f2b_ref[...].astype(F32)
+    vec_ref[5:6, 64:128] = ids_in_ref[:, 0:64]
+    vec_ref[6:8, :] = jnp.zeros((2, 128), F32)
     enter([sibling, across] + [((c + d) % clip_size, w) for d in range(1, clip_size)])
     send = Sender(send_sem, recv_sem)
-    waits = []
     units[k, c, x] = unit_ref[...]
     vecs[c] = vec_ref[...]
-    to_across = send.copy(unit_ref, units.at[k, c, x], across)
+    gather_units.begin()
     tokens_beside = [send.copy(tok_ref.at[i], beside.at[i], sibling) for i in range(items)]
-    from_sibling = [send.copy(unit_ref, units.at[k, c, x], sibling)]
     vec_copies = [
         send.copy(vec_ref, vecs.at[c], ((c + d) % clip_size, w)) for d in range(1, clip_size)
     ]
-    to_across.wait_recv()
-    along_z = [send.copy(units.at[k, c], units.at[k, c], (at(j, False), w)) for j in range(1, zs)]
-    along_y = [send.copy(units.at[k, c], units.at[k, c], (at(0, True), w))]
-    from_sibling.append(send.copy(units.at[k, c, 1 - x], units.at[k, c, 1 - x], sibling))
+    gather_units.second()
     early, low_h, low_w = row_masks(rows, feats)
     token_tops = []
     for i in range(items):
@@ -662,6 +900,9 @@
         token_tops.append(send.copy(mixed.at[i, pl.ds(0, TOP)], tops.at[i], across))
 
     heads = pairs_ref.shape[0] // 15
+    pairs_ref[...] = jnp.zeros(pairs_ref.shape, BF)
+    for a in range(15):
+        pairs_ref[a * heads : (a + 1) * heads, 0:169] = table_in_ref[:, 169 * a : 169 * a + 169]
     off_lane = lane_ids((pairs_ref.shape[1], 128))
     off_row = lax.broadcasted_iota(jnp.int32, (pairs_ref.shape[1], 128), 0)
     query_at = (off_lane // 7 + 4) % 7 * 13 + (off_lane % 7 + 4) % 7
@@ -678,12 +919,7 @@
 
     lax.fori_loop(0, 49, one_key, 0)
 
-    from_z = []
-    for j in range(1, zs):
-        along_z[j - 1].wait_recv()
-        slot = at(-j, False)
-        along_y.append(send.copy(units.at[k, slot], units.at[k, slot], (at(0, True), w)))
-        from_sibling.append(send.copy(units.at[k, slot], units.at[k, slot], sibling))
+    gather_units.from_z(0)
 
     for a in range(15):
         wide[:, 128 * a : 128 * a + 128] = found[a].astype(BF)
@@ -694,11 +930,9 @@
             (sel_lane == sel_row + (t + 4) % 8 * 49) & (sel_row < 49), 1.0, 0.0
         ).astype(BF)
 
-    for j in range(zs):
-        along_y[j].wait_recv()
-        slot = at(-j, True)
-        from_sibling.append(send.copy(units.at[k, slot], units.at[k, slot], sibling))
-
+    gather_units.from_y(-1)
+    gather_units.from_z(1)
+    gather_units.from_y(0)
     for block in range(8):
         t = (block + 4) % 8
         value = dot(wide[:, (7 - t) * 128 : (15 - t) * 128], select[...], NN) * LOG2E
@@ -706,6 +940,8 @@
             bias[m, 49 * block : 49 * block + 49, :] = value[56 * m : 56 * m + 49]
     out = pltpu.make_async_copy(bias, table_ref, out_sem)
     out.start()
+    gather_units.from_z(2)
+    gather_units.from_y(1)
 
     for copy in vec_copies:
         copy.wait_recv()
@@ -724,8 +960,8 @@
                 v[5:6, 64 + n : 65 + n], (1, ids_ref.shape[1])
             )
 
-    for copy in from_sibling:
-        copy.wait_recv()
+    gather_units.from_y(2)
+    gather_units.finish()
     for c2 in range(clip_size):
         for x2 in range(2):
             for k2 in range(2):
@@ -746,19 +982,19 @@
         for e in range(2):
             x_ref[i + e] = jnp.where(low_w, both[1 - e], both[e])
 
-    for copy in [to_across, *tokens_beside, *from_sibling, *vec_copies, *along_z, *along_y, *token_tops]:
+    for copy in [*tokens_beside, *vec_copies, *token_tops]:
         copy.wait_send()
     out.wait()
 
 
-def spread(tokens, unit, vec, pairs, clip_size):
+def spread(tokens, table, qkv_w, qkv_down, qkv_up, ids, vecs, clip_size):
     items, rows, feats = tokens.shape
-    heads = pairs.shape[0] // 15
+    heads = table.shape[0]
     f = functools.partial(jax.ShapeDtypeStruct)
     vm = pl.BlockSpec(memory_space=pltpu.VMEM)
     return pl.pallas_call(
         functools.partial(spread_kernel, clip_size=clip_size),
-        in_specs=[vm] * 4,
+        in_specs=[vm] * 12,
         out_specs=[vm] * 11 + [pl.BlockSpec(memory_space=pl.ANY)],
         out_shape=[
             f((items, rows, feats), BF),
@@ -775,6 +1011,9 @@
             f((heads, rows, rows), F32),
         ],
         scratch_shapes=[
+            pltpu.VMEM((64, 512), BF),
+            pltpu.VMEM((8, 128), F32),
+            pltpu.VMEM((15 * heads, 176), BF),
             pltpu.VMEM((2, clip_size, 2, 64, 512), BF),
             pltpu.VMEM((clip_size, 8, 128), F32),
             pltpu.VMEM((items, rows, feats), BF),
@@ -784,8 +1023,10 @@
             pltpu.VMEM((56 * heads, 15 * 128), BF),
             pltpu.VMEM((8 * 128, rows), BF),
             pltpu.VMEM((heads, rows, rows), F32),
-            pltpu.SemaphoreType.DMA((32,)),
-            pltpu.SemaphoreType.DMA((32,)),
+            pltpu.SemaphoreType.DMA((16,)),
+            pltpu.SemaphoreType.DMA((16,)),
+            pltpu.SemaphoreType.DMA((Gather.COPIES,)),
+            pltpu.SemaphoreType.DMA((Gather.COPIES,)),
             pltpu.SemaphoreType.DMA,
         ],
         compiler_params=pltpu.CompilerParams(
@@ -793,7 +1034,7 @@
         ),
         cost_estimate=pl.CostEstimate(flops=3 * 10**10, bytes_accessed=2 * 10**7, transcendentals=0),
         name="spread",
-    )(tokens, unit, vec, pairs)
+    )(tokens, table, qkv_w, qkv_down, qkv_up, ids, *vecs)
 
 
 PIECES = (("q", 0, 64), ("q", 512, 192), ("d", 0, 64), ("d", 512, 64), ("d", 1024, 64), ("d", 5632, 64), ("d", 1536, 256), ("d", 3584, 256))
@@ -970,27 +1211,6 @@
     )
 
 
-def place():
-    at = jnp.arange(TOK)
-    return at // 49, at // 7 % 7, at % 7
-
-
-def window_masks(win_index, local):
-    depth, height, across = place()
-    number = win_index * local + jnp.arange(local)
-    label = (
-        number[:, None] // 4 % 2 * (depth < 4) * 4
-        + number[:, None] // 2 % 2 * (height < 3) * 2
-        + number[:, None] % 2 * (across < 3)
-    )
-    lane = jnp.arange(128)
-    same = label[:, :, None] == lane
-    return (
-        same.astype(BF),
-        jnp.where(same | (lane >= 8), 0.0, -FAR).astype(BF),
-    )
-
-
 def bias_by_pair(table):
     heads = table.shape[0]
     side = jnp.arange(49)
@@ -1044,6 +1264,10 @@
     )
 
 
+def by_core(staged):
+    return staged.reshape(8, 2, 2, *staged.shape[2:]).transpose(2, 0, 1, 3, 4)
+
+
 def per_device(
     tokens, cotangent, adapter_ids, ln1_gain, qkv_weight, qkv_bias, proj_weight, proj_bias, ln2_gain,
     fc1_weight, fc1_bias, fc2_weight, fc2_bias, bias_table, qkv_down, qkv_up, proj_down, proj_up,
@@ -1053,40 +1277,18 @@
     items = clips * local
     heads = bias_table.shape[0]
     vecs = (ln1_gain, qkv_bias, proj_bias, ln2_gain, fc1_bias, fc2_bias)
-    item_ids = jnp.repeat(adapter_ids, local)
-    masks = window_masks(lax.axis_index("win"), local)
     flat = (items, rows, feats)
     downs = [a.transpose(0, 2, 1) for a in (qkv_down, proj_down, fc1_down, fc2_down)]
     own_kernels = (clip_size, win_size, clips, local) == (8, 4, 2, 2)
     if own_kernels:
-        maps = [a.reshape(32, -1) for a in (downs[1], proj_up, downs[2], fc1_up, downs[3], fc2_up)]
-        later = jnp.concatenate(
-            (
-                proj_weight,
-                fc1_weight.reshape(64, 4, 128).transpose(1, 0, 2).reshape(256, 128),
-                fc2_weight,
-                jnp.concatenate((maps[0], maps[1]), axis=1),
-                jnp.concatenate((maps[2], maps[5]), axis=1),
-                maps[3][:, :128],
-                maps[3][:, 128:],
-                maps[4][:, :128],
-                maps[4][:, 128:],
-            ),
-            axis=0,
+        rows_of_ids = jnp.pad(adapter_ids.astype(F32)[None], ((0, 0), (0, 126)))
+        x, qkv_w, down, up, *vectors, ids, table = spread(
+            tokens.reshape(flat), bias_table, qkv_weight, downs[0], qkv_up, rows_of_ids,
+            [v.reshape(1, -1) for v in vecs], clip_size,
         )
-        staged = lax.all_gather(later, ("clip", "win")).reshape(8, 4, 768, 128)
-        early = jnp.concatenate((downs[0].reshape(32, 64), qkv_up.reshape(32, 192)), axis=1)
-        unit = jnp.concatenate(
-            (qkv_weight, jnp.concatenate((early[:, :128], early[:, 128:]), axis=0)), axis=1
-        )
-        pairs = bias_table.reshape(heads, 15, 169).transpose(1, 0, 2).reshape(15 * heads, 169)
-        pairs = jnp.pad(pairs, ((0, 0), (0, 7)))
-        x, qkv_w, down, up, *vectors, ids, table = spread(
-            tokens.reshape(flat), unit, pack_vectors(vecs, adapter_ids), pairs, clip_size
-        )
-        later_dy, table = lax.optimization_barrier((cotangent, table))
-        dy = pieces_of(later_dy.reshape(flat))
+        dy = cotangent.reshape(flat)
         qkv_parts = (qkv_w, down, up)
+        later = (proj_weight, fc1_weight, fc2_weight, downs[1], proj_up, downs[2], fc1_up, downs[3], fc2_up)
     else:
         grid2, by_down, by_up = ("clip", "win"), ("win", None, "clip"), ("win", None, "clip")
         qkv_parts = (gather(qkv_weight, grid2), gather(downs[0], by_down), gather(qkv_up, by_up))
@@ -1095,12 +1297,13 @@
             *[gather(a, grid2) for a in (proj_weight, fc1_weight, fc2_weight)],
             [gather(a, by_up) for a in maps],
         )
+        later = (by_core(staged),)
         vectors = [gather(v, ("clip",)).reshape(1, -1).astype(F32) for v in vecs]
         table = bias_by_pair(bias_table)
         x = exchange(tokens, win_size).reshape(flat)
-        dy = (exchange(cotangent, win_size).reshape(flat),)
+        dy = exchange(cotangent, win_size).reshape(flat)
     act, dx, grad_qkv, grad_dense = compute(
-        x, dy, item_ids, vectors, qkv_parts, staged, masks, table, local
+        x, dy, adapter_ids, vectors, qkv_parts, later, table, local, clip_size if own_kernels else 0
     )
     if own_kernels:
         act_out, dx_out, qd, qu, pd, pu, f1d, f1u, f2d, f2u = finish(

time: 269 us -> 246 us (0.914)
  between operations: 14.3 us -> 0.78 us
  Pallas kernels: 216 us -> 227 us
  local copies, waits for them, and re-layouts: 24.7 us -> 14.9 us
  other arithmetic: 5.65 us -> 0.66 us
  waiting for transfers between devices: 3.26 us -> 0.01 us
    pallas_call x1, Pallas kernels: 37.6 us -> 55.7 us  [compute(): pl.pallas_call(functools.partial(attend_kernel, scale=scale, per_group=pe...]
    pallas_call x1, Pallas kernels: 48.7 us -> 41.7 us  [spread(): pl.pallas_call(functools.partial(spread_kernel, clip_size=clip_size), in_...]
    concatenate x2 -> x0, local copies, waits for them, and re-layouts: 4.78 us -> none  [the longest x1 4.08 us: pack_vectors(): flat = jnp.concatenate([v.astype(F32) for v in vecs] + [ids.astype(F32)])]
    unnamed x50 -> x32, local copies, waits for them, and re-layouts: 14.5 us -> 10 us
    ppermute x2 -> x1, waiting for transfers between devices: 3.23 us -> 0.01 us  [pieces_of(): lax.ppermute(top, 'win', [(i, i ^ 3) for i in range(4)])]
  transfers between devices with their start and end apart: 7 -> 3, of which waited for: 1 -> 0; matrix products, arithmetic and copies ran while one was open for 5% -> 0% of each run, Pallas kernels for 50% -> 19%
where the time goes in v4:
time: 246 us
  Pallas kernels  227 us (92%)
  local copies, waits for them, and re-layouts  14.9 us (6%)
    pallas_call x1, Pallas kernels, compute(): pl.pallas_call(functools.partial(attend_kernel, scale=scale, per_group=pe...  55.7 us
    pallas_call x1, Pallas kernels, compute(): pl.pallas_call(functools.partial(attend_back_kernel, scale=scale, per_gro...  46.4 us
    pallas_call x1, Pallas kernels, finish(): pl.pallas_call(functools.partial(finish_kernel, clip_size=clip_size), in_...  43.4 us
    pallas_call x1, Pallas kernels, spread(): pl.pallas_call(functools.partial(spread_kernel, clip_size=clip_size), in_...  41.7 us
    pallas_call x1, Pallas kernels, compute(): pl.pallas_call(functools.partial(dense_kernel, per_clip=per_clip, chunk=c...  40.2 us
    unnamed x32, local copies, waits for them, and re-layouts  10 us
  transfers between devices with their start and end apart: 3, of which 0 were waited for; matrix products, arithmetic and copies ran while one was open for 0% of the time, Pallas kernels for 19%

profile of v4, /device:TPU:0, one launch (start us, length us, event | category | flops | bytes accessed | tf_op | source)
XLA Modules:
  0.0 245.9 jit_solution(12624396004861451401)
XLA Ops:
  0.6 1.2 reshape.53.qb_ref
  1.9 1.2 reshape.56.f1b_ref
  3.1 0.7 fusion
  3.7 0.5 pad.4.ids_in_ref
  4.3 41.7 %spread.1 = (bf16[4,392,512]{2,1,0:T(8,128)(2,1)}, bf16[512,1536]{1,0:T(8,128)(2,1)}, bf16[8,16,512]{2,1,0:T(8,128)(2,1)}, bf16[8,16,1536]{2,1,0:T(8,128)(2,1)},...) custom-call(bf16[4,392,512]{2,1,0:T(8,128)(2,1)} %bitcast.24, ...), custom_call_target="tpu_custom_call" | custom-call | flops 30000001024 | bytes 20000000 | tf_op jit(solution)/shard_map/spread/pallas_call | solution.py:995
  46.0 0.6 broadcast_in_dim.10.ids_ref
  46.6 55.7 %attend.1 = (bf16[4,16,392,392]{3,2,1,0:T(8,128)(2,1)}, bf16[4,392,512]{2,1,0:T(8,128)(2,1)}, bf16[4,392,1536]{2,1,0:T(8,128)(2,1)}, bf16[4,16,392]{2,1,0:T(8,12...) custom-call(bf16[4,392,512]{2,1,0:T(8,128)(2,1)} %get-tuple-element., ...), custom_call_target="tpu_custom_call" | custom-call | flops 40000000000 | bytes 10000000 | tf_op jit(solution)/shard_map/attend/pallas_call | solution.py:691
  102.3 40.2 %dense.1 = (bf16[4,392,512]{2,1,0:T(8,128)(2,1)}, f32[4,392,512]{2,1,0:T(8,128)}, bf16[4,392,512]{2,1,0:T(8,128)(2,1)}, f32[2,16,6144]{2,1,0:T(8,128)}) custom-call(s32[2]{0:T(128)} %ids_ref.1, bf16[4,392,512]{2,1,0:T(8,128)(2,1)} %get-tuple-element.46.x_ref, bf16[4,392,512]{2,1,0:T(8,128)(2,1)} %get-tuple-element.53.attn_ref, ...), custom_call_target="tpu_custom_call" | custom-call | flops 49999998976 | bytes 10000000 | tf_op jit(solution)/shard_map/dense/pallas_call | solution.py:765
  142.5 0.0 copy-start.1
  142.5 1.3 slice.3
  143.8 0.7 collective-permute-start.2
  144.5 1.4 collective-permute-start.1
  145.9 0.0 collective-permute-start
  146.0 46.4 %attend_back.1 = (bf16[4,392,512]{2,1,0:T(8,128)(2,1)}, f32[2,16,2048]{2,1,0:T(8,128)}) custom-call(bf16[4,392,512]{2,1,0:T(8,128)(2,1)} %get-tuple-element.46.x_ref, f32[1,512]{1,0:T(1,128)} %get-tuple-element.47.gain_ref, bf16[512,1536]{1,0:T(8,128)(2,1)} %get-tuple-element.48.weight_ref, bf16[2,16,512]{2,1,0:T(8,128)(2,1)} %get-tuple-element.61.down_ref, ...), custom_call_target="tpu_custom_call" | custom-call | flops 49999998976 | bytes 10000000 | tf_op jit(solution)/shard_map/attend_back/pallas_call | solution.py:813
  192.3 0.0 collective-permute-done.2.act_far_ref
  192.3 0.0 collective-permute-done.1.act_across_ref
  192.3 0.0 collective-permute-done.act_beside_ref
  192.3 0.0 copy-start.10
  192.4 1.1 copy-done.10
  193.5 43.4 %finish.1 = (bf16[4,392,512]{2,1,0:T(8,128)(2,1)}, bf16[4,392,512]{2,1,0:T(8,128)(2,1)}, f32[2,16,64]{2,1,0:T(8,128)}, f32[2,16,192]{2,1,0:T(8,128)}, f32[2,16,6...) custom-call(bf16[4,392,512]{2,1,0:T(8,128)(2,1)} %get-tuple-element., ...), custom_call_target="tpu_custom_call" | custom-call | flops 20000000000 | bytes 20000000 | tf_op jit(solution)/shard_map/finish/pallas_call | solution.py:1159
  236.9 0.0 copy-start
  237.0 2.8 %copy.42 = bf16[2,2,392,512]{3,2,1,0:T(8,128)(2,1)} copy(bf16[2,2,392,512]{3,2,1,0:T(8,128)(2,1)} %bitcast.19) | data formatting | bytes 3211264
  239.8 1.2 copy.43
  241.0 0.6 copy.44
  241.6 0.6 copy.45
  242.2 0.6 copy.46
  242.8 0.6 copy.47
  243.4 0.6 copy.48
  244.0 0.6 copy.49
  244.6 0.6 copy.50
  245.3 0.0 copy-done.5
  245.3 0.6 copy.51
  (17 shorter events, 0.0 us)
Async XLA Ops:
  142.5 3.5 %copy-start.1 = (bf16[4,392,512]{2,1,0:T(8,128)(2,1)S(1)}, bf16[4,392,512]{2,1,0:T(8,128)(2,1)}, u32[]{:S(2)}) copy-start(bf16[4,392,512]{2,1,0:T(8,128)(2,1)} %get-tuple-element.60.act_ref) | copy-start | bytes 4816900
  143.8 48.5 %collective-permute-start.2 = (bf16[4,208,512]{2,1,0:T(8,128)(2,1)S(1)}, bf16[4,208,512]{2,1,0:T(8,128)(2,1)}, u32[]{:S(2)}, u32[]{:S(2)}) collective-permute-start(bf16[4,208,512]{2,1,0:T(8,128)(2,1)S(1)} %slice.3), channel_id=1, source_target_pairs={{0,3},{1,2},{2,1},{3,0},{4,7},{5,6},{6,5},{7,4},{8,11},{9,10},{10,... | collective-permute-start | bytes 2555912 | tf_op jit(solution)/shard_map/ppermute | solution.py:1210
  144.5 47.8 %collective-permute-start.1 = (bf16[4,208,512]{2,1,0:T(8,128)(2,1)S(1)}, bf16[4,208,512]{2,1,0:T(8,128)(2,1)}, u32[]{:S(2)}, u32[]{:S(2)}) collective-permute-start(bf16[4,208,512]{2,1,0:T(8,128)(2,1)S(1)} %slice.3), channel_id=1, source_target_pairs={{0,2},{1,3},{2,0},{3,1},{4,6},{5,7},{6,4},{7,5},{8,10},{9,11},{10,... | collective-permute-start | bytes 2555912 | tf_op jit(solution)/shard_map/ppermute | solution.py:1209
  145.9 46.4 %collective-permute-start = (bf16[4,392,512]{2,1,0:T(8,128)(2,1)S(1)}, bf16[4,392,512]{2,1,0:T(8,128)(2,1)S(1)}, u32[]{:S(2)}, u32[]{:S(2)}) collective-permute-start(bf16[4,392,512]{2,1,0:T(8,128)(2,1)S(1)} %copy-done.1), channel_id=1, source_target_pairs={{0,1},{1,0},{2,3},{3,2},{4,5},{5,4},{6,7},{7,6},{8,9},{9,8},{10,11... | collective-permute-start | bytes 4816904 | tf_op jit(solution)/shard_map/ppermute | solution.py:1208
  192.3 1.2 copy-start.10
  236.9 2.8 %copy-start = (bf16[4,392,512]{2,1,0:T(8,128)(2,1)S(1)}, bf16[4,392,512]{2,1,0:T(8,128)(2,1)}, u32[]{:S(2)}) copy-start(bf16[4,392,512]{2,1,0:T(8,128)(2,1)} %get-tuple-element.73) | copy-start | bytes 4816900
  239.8 1.2 copy-start.9
  239.8 1.8 copy-start.4
  239.8 2.4 copy-start.8
  239.8 3.0 %copy-start.7 = (f32[2,16,64]{2,1,0:T(8,128)S(1)}, f32[2,16,64]{2,1,0:T(8,128)}, u32[]{:S(2)}) copy-start(f32[2,16,64]{2,1,0:T(8,128)} %get-tuple-element.99) | copy-start | bytes 24580
  239.8 3.6 %copy-start.6 = (f32[2,16,64]{2,1,0:T(8,128)S(1)}, f32[2,16,64]{2,1,0:T(8,128)}, u32[]{:S(2)}) copy-start(f32[2,16,64]{2,1,0:T(8,128)} %get-tuple-element.78) | copy-start | bytes 24580
  239.8 4.2 %copy-start.3 = (f32[2,16,256]{2,1,0:T(8,128)S(1)}, f32[2,16,256]{2,1,0:T(8,128)}, u32[]{:S(2)}) copy-start(f32[2,16,256]{2,1,0:T(8,128)} %get-tuple-element.101) | copy-start | bytes 98308
  239.8 4.8 %copy-start.2 = (f32[2,16,256]{2,1,0:T(8,128)S(1)}, f32[2,16,256]{2,1,0:T(8,128)}, u32[]{:S(2)}) copy-start(f32[2,16,256]{2,1,0:T(8,128)} %get-tuple-element.80) | copy-start | bytes 98308
  239.8 5.5 %copy-start.5 = (f32[2,16,64]{2,1,0:T(8,128)S(1)}, f32[2,16,64]{2,1,0:T(8,128)}, u32[]{:S(2)}) copy-start(f32[2,16,64]{2,1,0:T(8,128)} %get-tuple-element.103) | copy-start | bytes 24580

commit v5 on v4

--- a/solution.py
+++ b/solution.py
@@ -42,14 +42,14 @@
     return inverse * (scaled - centre - normed * slope)
 
 
-def add_rows(ref, at, value, first):
+def add_rows(ref, n, at, value, first):
     @pl.when(first)
     def _():
-        ref[0, :, at] = value
+        ref[n, :, at] = value
 
     @pl.when(jnp.logical_not(first))
     def _():
-        ref[0, :, at] += value
+        ref[n, :, at] += value
 
 
 MESH = pl.DeviceIdType.MESH
@@ -547,6 +547,117 @@
     grad_ref[0, :, fc2_up_at:] = dot(reduced_fc2, dy, NN)
 
 
+PIECES = (
+    (0, 0, 64),
+    (0, 512, 192),
+    (1, 0, 64),
+    (1, 512, 64),
+    (1, 1024, 64),
+    (1, 5632, 64),
+    (1, 1536, 256),
+    (1, 3584, 256),
+)
+
+
+class Rows:
+    def __init__(self, place, own, beside, mixed, tops, send_sem, recv_sem):
+        self.place, self.own, self.beside, self.mixed, self.tops = place, own, beside, mixed, tops
+        self.send_sem, self.recv_sem = send_sem, recv_sem
+        self.items, self.rows, self.feats = own.shape
+
+    def copy(self, kind, i):
+        n = kind * self.items + i
+        sems = self.send_sem.at[n], self.recv_sem.at[n]
+        if kind == 0:
+            return remote(self.own.at[i], self.beside.at[i], *sems, self.place.sibling)
+        top = self.mixed.at[i, pl.ds(0, TOP)]
+        return remote(top, self.tops.at[i], *sems, self.place.across)
+
+    def begin(self, i):
+        self.copy(0, i).start()
+
+    def mix(self, i):
+        self.copy(0, i).wait_recv()
+        low_h = row_masks(self.rows, self.feats)[1]
+        self.mixed[i] = jnp.where(low_h, self.beside[i], self.own[i])
+        self.copy(1, i).start()
+
+    def end(self, out):
+        early, _, low_w = row_masks(self.rows, self.feats)
+        for i in range(0, self.items, 2):
+            both = []
+            for e in range(2):
+                self.copy(1, i + e).wait_recv()
+                both.append(with_top(self.mixed[i + e], self.tops[i + e], early))
+            for e in range(2):
+                out[i + e] = jnp.where(low_w, both[1 - e], both[e])
+        for i in range(self.items):
+            self.copy(0, i).wait_send()
+            self.copy(1, i).wait_send()
+
+
+def gradient_rows(sources, part, j):
+    halves = []
+    for n in range(2):
+        cells = []
+        for array, start, width in PIECES:
+            at = slice(start + j * width, start + (j + 1) * width)
+            cells.append(sources[array][n, pl.ds(pl.multiple_of(part * 8, 8), 8), at])
+        halves.append(jnp.concatenate(cells, axis=1))
+    return jnp.concatenate(halves, axis=0)
+
+
+def share_gradients(place, sources, ids_ref, refs, send, between):
+    own, other, from_core, half, from_x, shares, from_clips, adapters, from_win, out = refs
+    c, w, x, k = place.c, place.w, place.x, place.k
+    clip_size = own.shape[0]
+    for j in range(clip_size):
+        other[j] = gradient_rows(sources, 1 - k, j).astype(BF)
+    core_copy = send.copy(other, from_core, place.sibling)
+    between[0]()
+    for j in range(clip_size):
+        own[j] = gradient_rows(sources, k, j)
+    core_copy.wait_recv()
+    own[...] += from_core[...].astype(F32)
+    half[...] = own[:, :, pl.ds(pl.multiple_of((1 - x) * 512, 512), 512)].astype(BF)
+    x_copy = send.copy(half, from_x, place.across)
+    between[1]()
+    x_copy.wait_recv()
+    shares[...] = (
+        own[:, :, pl.ds(pl.multiple_of(x * 512, 512), 512)] + from_x[...].astype(F32)
+    ).astype(BF)
+    from_clips[c] = shares[c]
+    clip_copies = []
+    for d in range(1, clip_size):
+        to = (c + d) % clip_size
+        clip_copies.append(send.copy(shares.at[to], from_clips.at[c], (to, w)))
+    for copy in clip_copies:
+        copy.wait_recv()
+    for a in range(8):
+        total = None
+        for n in range(2 * clip_size):
+            value = from_clips[n // 2].astype(F32)[8 * (n % 2) : 8 * (n % 2) + 8]
+            value = jnp.where(ids_ref[n : n + 1, :] == float(a), value, 0.0)
+            total = value if total is None else total + value
+        adapters[a // 2, 8 * (a % 2) : 8 * (a % 2) + 8, :] = total
+    from_win[w] = adapters[w]
+    win_copies = []
+    for d in range(1, 4):
+        to = (w + d) % 4
+        win_copies.append(send.copy(adapters.at[to], from_win.at[w], (c, to)))
+    between[2]()
+    for copy in win_copies:
+        copy.wait_recv()
+    for x2 in range(2):
+        for k2 in range(2):
+            for a in range(2):
+                out[a, 8 * k2 : 8 * k2 + 8, 512 * x2 : 512 * x2 + 512] = from_win[
+                    2 * x2 + k2, 8 * a : 8 * a + 8, :
+                ]
+    for copy in [core_copy, x_copy, *clip_copies, *win_copies]:
+        copy.wait_send()
+
+
 def attend_back_kernel(
     x_ref,
     gain_ref,
@@ -559,21 +670,56 @@
     reduced_ref,
     dattn_ref,
     dx1_ref,
-    dx_ref,
-    grad_ref,
-    values,
-    keys_t,
-    inner,
-    dqkv,
-    dquery_t,
-    *,
+    *refs,
     scale,
     per_group,
     width,
     per_clip,
+    remote_size,
 ):
+    if remote_size:
+        act_ref, grad_dense_ref, ids_ref, act_out_ref, dx_out_ref, sums_ref, *refs = refs
+    else:
+        dx_ref, grad_ref, *refs = refs
+    values, keys_t, inner, dqkv, dquery_t, *refs = refs
     group = pl.program_id(1)
     groups = pl.num_programs(1)
+    item = pl.program_id(0)
+    step = item * groups + group
+    if remote_size:
+        items = act_ref.shape[0]
+        place = Place(remote_size)
+        act_rows = Rows(place, act_ref, *refs[:5])
+        dx_own = refs[5]
+        dx_rows = Rows(place, *refs[5:11])
+        grad_ref = refs[11]
+        share_refs, sems = refs[12:21], refs[21:]
+
+        @pl.when(step == 0)
+        def _():
+            enter(
+                [(place.c, (place.w + d) % 4) for d in range(1, 4)]
+                + [((place.c + d) % remote_size, place.w) for d in range(1, remote_size)]
+            )
+            for i in range(items):
+                act_rows.begin(i)
+
+        for i in range(items):
+
+            @pl.when(step == i + 1)
+            def _():
+                act_rows.mix(i)
+
+            if i < items - 1:
+
+                @pl.when(step == (i + 1) * 4 + 1)
+                def _():
+                    dx_rows.mix(i)
+
+        @pl.when(step == 4 * items - 3)
+        def _():
+            act_rows.end(act_out_ref)
+
     feats = x_ref.shape[-1]
     rows = x_ref.shape[1]
 
@@ -633,19 +779,44 @@
         normed, inverse = norm_stats(x_ref[0].astype(F32))
         low = (normed * gain_ref[...]).astype(BF)
         grad_reduced = dot(up_ref[0], dall, NT).astype(BF)
-        add_rows(grad_ref, slice(feats, 4 * feats), dot(reduced_ref[0], dall, NN), first)
-        add_rows(grad_ref, slice(0, feats), dot(grad_reduced, low, NN), first)
+        slot = item // per_clip if remote_size else 0
+        add_rows(grad_ref, slot, slice(feats, 4 * feats), dot(reduced_ref[0], dall, NN), first)
+        add_rows(grad_ref, slot, slice(0, feats), dot(grad_reduced, low, NN), first)
         dlow = (dot(dall, weight_ref[...], NT) + dot(grad_reduced, down_ref[0], TN)).astype(BF)
-        dx_ref[0] = (
-            dx1_ref[0] + norm_back(dlow.astype(F32), gain_ref[...], normed, inverse)
-        ).astype(BF)
+        dx = (dx1_ref[0] + norm_back(dlow.astype(F32), gain_ref[...], normed, inverse)).astype(BF)
+        if not remote_size:
+            dx_ref[0] = dx
+            return
+        dx_own[item] = dx
+        for i in range(items):
+
+            @pl.when(item == i)
+            def _():
+                dx_rows.begin(i)
+
+    if remote_size:
+
+        @pl.when(step == 4 * items - 1)
+        def _():
+            share_gradients(
+                place,
+                (grad_ref, grad_dense_ref),
+                ids_ref,
+                (*share_refs, sums_ref),
+                Sender(*sems),
+                (
+                    lambda: dx_rows.mix(items - 1),
+                    lambda: None,
+                    lambda: dx_rows.end(dx_out_ref),
+                ),
+            )
 
 
 def whole(shape):
     return pl.BlockSpec(shape, lambda *at: (0,) * len(shape), pipeline_mode=pl.Buffered(1))
 
 
-def compute(x, dy, adapter_ids, vectors, qkv_parts, later, table, per_clip, remote_size):
+def compute(x, dy, adapter_ids, all_ids, vectors, qkv_parts, later, table, per_clip, remote_size):
     items, rows, feats = x.shape
     heads = table.shape[0]
     width = feats // heads
@@ -810,9 +981,60 @@
         item_ids, x, attn, gain2, proj_bias, fc1_bias, fc2_bias, dy, staged, *([staged] * 6)
     )
 
-    dx, grad_qkv = pl.pallas_call(
+    if remote_size:
+        assert (clips, per_clip) == (2, 2)
+        count = remote_size
+        back_in = (act, grad_dense, all_ids)
+        back_out = [whole(x.shape), whole(x.shape), whole((2, rank, 1024))]
+        back_shape = [
+            jax.ShapeDtypeStruct(x.shape, BF),
+            jax.ShapeDtypeStruct(x.shape, BF),
+            jax.ShapeDtypeStruct((2, rank, 1024), F32),
+        ]
+        sems = pltpu.SemaphoreType.DMA
+        tops = pltpu.VMEM((items, TOP, feats), BF)
+        row_scratch = [
+            pltpu.VMEM(x.shape, BF),
+            pltpu.VMEM(x.shape, BF),
+            tops,
+            sems((2 * items,)),
+            sems((2 * items,)),
+        ]
+        back_scratch = [
+            *row_scratch,
+            pltpu.VMEM(x.shape, BF),
+            *row_scratch,
+            pltpu.VMEM((clips, rank, 4 * feats), F32),
+            pltpu.VMEM((count, 16, 1024), F32),
+            pltpu.VMEM((count, 16, 1024), BF),
+            pltpu.VMEM((count, 16, 1024), BF),
+            pltpu.VMEM((count, 16, 512), BF),
+            pltpu.VMEM((count, 16, 512), BF),
+            pltpu.VMEM((count, 16, 512), BF),
+            pltpu.VMEM((count, 16, 512), BF),
+            pltpu.VMEM((4, 16, 512), F32),
+            pltpu.VMEM((4, 16, 512), F32),
+            sems((16,)),
+            sems((16,)),
+        ]
+    else:
+        back_in, back_scratch = (), []
+        back_out = [
+            item((rows, feats)),
+            pl.BlockSpec((1, rank, 4 * feats), lambda i, g: (i // per_clip, 0, 0)),
+        ]
+        back_shape = [
+            jax.ShapeDtypeStruct((items, rows, feats), BF),
+            jax.ShapeDtypeStruct((clips, rank, 4 * feats), F32),
+        ]
+    results = pl.pallas_call(
         functools.partial(
-            attend_back_kernel, scale=scale, per_group=per_group, width=width, per_clip=per_clip
+            attend_back_kernel,
+            scale=scale,
+            per_group=per_group,
+            width=width,
+            per_clip=per_clip,
+            remote_size=remote_size,
         ),
         grid=(items, groups),
         in_specs=[
@@ -827,29 +1049,28 @@
             item((rank, rows)),
             item((rows, feats)),
             item((rows, feats)),
+            *[whole(a.shape) for a in back_in],
         ],
-        out_specs=[
-            item((rows, feats)),
-            pl.BlockSpec((1, rank, 4 * feats), lambda i, g: (i // per_clip, 0, 0)),
-        ],
+        out_specs=back_out,
         scratch_shapes=[
             pltpu.VMEM((rows, 2 * feats), BF),
             pltpu.VMEM((feats, rows), BF),
             pltpu.VMEM((rows, feats), BF),
             pltpu.VMEM((rows, 3 * feats), BF),
             pltpu.VMEM((feats, rows), BF),
+            *back_scratch,
         ],
-        out_shape=[
-            jax.ShapeDtypeStruct((items, rows, feats), BF),
-            jax.ShapeDtypeStruct((clips, rank, 4 * feats), F32),
-        ],
+        out_shape=back_shape,
         compiler_params=pltpu.CompilerParams(
-            vmem_limit_bytes=VMEM_LIMIT, dimension_semantics=("arbitrary", "arbitrary")
+            vmem_limit_bytes=VMEM_LIMIT, dimension_semantics=("arbitrary", "arbitrary"),
+            **({"collective_id": 1, "has_side_effects": True} if remote_size else {}),
         ),
         cost_estimate=pl.CostEstimate(flops=5 * 10**10, bytes_accessed=10**7, transcendentals=0),
         name="attend_back",
-    )(x, gain1, qkv_w, down_own, up_own, probs, attn, qkv, reduced, dattn, dx1)
-    return act, dx, grad_qkv, grad_dense
+    )(x, gain1, qkv_w, down_own, up_own, probs, attn, qkv, reduced, dattn, dx1, *back_in)
+    if remote_size:
+        return results
+    return (act, *results, grad_dense)
 
 
 def spread_kernel(
@@ -1037,155 +1258,6 @@
     )(tokens, table, qkv_w, qkv_down, qkv_up, ids, *vecs)
 
 
-PIECES = (("q", 0, 64), ("q", 512, 192), ("d", 0, 64), ("d", 512, 64), ("d", 1024, 64), ("d", 5632, 64), ("d", 1536, 256), ("d", 3584, 256))
-
-
-def finish_kernel(
-    act_ref, act_beside_ref, act_across_ref, act_far_ref, dx_ref, grad_qkv_ref, grad_dense_ref, ids_ref,
-    act_out_ref, dx_out_ref, qd_ref, qu_ref, pd_ref, pu_ref, f1d_ref, f1u_ref, f2d_ref, f2u_ref,
-    beside, mixed, tops, own, other, from_core, half, from_x, shares, from_clips, adapters, from_win, whole_out,
-    send_sem, recv_sem,
-    *, clip_size,
-):
-    c, w = lax.axis_index("clip"), lax.axis_index("win")
-    x, k = w // 2, w % 2
-    sibling = (c, x * 2 + 1 - k)
-    across = (c, (1 - x) * 2 + k)
-    items, rows, feats = dx_ref.shape
-    enter(
-        [(c, (w + d) % 4) for d in range(1, 4)]
-        + [((c + d) % clip_size, w) for d in range(1, clip_size)]
-    )
-    send = Sender(send_sem, recv_sem)
-    dx_beside = [send.copy(dx_ref.at[i], beside.at[i], sibling) for i in range(items)]
-
-    def rows_of(part, j):
-        halves = []
-        for n in range(2):
-            cells = []
-            for name, start, width in PIECES:
-                ref = grad_qkv_ref if name == "q" else grad_dense_ref
-                cells.append(
-                    ref[n, pl.ds(pl.multiple_of(part * 8, 8), 8), start + j * width : start + (j + 1) * width]
-                )
-            halves.append(jnp.concatenate(cells, axis=1))
-        return jnp.concatenate(halves, axis=0)
-
-    for j in range(clip_size):
-        other[j] = rows_of(1 - k, j).astype(BF)
-    core_copy = send.copy(other, from_core, sibling)
-
-    early, low_h, low_w = row_masks(rows, feats)
-    dx_tops = []
-    for i in range(items):
-        dx_beside[i].wait_recv()
-        mixed[i] = jnp.where(low_h, beside[i], dx_ref[i])
-        dx_tops.append(send.copy(mixed.at[i, pl.ds(0, TOP)], tops.at[i], across))
-
-    for j in range(clip_size):
-        own[j] = rows_of(k, j)
-    core_copy.wait_recv()
-    own[...] += from_core[...].astype(F32)
-    half[...] = own[:, :, pl.ds(pl.multiple_of((1 - x) * 512, 512), 512)].astype(BF)
-    x_copy = send.copy(half, from_x, across)
-
-    for i in range(0, items, 2):
-        both = []
-        for e in range(2):
-            part = jnp.where(low_h, act_beside_ref[i + e], act_ref[i + e])
-            top = jnp.where(low_h[:TOP], act_far_ref[i + e], act_across_ref[i + e])
-            both.append(with_top(part, top, early))
-        for e in range(2):
-            act_out_ref[i + e] = jnp.where(low_w, both[1 - e], both[e])
-
-    x_copy.wait_recv()
-    shares[...] = (
-        own[:, :, pl.ds(pl.multiple_of(x * 512, 512), 512)] + from_x[...].astype(F32)
-    ).astype(BF)
-    from_clips[c] = shares[c]
-    clip_copies = []
-    for d in range(1, clip_size):
-        to = (c + d) % clip_size
-        clip_copies.append(send.copy(shares.at[to], from_clips.at[c], (to, w)))
-    for copy in clip_copies:
-        copy.wait_recv()
-    for a in range(8):
-        total = None
-        for n in range(2 * clip_size):
-            value = from_clips[n // 2].astype(F32)[8 * (n % 2) : 8 * (n % 2) + 8]
-            value = jnp.where(ids_ref[n : n + 1, :] == float(a), value, 0.0)
-            total = value if total is None else total + value
-        adapters[a // 2, 8 * (a % 2) : 8 * (a % 2) + 8, :] = total
-    from_win[w] = adapters[w]
-    win_copies = []
-    for d in range(1, 4):
-        to = (w + d) % 4
-        win_copies.append(send.copy(adapters.at[to], from_win.at[w], (c, to)))
-
-    for i in range(0, items, 2):
-        both = []
-        for e in range(2):
-            dx_tops[i + e].wait_recv()
-            both.append(with_top(mixed[i + e], tops[i + e], early))
-        for e in range(2):
-            dx_out_ref[i + e] = jnp.where(low_w, both[1 - e], both[e])
-
-    for copy in win_copies:
-        copy.wait_recv()
-    for x2 in range(2):
-        for k2 in range(2):
-            for a in range(2):
-                whole_out[a, 8 * k2 : 8 * k2 + 8, 512 * x2 : 512 * x2 + 512] = from_win[
-                    2 * x2 + k2, 8 * a : 8 * a + 8, :
-                ]
-    for a in range(2):
-        qd_ref[a] = whole_out[a, :, 0:64]
-        qu_ref[a] = whole_out[a, :, 64:256]
-        pd_ref[a] = whole_out[a, :, 256:320]
-        pu_ref[a] = whole_out[a, :, 320:384]
-        f1d_ref[a] = whole_out[a, :, 384:448]
-        f2u_ref[a] = whole_out[a, :, 448:512]
-        f1u_ref[a] = whole_out[a, :, 512:768]
-        f2d_ref[a] = whole_out[a, :, 768:1024]
-    for copy in [*dx_beside, core_copy, *dx_tops, x_copy, *clip_copies, *win_copies]:
-        copy.wait_send()
-
-
-def finish(act, act_pieces, dx, grad_qkv, grad_dense, ids, clip_size):
-    items, rows, feats = dx.shape
-    f = jax.ShapeDtypeStruct
-    vm = pl.BlockSpec(memory_space=pltpu.VMEM)
-    widths = (64, 192, 64, 64, 64, 256, 256, 64)
-    return pl.pallas_call(
-        functools.partial(finish_kernel, clip_size=clip_size),
-        in_specs=[vm] * 8,
-        out_specs=[vm] * 10,
-        out_shape=[f(dx.shape, BF), f(dx.shape, BF)] + [f((2, 16, n), F32) for n in widths],
-        scratch_shapes=[
-            pltpu.VMEM((items, rows, feats), BF),
-            pltpu.VMEM((items, rows, feats), BF),
-            pltpu.VMEM((items, TOP, feats), BF),
-            pltpu.VMEM((clip_size, 16, 1024), F32),
-            pltpu.VMEM((clip_size, 16, 1024), BF),
-            pltpu.VMEM((clip_size, 16, 1024), BF),
-            pltpu.VMEM((clip_size, 16, 512), BF),
-            pltpu.VMEM((clip_size, 16, 512), BF),
-            pltpu.VMEM((clip_size, 16, 512), BF),
-            pltpu.VMEM((clip_size, 16, 512), BF),
-            pltpu.VMEM((4, 16, 512), F32),
-            pltpu.VMEM((4, 16, 512), F32),
-            pltpu.VMEM((2, 16, 1024), F32),
-            pltpu.SemaphoreType.DMA((20,)),
-            pltpu.SemaphoreType.DMA((20,)),
-        ],
-        compiler_params=pltpu.CompilerParams(
-            collective_id=1, has_side_effects=True, vmem_limit_bytes=VMEM_LIMIT
-        ),
-        cost_estimate=pl.CostEstimate(flops=2 * 10**10, bytes_accessed=2 * 10**7, transcendentals=0),
-        name="finish",
-    )(act, *act_pieces, dx, grad_qkv, grad_dense, ids)
-
-
 def exchange(x, win_size):
     local = x.shape[1]
     bits = local.bit_length() - 1
@@ -1199,16 +1271,6 @@
             other = lax.ppermute(x, "win", [(i, i ^ 1 << bit - bits) for i in range(win_size)])
         x = jnp.where(rows[None, None, :, None], other, x)
     return x
-
-
-def pieces_of(x):
-    top = x[:, :TOP]
-    return (
-        x,
-        lax.ppermute(x, "win", [(i, i ^ 1) for i in range(4)]),
-        lax.ppermute(top, "win", [(i, i ^ 2) for i in range(4)]),
-        lax.ppermute(top, "win", [(i, i ^ 3) for i in range(4)]),
-    )
 
 
 def bias_by_pair(table):
@@ -1299,21 +1361,27 @@
         )
         later = (by_core(staged),)
         vectors = [gather(v, ("clip",)).reshape(1, -1).astype(F32) for v in vecs]
-        table = bias_by_pair(bias_table)
+        table, ids = bias_by_pair(bias_table), None
         x = exchange(tokens, win_size).reshape(flat)
         dy = exchange(cotangent, win_size).reshape(flat)
-    act, dx, grad_qkv, grad_dense = compute(
-        x, dy, adapter_ids, vectors, qkv_parts, later, table, local, clip_size if own_kernels else 0
+    results = compute(
+        x, dy, adapter_ids, ids, vectors, qkv_parts, later, table, local,
+        clip_size if own_kernels else 0,
     )
     if own_kernels:
-        act_out, dx_out, qd, qu, pd, pu, f1d, f1u, f2d, f2u = finish(
-            act, pieces_of(act)[1:], dx, grad_qkv, grad_dense, ids, clip_size
-        )
+        act_out, dx_out, sums = results
+        qd, qu, pd, pu, f1d, f2u, f1u, f2d = [
+            sums[..., first:last]
+            for first, last in zip(
+                (0, 64, 256, 320, 384, 448, 512, 768), (64, 256, 320, 384, 448, 512, 768, 1024)
+            )
+        ]
         turned = [a.transpose(0, 2, 1) for a in (qd, pd, f1d, f2d)]
         return (
             act_out.reshape(tokens.shape), dx_out.reshape(tokens.shape),
             turned[0], qu, turned[1], pu, turned[2], f1u, turned[3], f2u,
         )
+    act, dx, grad_qkv, grad_dense = results
     activations = exchange(act.reshape(tokens.shape), win_size)
     input_grad = exchange(dx.reshape(tokens.shape), win_size)
     adapter_count = win_size * qkv_down.shape[0]

time: 246 us -> 226 us (0.919)
  Pallas kernels: 227 us -> 212 us
  local copies, waits for them, and re-layouts: 14.9 us -> 11.9 us
    pallas_call x1 -> x0, Pallas kernels: 43.4 us -> none  [finish(): pl.pallas_call(functools.partial(finish_kernel, clip_size=clip_size), in_...]
    pallas_call x1, Pallas kernels: 46.4 us -> 74.6 us  [compute(): pl.pallas_call(functools.partial(attend_back_kernel, scale=scale, per_gro...]
    unnamed x32 -> x4, local copies, waits for them, and re-layouts: 10 us -> 3.95 us
  transfers between devices with their start and end apart: 3 -> 0, of which waited for: 0 -> 0; matrix products, arithmetic and copies ran while one was open for 0% -> 0% of each run, Pallas kernels for 19% -> 0%
where the time goes in v5:
time: 226 us; the launch traced here: 225 us
  Pallas kernels  212 us (94%)
  local copies, waits for them, and re-layouts  11.9 us (5%)
    pallas_call x1, Pallas kernels, compute(): pl.pallas_call(functools.partial(attend_back_kernel, scale=scale, per_gro...  74.6 us
    pallas_call x1, Pallas kernels, compute(): pl.pallas_call(functools.partial(attend_kernel, scale=scale, per_group=pe...  55.6 us
    pallas_call x1, Pallas kernels, spread(): pl.pallas_call(functools.partial(spread_kernel, clip_size=clip_size), in_...  41.7 us
    pallas_call x1, Pallas kernels, compute(): pl.pallas_call(functools.partial(dense_kernel, per_clip=per_clip, chunk=c...  40.2 us

profile of v5, /device:TPU:0, one launch (start us, length us, event | category | flops | bytes accessed | tf_op | source)
XLA Modules:
  0.0 225.3 jit_solution(12381992423967414949)
XLA Ops:
  0.6 1.2 reshape.53.qb_ref
  1.9 1.2 reshape.56.f1b_ref
  3.1 0.7 fusion.1
  3.7 0.6 broadcast_in_dim.10.ids_ref
  4.4 0.5 pad.4.ids_in_ref
  4.9 41.7 %spread.1 = (bf16[4,392,512]{2,1,0:T(8,128)(2,1)}, bf16[512,1536]{1,0:T(8,128)(2,1)}, bf16[8,16,512]{2,1,0:T(8,128)(2,1)}, bf16[8,16,1536]{2,1,0:T(8,128)(2,1)},...) custom-call(bf16[4,392,512]{2,1,0:T(8,128)(2,1)} %bitcast.24, ...), custom_call_target="tpu_custom_call" | custom-call | flops 30000001024 | bytes 20000000 | tf_op jit(solution)/shard_map/spread/pallas_call | solution.py:1216
  46.6 55.6 %attend.1 = (bf16[4,16,392,392]{3,2,1,0:T(8,128)(2,1)}, bf16[4,392,512]{2,1,0:T(8,128)(2,1)}, bf16[4,392,1536]{2,1,0:T(8,128)(2,1)}, bf16[4,16,392]{2,1,0:T(8,12...) custom-call(bf16[4,392,512]{2,1,0:T(8,128)(2,1)} %get-tuple-element., ...), custom_call_target="tpu_custom_call" | custom-call | flops 40000000000 | bytes 10000000 | tf_op jit(solution)/shard_map/attend/pallas_call | solution.py:862
  102.2 40.2 %dense.1 = (bf16[4,392,512]{2,1,0:T(8,128)(2,1)}, f32[4,392,512]{2,1,0:T(8,128)}, bf16[4,392,512]{2,1,0:T(8,128)(2,1)}, f32[2,16,6144]{2,1,0:T(8,128)}) custom-call(s32[2]{0:T(128)} %ids_ref.1, bf16[4,392,512]{2,1,0:T(8,128)(2,1)} %get-tuple-element.37.x_ref, bf16[4,392,512]{2,1,0:T(8,128)(2,1)} %get-tuple-element.47.attn_ref, ...), custom_call_target="tpu_custom_call" | custom-call | flops 49999998976 | bytes 10000000 | tf_op jit(solution)/shard_map/dense/pallas_call | solution.py:936
  142.4 74.6 %attend_back.1 = (bf16[4,392,512]{2,1,0:T(8,128)(2,1)}, bf16[4,392,512]{2,1,0:T(8,128)(2,1)}, f32[2,16,1024]{2,1,0:T(8,128)}) custom-call(bf16[4,392,512]{2,1,0:T(8,128)(2,1)} %get-tuple-element.37.x_ref, f32[1,512]{1,0:T(1,128)} %get-tuple-element.38.gain_ref, bf16[512,1536]{1,0:T(8,128)(2,1)} %get-tuple-element.39.weight_ref, ...), custom_call_target="tpu_custom_call" | custom-call | flops 49999998976 | bytes 10000000 | tf_op jit(solution)/shard_map/attend_back/pallas_call | solution.py:1030
  217.0 1.5 slice.25
  218.5 1.4 slice_bitcast_fusion
  219.9 1.5 fusion
  221.4 0.0 copy-start
  221.4 2.8 %copy.34 = bf16[2,2,392,512]{3,2,1,0:T(8,128)(2,1)} copy(bf16[2,2,392,512]{3,2,1,0:T(8,128)(2,1)} %bitcast.23) | data formatting | bytes 3211264
  224.2 0.0 copy-done
  224.2 1.2 copy.35
Async XLA Ops:
  221.4 2.8 %copy-start = (bf16[4,392,512]{2,1,0:T(8,128)(2,1)S(1)}, bf16[4,392,512]{2,1,0:T(8,128)(2,1)}, u32[]{:S(2)}) copy-start(bf16[4,392,512]{2,1,0:T(8,128)(2,1)} %get-tuple-element.62) | copy-start | bytes 4816900
